TPU v7x, 768 devices: a whole 4x8x12 slice. The times are simulated.
768 devices in a mesh: dp: 192 (over y, z, x_hi), node: 4 (over x_lo, core).
Axes of the slice: x: 4 (x_hi: 2, x_lo: 2; x = x_hi * 2 + x_lo), y: 8, z: 12, core: 2. Of those that a mesh axis runs over, the one named last changes fastest.
Arguments:
- gate_up: bfloat16 [196608, 240], P(('dp', 'node')), may hold values from -6 to 6
- out_grad: bfloat16 [196608, 8192], P(('dp', 'node')), may hold values from -6 to 6
- weight_codes: bfloat16 [120, 8192], P('node'), may hold values from -440 to 440
- weight_scales: bfloat16 [120, 64], P('node'), may hold values from 2.9921532e-05 to 0.00029945374
- shard_order: int32 [768], replicated, may hold values from 0 to 767, each once
Outputs:
- grad_gate_up: bfloat16 [196608, 240], P(('dp', 'node'))
- weight_grad: float32 [768, 1280], P(('dp', 'node'))
Inputs may be any that keep to these rules, and one draw needn't show every extreme that they name: `shard_order`: a permutation: every span has exactly one owner.
All inputs are finite; a program needn't handle non-finite values.
Results may differ from a plain program's by a relative error of at most 0.014.
Values may be sent and summed in bfloat16 or wider, within the bound.
No kernel may reach another device: no remote copies, remote signals or barrier semaphores. Data moves between devices by JAX's collectives and lax.ppermute only.
A program may use at most 64 MiB of HBM per device.

v0:
```python
import jax
import jax.numpy as jnp
from jax import lax
from jax.sharding import PartitionSpec as P

QBLK = 128


epsilon = 1e-06
code_limit = 448.0


def quantize(values):
    largest = jnp.max(jnp.abs(values), axis=-1)
    block_scale = ((largest + epsilon) / code_limit).astype(jnp.bfloat16)
    code_values = (values / block_scale.astype(jnp.float32)[..., None]).astype(jnp.bfloat16)
    return (code_values, block_scale)


def dequantize(code_values, block_scale):
    return code_values.astype(jnp.float32) * block_scale.astype(jnp.float32)[..., None]


def dequant_weight(weight_codes, weight_scales):
    rows_here = weight_codes.shape[0]
    blocked = weight_codes.reshape(rows_here, -1, QBLK)
    return dequantize(blocked, weight_scales).reshape(rows_here, -1).astype(jnp.bfloat16)


def project_back(out_grad, weight):
    return lax.dot_general(
        out_grad, weight, (((1,), (1,)), ((), ())), preferred_element_type=jnp.float32
    )


def per_device(gate_up, out_grad, weight_codes, weight_scales, shard_order):
    data_size = lax.axis_size("dp")
    node_size = lax.axis_size("node")
    devices_all = data_size * node_size
    codes_all, scales_all = (
        lax.all_gather(weight_codes, "node", axis=0, tiled=True),
        lax.all_gather(weight_scales, "node", axis=0, tiled=True),
    )
    hidden_grad = project_back(out_grad, dequant_weight(codes_all, scales_all))
    half = gate_up.shape[1] // 2
    gate_pre = gate_up[:, :half].astype(jnp.float32)
    up_pre = gate_up[:, half:].astype(jnp.float32)
    sigmoid_gate = jax.nn.sigmoid(gate_pre)
    activated = gate_pre * sigmoid_gate
    hidden = (activated * up_pre).astype(jnp.bfloat16)
    gate_grad = hidden_grad * up_pre * sigmoid_gate * (1.0 + gate_pre * (1.0 - sigmoid_gate))
    up_grad = hidden_grad * activated
    grad_gate_up = jnp.concatenate([gate_grad, up_grad], axis=1).astype(jnp.bfloat16)
    partial_value = lax.dot_general(
        hidden, out_grad, (((0,), (0,)), ((), ())), preferred_element_type=jnp.float32
    )
    spans = partial_value.reshape(devices_all, -1, QBLK)[shard_order]
    code_values, block_scale = quantize(spans)
    per_block = code_values.shape[1]
    code_values = code_values.reshape(data_size, node_size, per_block, QBLK)
    block_scale = block_scale.reshape(data_size, node_size, per_block)
    got_codes, got_scales = (
        lax.all_to_all(code_values, "node", split_axis=1, concat_axis=1, tiled=True),
        lax.all_to_all(block_scale, "node", split_axis=1, concat_axis=1, tiled=True),
    )
    group_total = jnp.sum(dequantize(got_codes, got_scales), axis=1)
    second_codes, second_scale = quantize(group_total)
    requantized = dequantize(second_codes, second_scale)
    running = lax.psum_scatter(requantized, "dp", scatter_dimension=0, tiled=True)
    weight_grad = (running * (1.0 / devices_all)).reshape(1, -1)
    return (grad_gate_up, weight_grad)


def solution(mesh):
    return jax.shard_map(
        per_device,
        mesh=mesh,
        in_specs=(
            P(("dp", "node"), None),
            P(("dp", "node"), None),
            P("node", None),
            P("node", None),
            P(),
        ),
        out_specs=(P(("dp", "node"), None), P(("dp", "node"), None)),
        check_vma=False,
    )
```

profile of v0, /device:TPU:6, one launch (start us, length us, event | category | flops | bytes accessed | tf_op | source)
XLA Modules:
  0.0 2039.2 jit_solution(195518447504492596)
XLA Ops:
  8.0 4.9 fusion.15
  12.9 5.6 reshape.39
  18.5 0.0 copy-done.3
  18.6 6.6 gather_fusion
  25.2 4.5 abs_reduce_fusion
  29.7 0.1 multiply_convert_fusion
  29.8 0.1 copy.16
  29.9 0.7 reshape.59
  30.6 4.1 all-to-all-start.1
  34.7 0.1 copy.14
  34.8 6.1 fusion.1
  40.9 0.0 all-to-all-done.1
  40.9 3.6 all-to-all-start
  44.6 0.0 all-reduce.3.cloned.1.call-start
  44.6 0.1 reshape.60
  44.7 22.5 %all-to-all-done = bf16[192,4,10,128]{3,0,2,1:T(8,128)(2,1)S(1)} async-done(((bf16[192,4,10,128]{3,0,2,1:T(8,128)(2,1)}), bf16[192,4,10,128]{3,0,2,1:T(8,128)(2,1)S(1)}, u32[]{:S(2)}, u32[]{:S(2)}) %all-to-all-start) | async-done | bytes 1966112 | tf_op jit(solution)/shard_map/all_to_all | solution.py:63
  67.2 1.3 multiply_reduce_fusion
  68.5 0.4 abs_reduce_fusion.1
  69.0 1.3 convert_multiply_fusion
  70.3 0.0 all-reduce.3.cloned.1.call-update
  70.3 0.0 all-gather.4.cloned.1.call-start
  70.4 0.5 all-gather.4.cloned.1.call-update
  70.9 0.0 copy-done.2
  70.9 5.4 all-gather.1
  76.3 1.3 dynamic-slice
  77.6 1940.0 %all-reduce.3.cloned.1.call-done = f32[192,10,128]{2,0,1:T(8,128)} async-done(((f32[192,10,128]{2,0,1:T(8,128)}), f32[192,10,128]{2,0,1:T(8,128)}) %all-reduce.3.cloned.1.call-update) | async-done | bytes 983056
  2017.6 2.0 fusion.19
  2019.6 4.0 reshape.54
  2023.6 1.1 mul.52
  2024.7 1.0 copy-done
  2025.8 5.3 fusion.9
  2031.1 0.7 pad_maximum_fusion
  (11 shorter events, 0.0 us)
Async XLA Ops:
  12.9 5.6 copy-start.3
  30.6 10.3 all-to-all-start.1
  40.9 26.2 %all-to-all-start = ((bf16[192,4,10,128]{3,0,2,1:T(8,128)(2,1)}), bf16[192,4,10,128]{3,0,2,1:T(8,128)(2,1)S(1)}, u32[]{:S(2)}, u32[]{:S(2)}) async-start(bf16[192,4,10,128]{3,0,2,1:T(8,128)(2,1)} %fusion.1), calls=%async_computation | async-start | bytes 3932160 | tf_op jit(solution)/shard_map/all_to_all | solution.py:63
  44.5 26.3 %copy-start.2 = (bf16[30,64]{1,0:T(8,128)(2,1)S(1)}, bf16[30,64]{1,0:T(8,128)(2,1)}, u32[]{:S(2)}) copy-start(bf16[30,64]{1,0:T(8,128)(2,1)} %param.8) | copy-start | bytes 11524
  44.6 1973.1 %all-reduce.3.cloned.1.call-start = ((), (), s32[]{:S(2)}) async-start(), calls=%async_computation.3 | async-start | bytes 1966080
  70.3 1949.3 %all-gather.4.cloned.1.call-start = ((), (), s32[]{:S(2)}) async-start(), calls=%async_computation.2 | async-start | bytes 2621440 | tf_op jit(solution)/shard_map/all_gather | solution.py:41
  2019.6 5.1 copy-start.1
  2023.6 2.1 copy-start
Sparse Core Ops, SparseCore 0:
  70.4 1947.1 all-reduce.2
Sparse Core Ops, SparseCore 1:
  73.2 44.1 all-gather.3
where the time goes:
time: 2040 us
  waiting for transfers between devices  1960 us (96%)
  local copies, waits for them, and re-layouts  20.8 us (1%)
    unnamed x3, waiting for transfers between devices  1940 us
  transfers between devices with their start and end apart: 4, of which 2 were waited for; matrix products, arithmetic and copies ran while one was open for 0% of the time, Pallas kernels for 0%

commit v1 on v0

v1 whole, which is shorter than its diff:
```python
import jax
import jax.numpy as jnp
from jax import lax
from jax.experimental import pallas as pl
from jax.experimental.pallas import tpu as pltpu
from jax.sharding import Mesh
from jax.sharding import PartitionSpec as P

D = 8192
FW = 120
TOK = 256
QBLK = 128
SPAN = 10
DEVICES = 768
NY, NZ = 8, 12
NX = 4
NYZ = NY * NZ
ROWS = DEVICES * SPAN
HALF = ROWS // 2
XROWS = HALF // NX
NODE_ROWS = 30
PAD_ROWS = 32
BLOCKS = D // QBLK
STEP_BLOCKS = 8
STEPS = BLOCKS // STEP_BLOCKS
ALL = ("y", "z", "xh", "xl", "core")
X = ("xh", "xl")
YZ = ("y", "z")


def dequant_kernel(codes_ref, scales_ref, out_ref):
    scales = scales_ref[...].astype(jnp.float32)
    fill = jnp.zeros((PAD_ROWS - NODE_ROWS, QBLK), jnp.float32)
    for block in range(BLOCKS):
        columns = slice(block * QBLK, (block + 1) * QBLK)
        value = codes_ref[:, columns].astype(jnp.float32) * scales[:, block : block + 1]
        out_ref[:, columns] = jnp.concatenate([value, fill], axis=0).astype(jnp.bfloat16)


def dequant(codes, scales):
    return pl.pallas_call(
        dequant_kernel,
        out_shape=jax.ShapeDtypeStruct((PAD_ROWS, D), jnp.bfloat16),
        cost_estimate=pl.CostEstimate(flops=PAD_ROWS * D, bytes_accessed=4 * PAD_ROWS * D, transcendentals=0),
    )(codes, scales)


def partial_kernel(order_ref, core_ref, gate_up_ref, out_grad_ref, keep_ref, send_ref, hidden, blocks, staged):
    step = pl.program_id(0)

    @pl.when(step == 0)
    def _():
        both = gate_up_ref[...].astype(jnp.float32)
        gate, up = both[:FW], both[FW:]
        hidden[...] = (gate * jax.nn.sigmoid(gate) * up).astype(jnp.bfloat16)

    product = jnp.dot(hidden[...], out_grad_ref[...], preferred_element_type=jnp.float32)
    for block in range(STEP_BLOCKS):
        blocks[pl.ds(step * STEP_BLOCKS + block, FW, stride=BLOCKS), :] = product[:, block * QBLK : (block + 1) * QBLK]

    @pl.when(step == STEPS - 1)
    def _():
        core = core_ref[0]

        def gather(yz, carry):
            for low in range(8):
                x, owner_core = low // 2, low % 2
                span = order_ref[yz * 8 + low]
                value = blocks[pl.ds(span * SPAN, SPAN), :]
                place = (x * NYZ + yz) * SPAN

                @pl.when(core == owner_core)
                def _():
                    keep_ref[pl.ds(place, SPAN), :] = value

                @pl.when(core != owner_core)
                def _():
                    staged[pl.ds(place, SPAN), :] = value

            return carry

        lax.fori_loop(0, NYZ, gather, 0)
        send_ref[...] = staged[...].astype(jnp.bfloat16)


def partial_spans(order, core, gate_up_t, out_grad):
    width = STEP_BLOCKS * QBLK
    whole = lambda i, *_: (0, 0)
    return pl.pallas_call(
        partial_kernel,
        grid_spec=pltpu.PrefetchScalarGridSpec(
            num_scalar_prefetch=2,
            grid=(STEPS,),
            in_specs=[
                pl.BlockSpec((2 * FW, TOK), whole),
                pl.BlockSpec((TOK, width), lambda i, *_: (0, i)),
            ],
            out_specs=[pl.BlockSpec((HALF, QBLK), whole), pl.BlockSpec((HALF, QBLK), whole)],
            scratch_shapes=[
                pltpu.VMEM((FW, TOK), jnp.bfloat16),
                pltpu.VMEM((ROWS, QBLK), jnp.float32),
                pltpu.VMEM((HALF, QBLK), jnp.float32),
            ],
        ),
        out_shape=[
            jax.ShapeDtypeStruct((HALF, QBLK), jnp.float32),
            jax.ShapeDtypeStruct((HALF, QBLK), jnp.bfloat16),
        ],
        compiler_params=pltpu.CompilerParams(vmem_limit_bytes=24 * 2**20),
        cost_estimate=pl.CostEstimate(flops=2 * FW * TOK * D, bytes_accessed=2 * TOK * D + 6 * HALF * QBLK, transcendentals=FW * TOK),
    )(order, core, gate_up_t, out_grad)


def grads_kernel(gate_up_ref, weight_ref, out_grad_ref, out_ref, total):
    step = pl.program_id(0)
    product = lax.dot_general(
        weight_ref[...], out_grad_ref[...], (((1,), (1,)), ((), ())), preferred_element_type=jnp.float32
    )

    @pl.when(step == 0)
    def _():
        total[...] = product

    @pl.when(step > 0)
    def _():
        total[...] += product

    @pl.when(step == STEPS - 1)
    def _():
        hidden_grad = jnp.concatenate(
            [total[i * PAD_ROWS : i * PAD_ROWS + NODE_ROWS, :] for i in range(4)], axis=0
        )
        both = gate_up_ref[...].astype(jnp.float32)
        gate, up = both[:FW], both[FW:]
        sig = jax.nn.sigmoid(gate)
        gate_grad = hidden_grad * up * sig * (1.0 + gate * (1.0 - sig))
        up_grad = hidden_grad * (gate * sig)
        out_ref[...] = jnp.concatenate([gate_grad, up_grad], axis=0).astype(jnp.bfloat16)


def input_grads(gate_up_t, weight, out_grad):
    width = STEP_BLOCKS * QBLK
    whole = lambda i: (0, 0)
    return pl.pallas_call(
        grads_kernel,
        grid=(STEPS,),
        in_specs=[
            pl.BlockSpec((2 * FW, TOK), whole),
            pl.BlockSpec((4 * PAD_ROWS, width), lambda i: (0, i)),
            pl.BlockSpec((TOK, width), lambda i: (0, i)),
        ],
        out_specs=pl.BlockSpec((2 * FW, TOK), whole),
        out_shape=jax.ShapeDtypeStruct((2 * FW, TOK), jnp.bfloat16),
        scratch_shapes=[pltpu.VMEM((4 * PAD_ROWS, TOK), jnp.float32)],
        compiler_params=pltpu.CompilerParams(vmem_limit_bytes=12 * 2**20),
        cost_estimate=pl.CostEstimate(flops=2 * FW * TOK * D, bytes_accessed=2 * TOK * D + 2 * 128 * D, transcendentals=FW * TOK),
    )(gate_up_t, weight, out_grad)


def pair_sum_kernel(keep_ref, got_ref, out_ref):
    out_ref[...] = (keep_ref[...] + got_ref[...].astype(jnp.float32)).astype(jnp.bfloat16)


def pair_sum(keep, got):
    steps = 4
    spec = pl.BlockSpec((HALF // steps, QBLK), lambda i: (i, 0))
    return pl.pallas_call(
        pair_sum_kernel,
        grid=(steps,),
        in_specs=[spec, spec],
        out_specs=spec,
        out_shape=jax.ShapeDtypeStruct((HALF, QBLK), jnp.bfloat16),
    )(keep, got)


def x_sum_kernel(got_ref, out_ref):
    total = got_ref[:XROWS, :].astype(jnp.float32)
    for i in range(1, NX):
        total += got_ref[i * XROWS : (i + 1) * XROWS, :].astype(jnp.float32)
    out_ref[...] = total.astype(jnp.bfloat16)


def x_sum(got):
    return pl.pallas_call(
        x_sum_kernel,
        out_shape=jax.ShapeDtypeStruct((XROWS, QBLK), jnp.bfloat16),
    )(got)


def last_sum_kernel(got_ref, out_ref, total):
    rows = 8 * SPAN
    eight = got_ref[:rows, :].astype(jnp.float32)
    for i in range(1, XROWS // rows):
        eight += got_ref[i * rows : (i + 1) * rows, :].astype(jnp.float32)
    total[...] = eight
    span = total[:SPAN, :]
    for i in range(1, 8):
        span += total[i * SPAN : (i + 1) * SPAN, :]
    span = span * (1.0 / DEVICES)
    for i in range(SPAN):
        out_ref[:, i * QBLK : (i + 1) * QBLK] = span[i : i + 1, :]


def last_sum(got):
    return pl.pallas_call(
        last_sum_kernel,
        out_shape=jax.ShapeDtypeStruct((1, SPAN * QBLK), jnp.float32),
        scratch_shapes=[pltpu.VMEM((8 * SPAN, QBLK), jnp.float32)],
    )(got)


def per_device(gate_up, out_grad, weight_codes, weight_scales, shard_order):
    gate_up_t = gate_up.T
    core = lax.axis_index("core").astype(jnp.int32).reshape(1)
    weight = lax.all_gather(dequant(weight_codes, weight_scales), ("xl", "core"), axis=0, tiled=True)
    keep, send = partial_spans(shard_order, core, gate_up_t, out_grad)
    got = lax.ppermute(send, "core", [(0, 1), (1, 0)])
    pair = pair_sum(keep, got)
    got = lax.all_to_all(pair, X, split_axis=0, concat_axis=0, tiled=True)
    line = x_sum(got).reshape(XROWS // 2, 2, QBLK)
    got = lax.all_to_all(line, YZ, split_axis=0, concat_axis=0, tiled=True)
    weight_grad = last_sum(got.reshape(XROWS, QBLK))
    grad_gate_up = input_grads(gate_up_t, weight, out_grad).T
    return (grad_gate_up, weight_grad)


def solution(mesh):
    fine = Mesh(mesh.devices.reshape(NY, NZ, 2, 2, 2), ALL)
    return jax.shard_map(
        per_device,
        mesh=fine,
        in_specs=(P(ALL, None), P(ALL, None), P(("xl", "core"), None), P(("xl", "core"), None), P()),
        out_specs=(P(ALL, None), P(ALL, None)),
        check_vma=False,
    )
```

time: 2040 us -> 120 us (0.06)
  waiting for transfers between devices: 1960 us -> 2.55 us
  blocking collectives: 5.37 us -> 64.2 us
  Pallas kernels: 0 us -> 25.5 us
    unnamed x3 -> x1, waiting for transfers between devices: 1940 us -> 0.02 us
    all_to_all x0 -> x2, blocking collectives: none -> 64.2 us  [the longest x1 35.1 us: per_device(): got = lax.all_to_all(line, YZ, split_axis=0, concat_axis=0, tiled=True)]
    pallas_call x0 -> x6, Pallas kernels: none -> 25.5 us  [the longest x1 12.2 us: partial_spans(): pl.pallas_call(partial_kernel, grid_spec=pltpu.PrefetchScalarGridSpec(num...]
    all_to_all x2 -> x0, waiting for transfers between devices: 22.5 us -> none  [the longest x1 22.5 us: per_device(): lax.all_to_all(code_values, 'node', split_axis=1, concat_axis=1, tiled=True)]
  transfers between devices with their start and end apart: 4 -> 2, of which waited for: 2 -> 1; matrix products, arithmetic and copies ran while one was open for 0% -> 0% of each run, Pallas kernels for 0% -> 17%
where the time goes in v1:
time: 120 us; the launch traced here: 118 us
  blocking collectives  64.2 us (54%)
  Pallas kernels  25.5 us (21%)
  between operations  14.1 us (12%)
  local copies, waits for them, and re-layouts  9.8 us (8%)
  waiting for transfers between devices  2.55 us (2%)
  starting transfers between devices  1.95 us (2%)
    all_to_all x1, blocking collectives, per_device(): got = lax.all_to_all(line, YZ, split_axis=0, concat_axis=0, tiled=True)  35.1 us
    all_to_all x1, blocking collectives, per_device(): got = lax.all_to_all(pair, X, split_axis=0, concat_axis=0, tiled=True)  29.1 us
    pallas_call x1, Pallas kernels, partial_spans(): pl.pallas_call(partial_kernel, grid_spec=pltpu.PrefetchScalarGridSpec(num...  12.2 us
    unnamed x16, local copies, waits for them, and re-layouts  9.8 us
    pallas_call x1, Pallas kernels, input_grads(): pl.pallas_call(grads_kernel, grid=(STEPS,), in_specs=[pl.BlockSpec((2 * F...  3.8 us
    pallas_call x1, Pallas kernels, pair_sum(): pl.pallas_call(pair_sum_kernel, grid=(steps,), in_specs=[spec, spec], out...  3.77 us
    ppermute x1, waiting for transfers between devices, per_device(): got = lax.ppermute(send, 'core', [(0, 1), (1, 0)])  2.53 us
  transfers between devices with their start and end apart: 2, of which 1 were waited for; matrix products, arithmetic and copies ran while one was open for 0% of the time, Pallas kernels for 17%

profile of v1, /device:TPU:6, one launch (start us, length us, event | category | flops | bytes accessed | tf_op | source)
XLA Modules:
  0.0 118.1 jit_solution(17629233285642936668)
XLA Ops:
  7.2 0.0 all-gather.2.cloned.1.call-start
  7.2 2.1 %shard_map.68 = bf16[32,8192]{1,0:T(8,128)(2,1)} custom-call(bf16[30,8192]{1,0:T(8,128)(2,1)} %codes_ref.1, bf16[30,64]{1,0:T(8,128)(2,1)} %scales_ref.1), custom_call_target="tpu_custom_call" | custom-call | flops 262144 | bytes 1048576 | tf_op jit(solution)/shard_map/pallas_call | solution.py:41
  9.4 0.0 all-gather.2.cloned.1.call-update
  9.4 0.0 copy-start
  9.4 2.2 %copy-done = bf16[256,8192]{1,0:T(8,128)(2,1)S(1)} copy-done((bf16[256,8192]{1,0:T(8,128)(2,1)S(1)}, bf16[256,8192]{1,0:T(8,128)(2,1)}, u32[]{:S(2)}) %copy-start) | copy-done | bytes 4194328
  11.6 0.0 copy-start.4
  11.6 0.9 copy-done.4
  12.5 0.0 copy-start.6
  12.5 0.7 copy-done.6
  13.2 12.2 %shard_map.70 = (f32[3840,128]{1,0:T(8,128)S(1)}, bf16[3840,128]{1,0:T(8,128)(2,1)S(1)}) custom-call(s32[768]{0:T(1024)S(1)} %copy-done.6, s32[1]{0:T(128)} %bitcast.2.core_ref, bf16[240,256]{1,0:T(8,128)(2,1)S(1)} %bitcast.7, bf16[256,8192]{1,0:T(8,128)(2,1)S(1)} %copy-done), custom_call_target="tpu_custom_call" | custom-call | flops 503316480 | bytes 7143424 | tf_op jit(solution)/shard_map/pallas_call | solution.py:89
  25.4 0.0 copy-start.3
  25.4 1.2 %copy-done.3 = f32[3840,128]{1,0:T(8,128)} copy-done((f32[3840,128]{1,0:T(8,128)}, f32[3840,128]{1,0:T(8,128)S(1)}, u32[]{:S(2)}) %copy-start.3) | copy-done | bytes 1966104
  26.7 1.9 %collective-permute-start = (bf16[3840,128]{1,0:T(8,128)(2,1)S(1)}, bf16[3840,128]{1,0:T(8,128)(2,1)S(1)}, u32[]{:S(2)}, u32[]{:S(2)}) collective-permute-start(bf16[3840,128]{1,0:T(8,128)(2,1)S(1)} %get-tuple-element.5), channel_id=1, source_target_pairs={{0,1},{1,0},{2,3},{3,2},{4,5},{5,4},{6,7},{7,6},{8,9},{9,8},{10,11... | collective-permute-start | bytes 2949128 | tf_op jit(solution)/shard_map/ppermute | solution.py:217
  28.6 2.5 %collective-permute-done.got_ref = bf16[3840,128]{1,0:T(8,128)(2,1)S(1)} collective-permute-done((bf16[3840,128]{1,0:T(8,128)(2,1)S(1)}, bf16[3840,128]{1,0:T(8,128)(2,1)S(1)}, u32[]{:S(2)}, u32[]{:S(2)}) %collective-permute-start) | collective-permute-done | bytes 983072 | tf_op jit(solution)/shard_map/ppermute | solution.py:217
  31.1 0.0 copy-start.7
  31.1 1.0 copy-done.7
  32.1 3.8 %shard_map.71 = bf16[3840,128]{1,0:T(8,128)(2,1)} custom-call(f32[3840,128]{1,0:T(8,128)} %copy-done.3, bf16[3840,128]{1,0:T(8,128)(2,1)} %copy-done.7), custom_call_target="tpu_custom_call" | custom-call | tf_op jit(solution)/shard_map/pallas_call | solution.py:167
  35.9 0.0 copy-start.5
  35.9 29.1 %all_to_all.16 = bf16[4,960,128]{2,1,0:T(8,128)(2,1)} all-to-all(bf16[4,960,128]{2,1,0:T(8,128)(2,1)} %bitcast.10), channel_id=1, replica_groups=mesh['y'=8,'z'=12,'xh'=2,'xl'=2,'core'=2] {'xh','xl'}, dimensions={0} | all-to-all | bytes 1966080 | tf_op jit(solution)/shard_map/all_to_all | solution.py:219
  65.0 2.0 %shard_map.72 = bf16[960,128]{1,0:T(8,128)(2,1)} custom-call(bf16[3840,128]{1,0:T(8,128)(2,1)} %bitcast.9), custom_call_target="tpu_custom_call" | custom-call | tf_op jit(solution)/shard_map/pallas_call | solution.py:184
  67.0 35.1 %all_to_all.17 = bf16[480,2,128]{2,1,0:T(2,128)(2,1)} all-to-all(bf16[480,2,128]{2,1,0:T(2,128)(2,1)} %bitcast.11), channel_id=1, replica_groups=mesh['y'=8,'z'=12,'xh'=2,'xl'=2,'core'=2] {'y','z'}, dimensions={0} | all-to-all | bytes 491520 | tf_op jit(solution)/shard_map/all_to_all | solution.py:221
  102.1 1.6 %shard_map.73 = f32[1,1280]{1,0:T(1,128)} custom-call(bf16[960,128]{1,0:T(8,128)(2,1)} %bitcast.12), custom_call_target="tpu_custom_call" | custom-call | tf_op jit(solution)/shard_map/pallas_call | solution.py:205
  103.7 0.0 all-gather.2.cloned.1.call-done.weight_ref
  103.7 0.0 copy-done.5
  103.7 0.0 copy-start.1
  103.7 2.2 %copy-done.1 = bf16[256,8192]{1,0:T(8,128)(2,1)S(1)} copy-done((bf16[256,8192]{1,0:T(8,128)(2,1)S(1)}, bf16[256,8192]{1,0:T(8,128)(2,1)}, u32[]{:S(2)}) %copy-start.1) | copy-done | bytes 4194328
  105.9 0.0 copy-start.2
  105.9 1.6 %copy-done.2 = bf16[128,8192]{1,0:T(8,128)(2,1)S(1)} copy-done((bf16[128,8192]{1,0:T(8,128)(2,1)S(1)}, bf16[128,8192]{1,0:T(8,128)(2,1)}, u32[]{:S(2)}) %copy-start.2) | copy-done | bytes 2097176
  107.5 3.8 %shard_map.69 = bf16[240,256]{1,0:T(8,128)(2,1)} custom-call(bf16[240,256]{1,0:T(8,128)(2,1)S(1)} %bitcast.8, bf16[128,8192]{1,0:T(8,128)(2,1)S(1)} %copy-done.2, bf16[256,8192]{1,0:T(8,128)(2,1)S(1)} %copy-done.1), custom_call_target="tpu_custom_call" | custom-call | flops 503316480 | bytes 6291456 | tf_op jit(solution)/shard_map/pallas_call | solution.py:144
Async XLA Ops:
  7.2 96.5 %all-gather.2.cloned.1.call-start = ((), (), s32[]{:S(2)}) async-start(), calls=%async_computation.2 | async-start | bytes 2621440 | tf_op jit(solution)/shard_map/all_gather | solution.py:215
  9.4 2.2 %copy-start = (bf16[256,8192]{1,0:T(8,128)(2,1)S(1)}, bf16[256,8192]{1,0:T(8,128)(2,1)}, u32[]{:S(2)}) copy-start(bf16[256,8192]{1,0:T(8,128)(2,1)} %out_grad_ref.3) | copy-start | bytes 12582916
  11.6 0.9 copy-start.4
  12.5 0.7 copy-start.6
  25.4 1.3 %copy-start.3 = (f32[3840,128]{1,0:T(8,128)}, f32[3840,128]{1,0:T(8,128)S(1)}, u32[]{:S(2)}) copy-start(f32[3840,128]{1,0:T(8,128)S(1)} %get-tuple-element.4.keep_ref) | copy-start | bytes 5898244
  26.7 4.4 %collective-permute-start = (bf16[3840,128]{1,0:T(8,128)(2,1)S(1)}, bf16[3840,128]{1,0:T(8,128)(2,1)S(1)}, u32[]{:S(2)}, u32[]{:S(2)}) collective-permute-start(bf16[3840,128]{1,0:T(8,128)(2,1)S(1)} %get-tuple-element.5), channel_id=1, source_target_pairs={{0,1},{1,0},{2,3},{3,2},{4,5},{5,4},{6,7},{7,6},{8,9},{9,8},{10,11... | collective-permute-start | bytes 2949128 | tf_op jit(solution)/shard_map/ppermute | solution.py:217
  31.1 1.0 copy-start.7
  35.9 67.8 %copy-start.5 = (bf16[256,240]{0,1:T(8,128)(2,1)S(1)}, bf16[256,240]{0,1:T(8,128)(2,1)}, u32[]{:S(2)}) copy-start(bf16[256,240]{0,1:T(8,128)(2,1)} %param.5) | copy-start | bytes 368644
  103.7 2.2 %copy-start.1 = (bf16[256,8192]{1,0:T(8,128)(2,1)S(1)}, bf16[256,8192]{1,0:T(8,128)(2,1)}, u32[]{:S(2)}) copy-start(bf16[256,8192]{1,0:T(8,128)(2,1)} %out_grad_ref.3) | copy-start | bytes 12582916
  105.9 1.6 %copy-start.2 = (bf16[128,8192]{1,0:T(8,128)(2,1)S(1)}, bf16[128,8192]{1,0:T(8,128)(2,1)}, u32[]{:S(2)}) copy-start(bf16[128,8192]{1,0:T(8,128)(2,1)} %all-gather.2.cloned.1.call-done.weight_ref) | copy-start | bytes 6291460
Sparse Core Ops, SparseCore 0:
  10.4 44.7 all-gather.1

commit v2 on v1

v2 whole, which is shorter than its diff:
```python
import jax
import jax.numpy as jnp
from jax import lax
from jax.experimental import pallas as pl
from jax.experimental.pallas import tpu as pltpu
from jax.sharding import Mesh
from jax.sharding import PartitionSpec as P

D = 8192
FW = 120
TOK = 256
QBLK = 128
SPAN = 10
DEVICES = 768
NY, NZ = 8, 12
NX = 4
NYZ = NY * NZ
ROWS = DEVICES * SPAN
HALF = ROWS // 2
XROWS = HALF // NX
NODE_ROWS = 30
PAD_ROWS = 32
BLOCKS = D // QBLK
STEP_BLOCKS = 8
STEPS = BLOCKS // STEP_BLOCKS
WIDTH = STEP_BLOCKS * QBLK
SWAP = [(0, 1), (1, 0)]
ALL = ("y", "z", "xh", "xl", "core")
X = ("xh", "xl")
YZ = ("y", "z")


def partial_kernel(
    order_ref, core_ref, gate_up_ref, out_grad_ref, codes_ref, scales_ref, keep_ref, send_ref, weight_ref, hidden, blocks, staged
):
    step = pl.program_id(0)

    @pl.when(step == 0)
    def _():
        both = gate_up_ref[...].astype(jnp.float32)
        gate, up = both[:FW], both[FW:]
        hidden[...] = (gate * jax.nn.sigmoid(gate) * up).astype(jnp.bfloat16)

    product = jnp.dot(hidden[...], out_grad_ref[...], preferred_element_type=jnp.float32)
    for block in range(STEP_BLOCKS):
        blocks[pl.ds(step * STEP_BLOCKS + block, FW, stride=BLOCKS), :] = product[:, block * QBLK : (block + 1) * QBLK]

    block_of = lax.broadcasted_iota(jnp.int32, (BLOCKS, WIDTH), 1) // QBLK + step * STEP_BLOCKS
    one_hot = (lax.broadcasted_iota(jnp.int32, (BLOCKS, WIDTH), 0) == block_of).astype(jnp.float32).astype(jnp.bfloat16)
    scales = jnp.dot(scales_ref[...], one_hot, preferred_element_type=jnp.float32)
    weight = codes_ref[...].astype(jnp.float32) * scales
    fill = jnp.zeros((PAD_ROWS - NODE_ROWS, WIDTH), jnp.float32)
    weight_ref[...] = jnp.concatenate([weight, fill], axis=0).astype(jnp.bfloat16)

    @pl.when(step == STEPS - 1)
    def _():
        core = core_ref[0]
        first = (core * HALF, (1 - core) * HALF)

        def gather(yz, carry):
            for low in range(8):
                span = order_ref[yz * 8 + low]
                place = first[low % 2] + ((low // 2) * NYZ + yz) * SPAN
                staged[pl.ds(place, SPAN), :] = blocks[pl.ds(span * SPAN, SPAN), :]
            return carry

        lax.fori_loop(0, NYZ, gather, 0)
        keep_ref[...] = staged[:HALF, :].astype(jnp.bfloat16)
        send_ref[...] = staged[HALF:, :].astype(jnp.bfloat16)


def partial_spans(order, core, gate_up_t, out_grad, codes, scales):
    whole = lambda i, *_: (0, 0)
    columns = lambda i, *_: (0, i)
    return pl.pallas_call(
        partial_kernel,
        grid_spec=pltpu.PrefetchScalarGridSpec(
            num_scalar_prefetch=2,
            grid=(STEPS,),
            in_specs=[
                pl.BlockSpec((2 * FW, TOK), whole),
                pl.BlockSpec((TOK, WIDTH), columns),
                pl.BlockSpec((NODE_ROWS, WIDTH), columns),
                pl.BlockSpec((NODE_ROWS, BLOCKS), whole),
            ],
            out_specs=[
                pl.BlockSpec((HALF, QBLK), whole),
                pl.BlockSpec((HALF, QBLK), whole),
                pl.BlockSpec((PAD_ROWS, WIDTH), columns),
            ],
            scratch_shapes=[
                pltpu.VMEM((FW, TOK), jnp.bfloat16),
                pltpu.VMEM((ROWS, QBLK), jnp.float32),
                pltpu.VMEM((ROWS, QBLK), jnp.float32),
            ],
        ),
        out_shape=[
            jax.ShapeDtypeStruct((HALF, QBLK), jnp.bfloat16),
            jax.ShapeDtypeStruct((HALF, QBLK), jnp.bfloat16),
            jax.ShapeDtypeStruct((PAD_ROWS, D), jnp.bfloat16),
        ],
        compiler_params=pltpu.CompilerParams(vmem_limit_bytes=56 * 2**20),
        cost_estimate=pl.CostEstimate(flops=2 * FW * TOK * D, bytes_accessed=2 * TOK * D + 4 * HALF * QBLK, transcendentals=FW * TOK),
    )(order, core, gate_up_t, out_grad, codes, scales)


def grads_kernel(place_ref, gate_up_ref, own_ref, core_ref, x_ref, both_ref, out_grad_ref, out_ref, weight, total):
    step = pl.program_id(0)
    for i, part in enumerate((own_ref, core_ref, x_ref, both_ref)):
        row = pl.multiple_of(jnp.bitwise_xor(place_ref[0], i) * PAD_ROWS, PAD_ROWS)
        weight[pl.ds(row, PAD_ROWS), :] = part[...]
    product = lax.dot_general(
        weight[...], out_grad_ref[...], (((1,), (1,)), ((), ())), preferred_element_type=jnp.float32
    )

    @pl.when(step == 0)
    def _():
        total[...] = product

    @pl.when(step > 0)
    def _():
        total[...] += product

    @pl.when(step == STEPS - 1)
    def _():
        hidden_grad = jnp.concatenate(
            [total[i * PAD_ROWS : i * PAD_ROWS + NODE_ROWS, :] for i in range(4)], axis=0
        )
        both = gate_up_ref[...].astype(jnp.float32)
        gate, up = both[:FW], both[FW:]
        sig = jax.nn.sigmoid(gate)
        gate_grad = hidden_grad * up * sig * (1.0 + gate * (1.0 - sig))
        up_grad = hidden_grad * (gate * sig)
        out_ref[...] = jnp.concatenate([gate_grad, up_grad], axis=0).astype(jnp.bfloat16)


def input_grads(place, gate_up_t, parts, out_grad):
    whole = lambda i, *_: (0, 0)
    columns = lambda i, *_: (0, i)
    return pl.pallas_call(
        grads_kernel,
        grid_spec=pltpu.PrefetchScalarGridSpec(
            num_scalar_prefetch=1,
            grid=(STEPS,),
            in_specs=[pl.BlockSpec((2 * FW, TOK), whole)]
            + [pl.BlockSpec((PAD_ROWS, WIDTH), columns)] * 4
            + [pl.BlockSpec((TOK, WIDTH), columns)],
            out_specs=pl.BlockSpec((2 * FW, TOK), whole),
            scratch_shapes=[
                pltpu.VMEM((4 * PAD_ROWS, WIDTH), jnp.bfloat16),
                pltpu.VMEM((4 * PAD_ROWS, TOK), jnp.float32),
            ],
        ),
        out_shape=jax.ShapeDtypeStruct((2 * FW, TOK), jnp.bfloat16),
        compiler_params=pltpu.CompilerParams(vmem_limit_bytes=56 * 2**20),
        cost_estimate=pl.CostEstimate(flops=2 * FW * TOK * D, bytes_accessed=2 * TOK * D + 2 * 128 * D, transcendentals=FW * TOK),
    )(place, gate_up_t, *parts, out_grad)


def last_sum_kernel(got_ref, out_ref, total):
    rows = 8 * SPAN
    eight = got_ref[:rows, :].astype(jnp.float32)
    for i in range(1, XROWS // rows):
        eight += got_ref[i * rows : (i + 1) * rows, :].astype(jnp.float32)
    total[...] = eight
    span = total[:SPAN, :]
    for i in range(1, 8):
        span += total[i * SPAN : (i + 1) * SPAN, :]
    span = span * (1.0 / DEVICES)
    for i in range(SPAN):
        out_ref[:, i * QBLK : (i + 1) * QBLK] = span[i : i + 1, :]


def last_sum(got):
    return pl.pallas_call(
        last_sum_kernel,
        out_shape=jax.ShapeDtypeStruct((1, SPAN * QBLK), jnp.float32),
        scratch_shapes=[pltpu.VMEM((8 * SPAN, QBLK), jnp.float32)],
    )(got)


def per_device(gate_up, out_grad, weight_codes, weight_scales, shard_order):
    gate_up_t = gate_up.T
    core = lax.axis_index("core").astype(jnp.int32).reshape(1)
    place = lax.axis_index(("xl", "core")).astype(jnp.int32).reshape(1)
    keep, send, weight = partial_spans(shard_order, core, gate_up_t, out_grad, weight_codes, weight_scales)
    got = lax.ppermute(send, "core", SWAP)
    pair = (keep.astype(jnp.float32) + got.astype(jnp.float32)).astype(jnp.bfloat16)
    got = lax.all_to_all(pair, X, split_axis=0, concat_axis=0, tiled=True)
    parts = [got[i * XROWS : (i + 1) * XROWS].astype(jnp.float32) for i in range(NX)]
    line = (parts[0] + parts[1] + parts[2] + parts[3]).astype(jnp.bfloat16)
    line, weight = lax.optimization_barrier((line, weight))
    weight_x = lax.ppermute(weight, "xl", SWAP)
    weight_core = lax.ppermute(weight, "core", SWAP)
    weight_both = lax.ppermute(weight_x, "core", SWAP)
    got = lax.all_to_all(line.reshape(XROWS // 2, 2, QBLK), YZ, split_axis=0, concat_axis=0, tiled=True)
    grad_gate_up = input_grads(place, gate_up_t, (weight, weight_core, weight_x, weight_both), out_grad).T
    weight_grad = last_sum(got.reshape(XROWS, QBLK))
    return (grad_gate_up, weight_grad)


def solution(mesh):
    fine = Mesh(mesh.devices.reshape(NY, NZ, 2, 2, 2), ALL)
    return jax.shard_map(
        per_device,
        mesh=fine,
        in_specs=(P(ALL, None), P(ALL, None), P(("xl", "core"), None), P(("xl", "core"), None), P()),
        out_specs=(P(ALL, None), P(ALL, None)),
        check_vma=False,
    )
```

time: 120 us -> 90 us (0.75)
  the two profiles are of different devices: /device:TPU:6 before, /device:TPU:2 now
where the time goes in v2:
time: 90 us; the launch traced here: 89.3 us
  blocking collectives  25.6 us (28%)
  starting transfers between devices  24 us (27%)
  Pallas kernels  19.5 us (22%)
  waiting for transfers between devices  15.6 us (17%)
  other arithmetic  2.27 us (3%)
  local copies, waits for them, and re-layouts  1.66 us (2%)
    all_to_all x1, blocking collectives, per_device(): got = lax.all_to_all(pair, X, split_axis=0, concat_axis=0, tiled=True)  25.6 us
    all_to_all x1, starting transfers between devices, per_device(): lax.all_to_all(line.reshape(XROWS // 2, 2, QBLK), YZ, split_axis=0, conca...  14.4 us
    all_to_all x1, waiting for transfers between devices, per_device(): lax.all_to_all(line.reshape(XROWS // 2, 2, QBLK), YZ, split_axis=0, conca...  12.8 us
    pallas_call x1, Pallas kernels, partial_spans(): pl.pallas_call(partial_kernel, grid_spec=pltpu.PrefetchScalarGridSpec(num...  10.7 us
    pallas_call x1, Pallas kernels, input_grads(): pl.pallas_call(grads_kernel, grid_spec=pltpu.PrefetchScalarGridSpec(num_s...  7.2 us
    ppermute x1, starting transfers between devices, per_device(): weight_x = lax.ppermute(weight, 'xl', SWAP)  3.36 us
    ppermute x1, waiting for transfers between devices, per_device(): got = lax.ppermute(send, 'core', SWAP)  2.74 us
    ppermute x1, starting transfers between devices, per_device(): weight_both = lax.ppermute(weight_x, 'core', SWAP)  2.41 us
  transfers between devices with their start and end apart: 5, of which 2 were waited for; matrix products, arithmetic and copies ran while one was open for 0% of the time, Pallas kernels for 2%

profile of v2, /device:TPU:2, one launch (start us, length us, event | category | flops | bytes accessed | tf_op | source)
XLA Modules:
  0.0 89.3 jit_solution(8791201791951636503)
XLA Ops:
  0.6 10.7 %shard_map.68 = (bf16[3840,128]{1,0:T(8,128)(2,1)}, bf16[3840,128]{1,0:T(8,128)(2,1)}, bf16[32,8192]{1,0:T(8,128)(2,1)}) custom-call(s32[768]{0:T(1024)} %order_ref.1, s32[1]{0:T(128)} %bitcast.2.core_ref, bf16[240,256]{1,0:T(8,128)(2,1)} %bitcast.11, bf16[256,8192]{1,0:T(8,128)(2,1)} %out_grad_ref.3, bf16[30,8192]{1,0:T(8,128)(2,1)} %codes_ref.1, ...), custom_call_target="tpu_custom_call" | custom-call | flops 503316480 | bytes 6160384 | tf_op jit(solution)/shard_map/pallas_call | solution.py:75
  11.3 1.9 %collective-permute-start = (bf16[3840,128]{1,0:T(8,128)(2,1)}, bf16[3840,128]{1,0:T(8,128)(2,1)S(1)}, u32[]{:S(2)}, u32[]{:S(2)}) collective-permute-start(bf16[3840,128]{1,0:T(8,128)(2,1)} %get-tuple-element.8), channel_id=1, source_target_pairs={{0,1},{1,0},{2,3},{3,2},{4,5},{5,4},{6,7},{7,6},{8,9},{9,8},{10,11... | collective-permute-start | bytes 2949128 | tf_op jit(solution)/shard_map/ppermute | solution.py:187
  13.3 2.7 %collective-permute-done = bf16[3840,128]{1,0:T(8,128)(2,1)S(1)} collective-permute-done((bf16[3840,128]{1,0:T(8,128)(2,1)}, bf16[3840,128]{1,0:T(8,128)(2,1)S(1)}, u32[]{:S(2)}, u32[]{:S(2)}) %collective-permute-start) | collective-permute-done | bytes 983072 | tf_op jit(solution)/shard_map/ppermute | solution.py:187
  16.0 1.5 %add_convert_fusion = bf16[3840,128]{1,0:T(8,128)(2,1)S(1)} fusion(bf16[3840,128]{1,0:T(8,128)(2,1)S(1)} %collective-permute-done, bf16[3840,128]{1,0:T(8,128)(2,1)} %get-tuple-element.7), kind=kLoop, calls=%fused_computation | loop fusion | flops 1966080 | bytes 2949120 | tf_op jit(solution)/shard_map/convert_element_type | solution.py:188
  17.5 0.0 copy-start.1
  17.5 25.6 %all_to_all.14 = bf16[4,960,128]{2,1,0:T(8,128)(2,1)S(1)} all-to-all(bf16[4,960,128]{2,1,0:T(8,128)(2,1)S(1)} %bitcast.9), channel_id=1, replica_groups=mesh['y'=8,'z'=12,'xh'=2,'xl'=2,'core'=2] {'xh','xl'}, dimensions={0} | all-to-all | bytes 1966080 | tf_op jit(solution)/shard_map/all_to_all | solution.py:189
  43.1 0.8 fusion
  43.9 0.0 copy-done.1
  43.9 3.4 %collective-permute-start.2 = (bf16[32,8192]{1,0:T(8,128)(2,1)S(1)}, bf16[32,8192]{1,0:T(8,128)(2,1)S(1)}, u32[]{:S(2)}, u32[]{:S(2)}) collective-permute-start(bf16[32,8192]{1,0:T(8,128)(2,1)S(1)} %copy-done.1), channel_id=1, source_target_pairs={{0,2},{2,0},{1,3},{3,1},{4,6},{6,4},{5,7},{7,5},{8,10},{10,8},{9,1... | collective-permute-start | bytes 1572872 | tf_op jit(solution)/shard_map/ppermute | solution.py:193
  47.3 14.4 %all-to-all-start.1 = ((bf16[480,2,128]{2,1,0:T(2,128)(2,1)}), bf16[480,2,128]{2,1,0:T(2,128)(2,1)S(1)}, u32[]{:S(2)}, u32[]{:S(2)}) async-start(bf16[480,2,128]{2,1,0:T(2,128)(2,1)} %bitcast.6), calls=%async_computation.1 | async-start | bytes 491520 | tf_op jit(solution)/shard_map/all_to_all | solution.py:196
  61.7 1.9 %collective-permute-start.1 = (bf16[32,8192]{1,0:T(8,128)(2,1)S(1)}, bf16[32,8192]{1,0:T(8,128)(2,1)S(1)}, u32[]{:S(2)}, u32[]{:S(2)}) collective-permute-start(bf16[32,8192]{1,0:T(8,128)(2,1)S(1)} %copy-done.1), channel_id=1, source_target_pairs={{0,1},{1,0},{2,3},{3,2},{4,5},{5,4},{6,7},{7,6},{8,9},{9,8},{10,11... | collective-permute-start | bytes 1572872 | tf_op jit(solution)/shard_map/ppermute | solution.py:194
  63.6 0.0 collective-permute-done.2.x_ref
  63.6 0.0 copy-start.2
  63.6 2.4 %collective-permute-start.3 = (bf16[32,8192]{1,0:T(8,128)(2,1)S(1)}, bf16[32,8192]{1,0:T(8,128)(2,1)S(1)}, u32[]{:S(2)}, u32[]{:S(2)}) collective-permute-start(bf16[32,8192]{1,0:T(8,128)(2,1)S(1)} %collective-permute-done.2.x_ref), channel_id=1, source_target_pairs={{0,1},{1,0},{2,3},{3,2},{4,5},{5,4},{6,7},{7,6},{8,9},{9,8},{10,11... | collective-permute-start | bytes 1572872 | tf_op jit(solution)/shard_map/ppermute | solution.py:195
  66.0 12.8 %all-to-all-done.1 = bf16[480,2,128]{2,1,0:T(2,128)(2,1)S(1)} async-done(((bf16[480,2,128]{2,1,0:T(2,128)(2,1)}), bf16[480,2,128]{2,1,0:T(2,128)(2,1)S(1)}, u32[]{:S(2)}, u32[]{:S(2)}) %all-to-all-start.1) | async-done | bytes 245792 | tf_op jit(solution)/shard_map/all_to_all | solution.py:196
  78.9 0.0 copy-start
  78.9 0.7 copy-done
  79.5 1.6 %shard_map.70 = f32[1,1280]{1,0:T(1,128)} custom-call(bf16[960,128]{1,0:T(8,128)(2,1)} %bitcast.10), custom_call_target="tpu_custom_call" | custom-call | tf_op jit(solution)/shard_map/pallas_call | solution.py:175
  81.1 0.0 collective-permute-done.1.core_ref
  81.1 0.0 copy-start.3
  81.1 0.0 collective-permute-done.3.both_ref
  81.1 0.0 copy-start.4
  81.2 0.0 copy-done.2
  81.2 0.8 copy-done.3
  81.9 0.2 copy-done.4
  82.1 7.2 %shard_map.69 = bf16[240,256]{1,0:T(8,128)(2,1)} custom-call(s32[1]{0:T(128)} %bitcast.place_ref, bf16[240,256]{1,0:T(8,128)(2,1)} %bitcast.12, bf16[32,8192]{1,0:T(8,128)(2,1)} %get-tuple-element.10.own_ref, bf16[32,8192]{1,0:T(8,128)(2,1)} %copy-done.3, bf16[32,8192]{1,0:T(8,128)(2,1)} %copy-done.2, bf16[32,8192]{1,0:T(8,128)(2,1)} %copy-done.4, ...), custom_call_target="tpu_custom_call" | custom-call | flops 503316480 | bytes 6291456 | tf_op jit(solution)/shard_map/pallas_call | solution.py:140
Async XLA Ops:
  11.3 4.7 %collective-permute-start = (bf16[3840,128]{1,0:T(8,128)(2,1)}, bf16[3840,128]{1,0:T(8,128)(2,1)S(1)}, u32[]{:S(2)}, u32[]{:S(2)}) collective-permute-start(bf16[3840,128]{1,0:T(8,128)(2,1)} %get-tuple-element.8), channel_id=1, source_target_pairs={{0,1},{1,0},{2,3},{3,2},{4,5},{5,4},{6,7},{7,6},{8,9},{9,8},{10,11... | collective-permute-start | bytes 2949128 | tf_op jit(solution)/shard_map/ppermute | solution.py:187
  17.5 26.4 %copy-start.1 = (bf16[32,8192]{1,0:T(8,128)(2,1)S(1)}, bf16[32,8192]{1,0:T(8,128)(2,1)}, u32[]{:S(2)}) copy-start(bf16[32,8192]{1,0:T(8,128)(2,1)} %get-tuple-element.10.own_ref) | copy-start | bytes 1572868
  43.9 19.7 %collective-permute-start.2 = (bf16[32,8192]{1,0:T(8,128)(2,1)S(1)}, bf16[32,8192]{1,0:T(8,128)(2,1)S(1)}, u32[]{:S(2)}, u32[]{:S(2)}) collective-permute-start(bf16[32,8192]{1,0:T(8,128)(2,1)S(1)} %copy-done.1), channel_id=1, source_target_pairs={{0,2},{2,0},{1,3},{3,1},{4,6},{6,4},{5,7},{7,5},{8,10},{10,8},{9,1... | collective-permute-start | bytes 1572872 | tf_op jit(solution)/shard_map/ppermute | solution.py:193
  47.3 31.6 %all-to-all-start.1 = ((bf16[480,2,128]{2,1,0:T(2,128)(2,1)}), bf16[480,2,128]{2,1,0:T(2,128)(2,1)S(1)}, u32[]{:S(2)}, u32[]{:S(2)}) async-start(bf16[480,2,128]{2,1,0:T(2,128)(2,1)} %bitcast.6), calls=%async_computation.1 | async-start | bytes 491520 | tf_op jit(solution)/shard_map/all_to_all | solution.py:196
  61.7 19.5 %collective-permute-start.1 = (bf16[32,8192]{1,0:T(8,128)(2,1)S(1)}, bf16[32,8192]{1,0:T(8,128)(2,1)S(1)}, u32[]{:S(2)}, u32[]{:S(2)}) collective-permute-start(bf16[32,8192]{1,0:T(8,128)(2,1)S(1)} %copy-done.1), channel_id=1, source_target_pairs={{0,1},{1,0},{2,3},{3,2},{4,5},{5,4},{6,7},{7,6},{8,9},{9,8},{10,11... | collective-permute-start | bytes 1572872 | tf_op jit(solution)/shard_map/ppermute | solution.py:194
  63.6 17.5 %copy-start.2 = (bf16[32,8192]{1,0:T(8,128)(2,1)}, bf16[32,8192]{1,0:T(8,128)(2,1)S(1)}, u32[]{:S(2)}) copy-start(bf16[32,8192]{1,0:T(8,128)(2,1)S(1)} %collective-permute-done.2.x_ref) | copy-start | bytes 1572868
  63.6 17.5 %collective-permute-start.3 = (bf16[32,8192]{1,0:T(8,128)(2,1)S(1)}, bf16[32,8192]{1,0:T(8,128)(2,1)S(1)}, u32[]{:S(2)}, u32[]{:S(2)}) collective-permute-start(bf16[32,8192]{1,0:T(8,128)(2,1)S(1)} %collective-permute-done.2.x_ref), channel_id=1, source_target_pairs={{0,1},{1,0},{2,3},{3,2},{4,5},{5,4},{6,7},{7,6},{8,9},{9,8},{10,11... | collective-permute-start | bytes 1572872 | tf_op jit(solution)/shard_map/ppermute | solution.py:195
  78.9 0.7 copy-start
  81.1 0.8 copy-start.3
  81.1 1.0 %copy-start.4 = (bf16[32,8192]{1,0:T(8,128)(2,1)}, bf16[32,8192]{1,0:T(8,128)(2,1)S(1)}, u32[]{:S(2)}) copy-start(bf16[32,8192]{1,0:T(8,128)(2,1)S(1)} %collective-permute-done.3.both_ref) | copy-start | bytes 1572868

commit v3 on v2

v3 whole, which is shorter than its diff:
```python
import jax
import jax.numpy as jnp
from jax import lax
from jax.experimental import pallas as pl
from jax.experimental.pallas import tpu as pltpu
from jax.sharding import Mesh
from jax.sharding import PartitionSpec as P

D = 8192
FW = 120
TOK = 256
QBLK = 128
SPAN = 10
DEVICES = 768
NY, NZ = 8, 12
NX = 4
ROWS = DEVICES * SPAN
HALF = ROWS // 2
NODE_ROWS = 30
PAD_ROWS = 32
BLOCKS = D // QBLK
STEP_BLOCKS = 16
STEPS = BLOCKS // STEP_BLOCKS
WIDTH = STEP_BLOCKS * QBLK
SWAP = [(0, 1), (1, 0)]
ALL = ("y", "z", "xh", "xl", "core")
PLANE = ("y", "xh", "xl")


def read_columns(source, target, sems, chunk):
    columns = pl.ds(chunk * WIDTH, WIDTH)
    return pltpu.make_async_copy(source.at[:, columns], target.at[:, columns], sems.at[chunk])


def partial_kernel(
    core_ref, order_hbm, gate_up_hbm, out_grad_hbm, codes_hbm, scales_hbm, keep_ref, send_ref, weight_ref,
    order, gate_up, codes, scales, out_grad, blocks, staged, sems, small_sems,
):
    small = [
        pltpu.make_async_copy(source, target, small_sems.at[i])
        for i, (source, target) in enumerate(
            ((gate_up_hbm, gate_up), (scales_hbm, scales), (codes_hbm, codes), (order_hbm, order))
        )
    ]
    small[0].start()
    for chunk in range(STEPS):
        read_columns(out_grad_hbm, out_grad, sems, chunk).start()
    for read in small[1:]:
        read.start()
    small[0].wait()
    both = gate_up[...].astype(jnp.float32)
    gate, up = both[:FW], both[FW:]
    hidden = (gate * jax.nn.sigmoid(gate) * up).astype(jnp.bfloat16)
    for chunk in range(STEPS):
        columns = slice(chunk * WIDTH, (chunk + 1) * WIDTH)
        read_columns(out_grad_hbm, out_grad, sems, chunk).wait()
        product = jnp.dot(hidden, out_grad[:, columns], preferred_element_type=jnp.float32)
        for block in range(STEP_BLOCKS):
            blocks[pl.ds(chunk * STEP_BLOCKS + block, FW, stride=BLOCKS), :] = product[:, block * QBLK : (block + 1) * QBLK]
    for read in small[1:]:
        read.wait()
    fill = jnp.zeros((PAD_ROWS - NODE_ROWS, WIDTH), jnp.float32)
    for chunk in range(STEPS):
        columns = slice(chunk * WIDTH, (chunk + 1) * WIDTH)
        block_of = lax.broadcasted_iota(jnp.int32, (BLOCKS, WIDTH), 1) // QBLK + chunk * STEP_BLOCKS
        one_hot = (lax.broadcasted_iota(jnp.int32, (BLOCKS, WIDTH), 0) == block_of).astype(jnp.float32)
        wide = jnp.dot(scales[...], one_hot.astype(jnp.bfloat16), preferred_element_type=jnp.float32)
        weight = codes[:, columns].astype(jnp.float32) * wide
        weight_ref[:, columns] = jnp.concatenate([weight, fill], axis=0).astype(jnp.bfloat16)

    core = core_ref[0]
    first = (core * HALF, (1 - core) * HALF)

    def gather(y, carry):
        for z in range(NZ):
            for low in range(8):
                span = order[y * (8 * NZ) + z * 8 + low]
                place = first[low % 2] + y * (NX * NZ * SPAN) + ((low // 2) * NZ + z) * SPAN
                staged[pl.ds(place, SPAN), :] = blocks[pl.ds(span * SPAN, SPAN), :]
        return carry

    lax.fori_loop(0, NY, gather, 0)
    keep_ref[...] = staged[:HALF, :].astype(jnp.bfloat16)
    send_ref[...] = staged[HALF:, :].astype(jnp.bfloat16)


def partial_spans(order, core, gate_up_t, out_grad, codes, scales):
    hbm = pl.BlockSpec(memory_space=pltpu.HBM)
    vmem = pl.BlockSpec(memory_space=pltpu.VMEM)
    return pl.pallas_call(
        partial_kernel,
        in_specs=[pl.BlockSpec(memory_space=pltpu.SMEM)] + [hbm] * 5,
        out_specs=[vmem, vmem, vmem],
        scratch_shapes=[
            pltpu.SMEM((DEVICES,), jnp.int32),
            pltpu.VMEM((2 * FW, TOK), jnp.bfloat16),
            pltpu.VMEM((NODE_ROWS, D), jnp.bfloat16),
            pltpu.VMEM((NODE_ROWS, BLOCKS), jnp.bfloat16),
            pltpu.VMEM((TOK, D), jnp.bfloat16),
            pltpu.VMEM((ROWS, QBLK), jnp.float32),
            pltpu.VMEM((ROWS, QBLK), jnp.float32),
            pltpu.SemaphoreType.DMA((STEPS,)),
            pltpu.SemaphoreType.DMA((4,)),
        ],
        out_shape=[
            jax.ShapeDtypeStruct((HALF, QBLK), jnp.bfloat16),
            jax.ShapeDtypeStruct((HALF, QBLK), jnp.bfloat16),
            jax.ShapeDtypeStruct((PAD_ROWS, D), jnp.bfloat16),
        ],
        compiler_params=pltpu.CompilerParams(vmem_limit_bytes=56 * 2**20),
        cost_estimate=pl.CostEstimate(flops=2 * FW * TOK * D, bytes_accessed=2 * TOK * D + 4 * HALF * QBLK, transcendentals=FW * TOK),
    )(core, order, gate_up_t, out_grad, codes, scales)


def grads_kernel(place_ref, gate_up_ref, own_hbm, core_hbm, x_hbm, both_hbm, out_grad_hbm, out_ref, weight, out_grad, weight_sems, sems):
    reads = []
    for i, part in enumerate((own_hbm, core_hbm, x_hbm, both_hbm)):
        row = pl.multiple_of(jnp.bitwise_xor(place_ref[0], i) * PAD_ROWS, PAD_ROWS)
        reads.append(pltpu.make_async_copy(part, weight.at[pl.ds(row, PAD_ROWS), :], weight_sems.at[i]))
        reads[-1].start()
    for chunk in range(STEPS):
        read_columns(out_grad_hbm, out_grad, sems, chunk).start()
    both = gate_up_ref[...].astype(jnp.float32)
    gate, up = both[:FW], both[FW:]
    sig = jax.nn.sigmoid(gate)
    for read in reads:
        read.wait()
    total = jnp.zeros((TOK, 4 * PAD_ROWS), jnp.float32)
    for chunk in range(STEPS):
        columns = slice(chunk * WIDTH, (chunk + 1) * WIDTH)
        read_columns(out_grad_hbm, out_grad, sems, chunk).wait()
        total += lax.dot_general(
            out_grad[:, columns], weight[:, columns], (((1,), (1,)), ((), ())), preferred_element_type=jnp.float32
        )
    total = total.T
    hidden_grad = jnp.concatenate([total[i * PAD_ROWS : i * PAD_ROWS + NODE_ROWS, :] for i in range(4)], axis=0)
    gate_grad = hidden_grad * up * sig * (1.0 + gate * (1.0 - sig))
    up_grad = hidden_grad * (gate * sig)
    out_ref[...] = jnp.concatenate([gate_grad, up_grad], axis=0).astype(jnp.bfloat16)


def input_grads(place, gate_up_t, parts, out_grad):
    smem = pl.BlockSpec(memory_space=pltpu.SMEM)
    vmem = pl.BlockSpec(memory_space=pltpu.VMEM)
    anywhere = pl.BlockSpec(memory_space=pl.ANY)
    return pl.pallas_call(
        grads_kernel,
        in_specs=[smem, vmem] + [anywhere] * 4 + [pl.BlockSpec(memory_space=pltpu.HBM)],
        out_specs=vmem,
        scratch_shapes=[
            pltpu.VMEM((4 * PAD_ROWS, D), jnp.bfloat16),
            pltpu.VMEM((TOK, D), jnp.bfloat16),
            pltpu.SemaphoreType.DMA((4,)),
            pltpu.SemaphoreType.DMA((STEPS,)),
        ],
        out_shape=jax.ShapeDtypeStruct((2 * FW, TOK), jnp.bfloat16),
        compiler_params=pltpu.CompilerParams(vmem_limit_bytes=56 * 2**20),
        cost_estimate=pl.CostEstimate(flops=2 * FW * TOK * D, bytes_accessed=2 * TOK * D + 2 * 128 * D, transcendentals=FW * TOK),
    )(place, gate_up_t, *parts, out_grad)


def plane_sum_kernel(got_ref, out_ref):
    rows = 2 * NZ * SPAN
    total = got_ref[:rows, :].astype(jnp.float32)
    for i in range(1, HALF // rows):
        total += got_ref[i * rows : (i + 1) * rows, :].astype(jnp.float32)
    out_ref[...] = (total[: rows // 2] + total[rows // 2 :]).astype(jnp.bfloat16)


def plane_sum(got):
    return pl.pallas_call(
        plane_sum_kernel,
        in_specs=[pl.BlockSpec(memory_space=pltpu.VMEM)],
        out_specs=pl.BlockSpec(memory_space=pltpu.VMEM),
        out_shape=jax.ShapeDtypeStruct((NZ * SPAN, QBLK), jnp.bfloat16),
        compiler_params=pltpu.CompilerParams(vmem_limit_bytes=4 * 2**20),
    )(got)


def last_sum_kernel(got_ref, out_ref, spans):
    spans[...] = got_ref[...].astype(jnp.float32)
    span = spans[:SPAN, :]
    for i in range(1, NZ):
        span += spans[i * SPAN : (i + 1) * SPAN, :]
    span = span * (1.0 / DEVICES)
    for i in range(SPAN):
        out_ref[:, i * QBLK : (i + 1) * QBLK] = span[i : i + 1, :]


def last_sum(got):
    return pl.pallas_call(
        last_sum_kernel,
        in_specs=[pl.BlockSpec(memory_space=pltpu.VMEM)],
        out_specs=pl.BlockSpec(memory_space=pltpu.VMEM),
        out_shape=jax.ShapeDtypeStruct((1, SPAN * QBLK), jnp.float32),
        scratch_shapes=[pltpu.VMEM((NZ * SPAN, QBLK), jnp.float32)],
        compiler_params=pltpu.CompilerParams(vmem_limit_bytes=2 * 2**20),
    )(got)


def per_device(gate_up, out_grad, weight_codes, weight_scales, shard_order):
    gate_up_t = gate_up.T
    core = lax.axis_index("core").astype(jnp.int32).reshape(1)
    place = lax.axis_index(("xl", "core")).astype(jnp.int32).reshape(1)
    keep, send, weight = partial_spans(shard_order, core, gate_up_t, out_grad, weight_codes, weight_scales)
    got = lax.ppermute(send, "core", SWAP)
    weight_x = lax.ppermute(weight, "xl", SWAP)
    pair = (keep.astype(jnp.float32) + got.astype(jnp.float32)).astype(jnp.bfloat16)
    got = lax.all_to_all(pair, PLANE, split_axis=0, concat_axis=0, tiled=True)
    weight_x, weight = lax.optimization_barrier((weight_x, weight))
    weight_core = lax.ppermute(weight, "core", SWAP)
    weight_both = lax.ppermute(weight_x, "core", SWAP)
    grads = input_grads(place, gate_up_t, (weight, weight_core, weight_x, weight_both), out_grad)
    got, grads = lax.optimization_barrier((got, grads))
    line = plane_sum(got).reshape(NZ * SPAN // 2, 2, QBLK)
    got = lax.all_to_all(line, "z", split_axis=0, concat_axis=0, tiled=True)
    weight_grad = last_sum(got.reshape(NZ * SPAN, QBLK))
    return (grads.T, weight_grad)


def solution(mesh):
    fine = Mesh(mesh.devices.reshape(NY, NZ, 2, 2, 2), ALL)
    return jax.shard_map(
        per_device,
        mesh=fine,
        in_specs=(P(ALL, None), P(ALL, None), P(("xl", "core"), None), P(("xl", "core"), None), P()),
        out_specs=(P(ALL, None), P(ALL, None)),
        check_vma=False,
    )
```

time: 90 us -> 90 us (level)
  the two profiles are of different devices: /device:TPU:2 before, /device:TPU:6 now
where the time goes in v3:
time: 90 us; the launch traced here: 89.2 us
  waiting for transfers between devices  25.7 us (29%)
  blocking collectives  22.5 us (25%)
  starting transfers between devices  22.1 us (25%)
  Pallas kernels  14.9 us (17%)
  other arithmetic  2.46 us (3%)
    all_to_all x1, blocking collectives, per_device(): got = lax.all_to_all(line, 'z', split_axis=0, concat_axis=0, tiled=True)  22.5 us
    ppermute x1, waiting for transfers between devices, per_device(): weight_x = lax.ppermute(weight, 'xl', SWAP)  21.4 us
    all_to_all x1, starting transfers between devices, per_device(): got = lax.all_to_all(pair, PLANE, split_axis=0, concat_axis=0, tiled=True)  13.1 us
    pallas_call x1, Pallas kernels, partial_spans(): pl.pallas_call(partial_kernel, in_specs=[pl.BlockSpec(memory_space=pltpu....  7.36 us
    pallas_call x1, Pallas kernels, input_grads(): pl.pallas_call(grads_kernel, in_specs=[smem, vmem] + [anywhere] * 4 + [pl...  6.76 us
    ppermute x1, starting transfers between devices, per_device(): weight_x = lax.ppermute(weight, 'xl', SWAP)  2.76 us
    ppermute x1, waiting for transfers between devices, per_device(): got = lax.ppermute(send, 'core', SWAP)  2.74 us
    convert_element_type x1, other arithmetic, per_device(): (keep.astype(jnp.float32) + got.astype(jnp.float32)).astype(jnp.bfloat16)  2.46 us
  transfers between devices with their start and end apart: 5, of which 3 were waited for; matrix products, arithmetic and copies ran while one was open for 0% of the time, Pallas kernels for 8%

profile of v3, /device:TPU:6, one launch (start us, length us, event | category | flops | bytes accessed | tf_op | source)
XLA Modules:
  0.0 89.2 jit_solution(3976358569743874752)
XLA Ops:
  0.6 7.4 %shard_map.68 = (bf16[3840,128]{1,0:T(8,128)(2,1)}, bf16[3840,128]{1,0:T(8,128)(2,1)}, bf16[32,8192]{1,0:T(8,128)(2,1)}) custom-call(s32[1]{0:T(128)} %bitcast.core_ref, s32[768]{0:T(1024)} %order_hbm.1, bf16[240,256]{1,0:T(8,128)(2,1)} %bitcast.11, bf16[256,8192]{1,0:T(8,128)(2,1)} %out_grad_hbm.3, bf16[30,8192]{1,0:T(8,128)(2,1)} %codes_hbm.1, ...), custom_call_target="tpu_custom_call" | custom-call | flops 503316480 | bytes 6160384 | tf_op jit(solution)/shard_map/pallas_call | solution.py:90
  8.0 1.9 %collective-permute-start = (bf16[3840,128]{1,0:T(8,128)(2,1)}, bf16[3840,128]{1,0:T(8,128)(2,1)S(1)}, u32[]{:S(2)}, u32[]{:S(2)}) collective-permute-start(bf16[3840,128]{1,0:T(8,128)(2,1)} %get-tuple-element.10), channel_id=1, source_target_pairs={{0,1},{1,0},{2,3},{3,2},{4,5},{5,4},{6,7},{7,6},{8,9},{9,8},{10,11... | collective-permute-start | bytes 2949128 | tf_op jit(solution)/shard_map/ppermute | solution.py:206
  9.9 2.7 %collective-permute-done = bf16[3840,128]{1,0:T(8,128)(2,1)S(1)} collective-permute-done((bf16[3840,128]{1,0:T(8,128)(2,1)}, bf16[3840,128]{1,0:T(8,128)(2,1)S(1)}, u32[]{:S(2)}, u32[]{:S(2)}) %collective-permute-start) | collective-permute-done | bytes 983072 | tf_op jit(solution)/shard_map/ppermute | solution.py:206
  12.7 0.0 copy-start
  12.7 2.5 %add_convert_fusion = bf16[3840,128]{1,0:T(8,128)(2,1)} fusion(bf16[3840,128]{1,0:T(8,128)(2,1)S(1)} %collective-permute-done, bf16[3840,128]{1,0:T(8,128)(2,1)} %get-tuple-element.9), kind=kLoop, calls=%fused_computation | loop fusion | flops 1966080 | bytes 2949120 | tf_op jit(solution)/shard_map/convert_element_type | solution.py:208
  15.1 13.1 %all-to-all-start = ((bf16[32,120,128]{2,1,0:T(8,128)(2,1)}), bf16[32,120,128]{2,1,0:T(8,128)(2,1)S(1)}, u32[]{:S(2)}, u32[]{:S(2)}) async-start(bf16[32,120,128]{2,1,0:T(8,128)(2,1)} %bitcast.2), calls=%async_computation | async-start | bytes 1966080 | tf_op jit(solution)/shard_map/all_to_all | solution.py:209
  28.2 0.0 copy-done
  28.2 2.8 %collective-permute-start.1 = (bf16[32,8192]{1,0:T(8,128)(2,1)S(1)}, bf16[32,8192]{1,0:T(8,128)(2,1)S(1)}, u32[]{:S(2)}, u32[]{:S(2)}) collective-permute-start(bf16[32,8192]{1,0:T(8,128)(2,1)S(1)} %copy-done), channel_id=1, source_target_pairs={{0,2},{2,0},{1,3},{3,1},{4,6},{6,4},{5,7},{7,5},{8,10},{10,8},{9,1... | collective-permute-start | bytes 1572872 | tf_op jit(solution)/shard_map/ppermute | solution.py:207
  31.0 21.4 %collective-permute-done.1.x_hbm = bf16[32,8192]{1,0:T(8,128)(2,1)S(1)} collective-permute-done((bf16[32,8192]{1,0:T(8,128)(2,1)S(1)}, bf16[32,8192]{1,0:T(8,128)(2,1)S(1)}, u32[]{:S(2)}, u32[]{:S(2)}) %collective-permute-start.1) | collective-permute-done | bytes 524320 | tf_op jit(solution)/shard_map/ppermute | solution.py:207
  52.4 0.0 copy-start.1
  52.4 1.9 %collective-permute-start.2 = (bf16[32,8192]{1,0:T(8,128)(2,1)S(1)}, bf16[32,8192]{1,0:T(8,128)(2,1)S(1)}, u32[]{:S(2)}, u32[]{:S(2)}) collective-permute-start(bf16[32,8192]{1,0:T(8,128)(2,1)S(1)} %copy-done), channel_id=1, source_target_pairs={{0,1},{1,0},{2,3},{3,2},{4,5},{5,4},{6,7},{7,6},{8,9},{9,8},{10,11... | collective-permute-start | bytes 1572872 | tf_op jit(solution)/shard_map/ppermute | solution.py:211
  54.4 2.4 %collective-permute-start.3 = (bf16[32,8192]{1,0:T(8,128)(2,1)S(1)}, bf16[32,8192]{1,0:T(8,128)(2,1)S(1)}, u32[]{:S(2)}, u32[]{:S(2)}) collective-permute-start(bf16[32,8192]{1,0:T(8,128)(2,1)S(1)} %collective-permute-done.1.x_hbm), channel_id=1, source_target_pairs={{0,1},{1,0},{2,3},{3,2},{4,5},{5,4},{6,7},{7,6},{8,9},{9,8},{10,11... | collective-permute-start | bytes 1572872 | tf_op jit(solution)/shard_map/ppermute | solution.py:212
  56.8 0.0 collective-permute-done.2.core_hbm
  56.8 0.0 copy-start.2
  56.8 1.5 %collective-permute-done.3.both_hbm = bf16[32,8192]{1,0:T(8,128)(2,1)S(1)} collective-permute-done((bf16[32,8192]{1,0:T(8,128)(2,1)S(1)}, bf16[32,8192]{1,0:T(8,128)(2,1)S(1)}, u32[]{:S(2)}, u32[]{:S(2)}) %collective-permute-start.3) | collective-permute-done | bytes 524320 | tf_op jit(solution)/shard_map/ppermute | solution.py:212
  58.3 0.0 copy-start.3
  58.3 0.0 copy-done.1
  58.3 0.0 copy-done.2
  58.3 0.8 copy-done.3
  59.1 6.8 %shard_map.69 = bf16[240,256]{1,0:T(8,128)(2,1)} custom-call(s32[1]{0:T(128)} %bitcast.4.place_ref, bf16[240,256]{1,0:T(8,128)(2,1)} %bitcast.12, bf16[32,8192]{1,0:T(8,128)(2,1)} %get-tuple-element.12.own_hbm, bf16[32,8192]{1,0:T(8,128)(2,1)} %copy-done.2, bf16[32,8192]{1,0:T(8,128)(2,1)} %copy-done.1, bf16[32,8192]{1,0:T(8,128)(2,1)} %copy-done.3, ...), custom_call_target="tpu_custom_call" | custom-call | flops 503316480 | bytes 6291456 | tf_op jit(solution)/shard_map/pallas_call | solution.py:146
  65.9 0.0 all-to-all-done
  65.9 0.1 shard_map.70
  66.0 22.5 %all_to_all.17 = bf16[60,2,128]{2,1,0:T(2,128)(2,1)S(1)} all-to-all(bf16[60,2,128]{2,1,0:T(2,128)(2,1)S(1)} %bitcast.9), channel_id=1, replica_groups=mesh['y'=8,'z'=12,'xh'=2,'xl'=2,'core'=2] {'z'}, dimensions={0} | all-to-all | bytes 61440 | tf_op jit(solution)/shard_map/all_to_all | solution.py:216
  88.5 0.6 shard_map.71
Async XLA Ops:
  8.0 4.7 %collective-permute-start = (bf16[3840,128]{1,0:T(8,128)(2,1)}, bf16[3840,128]{1,0:T(8,128)(2,1)S(1)}, u32[]{:S(2)}, u32[]{:S(2)}) collective-permute-start(bf16[3840,128]{1,0:T(8,128)(2,1)} %get-tuple-element.10), channel_id=1, source_target_pairs={{0,1},{1,0},{2,3},{3,2},{4,5},{5,4},{6,7},{7,6},{8,9},{9,8},{10,11... | collective-permute-start | bytes 2949128 | tf_op jit(solution)/shard_map/ppermute | solution.py:206
  12.7 15.6 %copy-start = (bf16[32,8192]{1,0:T(8,128)(2,1)S(1)}, bf16[32,8192]{1,0:T(8,128)(2,1)}, u32[]{:S(2)}) copy-start(bf16[32,8192]{1,0:T(8,128)(2,1)} %get-tuple-element.12.own_hbm) | copy-start | bytes 1572868
  15.1 50.7 %all-to-all-start = ((bf16[32,120,128]{2,1,0:T(8,128)(2,1)}), bf16[32,120,128]{2,1,0:T(8,128)(2,1)S(1)}, u32[]{:S(2)}, u32[]{:S(2)}) async-start(bf16[32,120,128]{2,1,0:T(8,128)(2,1)} %bitcast.2), calls=%async_computation | async-start | bytes 1966080 | tf_op jit(solution)/shard_map/all_to_all | solution.py:209
  28.2 24.2 %collective-permute-start.1 = (bf16[32,8192]{1,0:T(8,128)(2,1)S(1)}, bf16[32,8192]{1,0:T(8,128)(2,1)S(1)}, u32[]{:S(2)}, u32[]{:S(2)}) collective-permute-start(bf16[32,8192]{1,0:T(8,128)(2,1)S(1)} %copy-done), channel_id=1, source_target_pairs={{0,2},{2,0},{1,3},{3,1},{4,6},{6,4},{5,7},{7,5},{8,10},{10,8},{9,1... | collective-permute-start | bytes 1572872 | tf_op jit(solution)/shard_map/ppermute | solution.py:207
  52.4 5.9 %copy-start.1 = (bf16[32,8192]{1,0:T(8,128)(2,1)}, bf16[32,8192]{1,0:T(8,128)(2,1)S(1)}, u32[]{:S(2)}) copy-start(bf16[32,8192]{1,0:T(8,128)(2,1)S(1)} %collective-permute-done.1.x_hbm) | copy-start | bytes 1572868
  52.4 4.3 %collective-permute-start.2 = (bf16[32,8192]{1,0:T(8,128)(2,1)S(1)}, bf16[32,8192]{1,0:T(8,128)(2,1)S(1)}, u32[]{:S(2)}, u32[]{:S(2)}) collective-permute-start(bf16[32,8192]{1,0:T(8,128)(2,1)S(1)} %copy-done), channel_id=1, source_target_pairs={{0,1},{1,0},{2,3},{3,2},{4,5},{5,4},{6,7},{7,6},{8,9},{9,8},{10,11... | collective-permute-start | bytes 1572872 | tf_op jit(solution)/shard_map/ppermute | solution.py:211
  54.4 3.9 %collective-permute-start.3 = (bf16[32,8192]{1,0:T(8,128)(2,1)S(1)}, bf16[32,8192]{1,0:T(8,128)(2,1)S(1)}, u32[]{:S(2)}, u32[]{:S(2)}) collective-permute-start(bf16[32,8192]{1,0:T(8,128)(2,1)S(1)} %collective-permute-done.1.x_hbm), channel_id=1, source_target_pairs={{0,1},{1,0},{2,3},{3,2},{4,5},{5,4},{6,7},{7,6},{8,9},{9,8},{10,11... | collective-permute-start | bytes 1572872 | tf_op jit(solution)/shard_map/ppermute | solution.py:212
  56.8 1.5 %copy-start.2 = (bf16[32,8192]{1,0:T(8,128)(2,1)}, bf16[32,8192]{1,0:T(8,128)(2,1)S(1)}, u32[]{:S(2)}) copy-start(bf16[32,8192]{1,0:T(8,128)(2,1)S(1)} %collective-permute-done.2.core_hbm) | copy-start | bytes 1572868
  58.3 0.8 copy-start.3

commit v4 on v3

--- a/solution.py
+++ b/solution.py
@@ -23,6 +23,7 @@
 STEPS = BLOCKS // STEP_BLOCKS
 WIDTH = STEP_BLOCKS * QBLK
 SWAP = [(0, 1), (1, 0)]
+OPPOSITE = [(x * 2 + c, (x + (1 if (x + c) % 2 == 0 else -1)) % NX * 2 + c) for x in range(NX) for c in range(2)]
 ALL = ("y", "z", "xh", "xl", "core")
 PLANE = ("y", "xh", "xl")
 
@@ -32,21 +33,59 @@
     return pltpu.make_async_copy(source.at[:, columns], target.at[:, columns], sems.at[chunk])
 
 
+def dequant_kernel(codes_hbm, scales_hbm, out_hbm, codes, scales, out, scale_sem, read_sems, write_sems):
+    scale_read = pltpu.make_async_copy(scales_hbm, scales, scale_sem)
+    scale_read.start()
+    for chunk in range(STEPS):
+        read_columns(codes_hbm, codes, read_sems, chunk).start()
+    scale_read.wait()
+    fill = jnp.zeros((PAD_ROWS - NODE_ROWS, WIDTH), jnp.float32)
+    for chunk in range(STEPS):
+        columns = slice(chunk * WIDTH, (chunk + 1) * WIDTH)
+        block_of = lax.broadcasted_iota(jnp.int32, (BLOCKS, WIDTH), 1) // QBLK + chunk * STEP_BLOCKS
+        one_hot = (lax.broadcasted_iota(jnp.int32, (BLOCKS, WIDTH), 0) == block_of).astype(jnp.float32)
+        wide = jnp.dot(scales[...], one_hot.astype(jnp.bfloat16), preferred_element_type=jnp.float32)
+        read_columns(codes_hbm, codes, read_sems, chunk).wait()
+        weight = codes[:, columns].astype(jnp.float32) * wide
+        out[:, columns] = jnp.concatenate([weight, fill], axis=0).astype(jnp.bfloat16)
+        read_columns(out, out_hbm, write_sems, chunk).start()
+    for chunk in range(STEPS):
+        read_columns(out, out_hbm, write_sems, chunk).wait()
+
+
+def dequant(codes, scales):
+    hbm = pl.BlockSpec(memory_space=pltpu.HBM)
+    return pl.pallas_call(
+        dequant_kernel,
+        in_specs=[hbm, hbm],
+        out_specs=hbm,
+        scratch_shapes=[
+            pltpu.VMEM((NODE_ROWS, D), jnp.bfloat16),
+            pltpu.VMEM((NODE_ROWS, BLOCKS), jnp.bfloat16),
+            pltpu.VMEM((PAD_ROWS, D), jnp.bfloat16),
+            pltpu.SemaphoreType.DMA,
+            pltpu.SemaphoreType.DMA((STEPS,)),
+            pltpu.SemaphoreType.DMA((STEPS,)),
+        ],
+        out_shape=jax.ShapeDtypeStruct((PAD_ROWS, D), jnp.bfloat16),
+        compiler_params=pltpu.CompilerParams(vmem_limit_bytes=56 * 2**20),
+        cost_estimate=pl.CostEstimate(flops=PAD_ROWS * D, bytes_accessed=4 * PAD_ROWS * D, transcendentals=0),
+    )(codes, scales)
+
+
 def partial_kernel(
-    core_ref, order_hbm, gate_up_hbm, out_grad_hbm, codes_hbm, scales_hbm, keep_ref, send_ref, weight_ref,
-    order, gate_up, codes, scales, out_grad, blocks, staged, sems, small_sems,
+    core_ref, order_hbm, gate_up_hbm, out_grad_hbm, keep_ref, send_ref, order, gate_up, out_grad, blocks, staged, sems, small_sems
 ):
     small = [
         pltpu.make_async_copy(source, target, small_sems.at[i])
         for i, (source, target) in enumerate(
-            ((gate_up_hbm, gate_up), (scales_hbm, scales), (codes_hbm, codes), (order_hbm, order))
+            ((gate_up_hbm, gate_up), (order_hbm, order))
         )
     ]
     small[0].start()
     for chunk in range(STEPS):
         read_columns(out_grad_hbm, out_grad, sems, chunk).start()
-    for read in small[1:]:
-        read.start()
+    small[1].start()
     small[0].wait()
     both = gate_up[...].astype(jnp.float32)
     gate, up = both[:FW], both[FW:]
@@ -57,17 +96,7 @@
         product = jnp.dot(hidden, out_grad[:, columns], preferred_element_type=jnp.float32)
         for block in range(STEP_BLOCKS):
             blocks[pl.ds(chunk * STEP_BLOCKS + block, FW, stride=BLOCKS), :] = product[:, block * QBLK : (block + 1) * QBLK]
-    for read in small[1:]:
-        read.wait()
-    fill = jnp.zeros((PAD_ROWS - NODE_ROWS, WIDTH), jnp.float32)
-    for chunk in range(STEPS):
-        columns = slice(chunk * WIDTH, (chunk + 1) * WIDTH)
-        block_of = lax.broadcasted_iota(jnp.int32, (BLOCKS, WIDTH), 1) // QBLK + chunk * STEP_BLOCKS
-        one_hot = (lax.broadcasted_iota(jnp.int32, (BLOCKS, WIDTH), 0) == block_of).astype(jnp.float32)
-        wide = jnp.dot(scales[...], one_hot.astype(jnp.bfloat16), preferred_element_type=jnp.float32)
-        weight = codes[:, columns].astype(jnp.float32) * wide
-        weight_ref[:, columns] = jnp.concatenate([weight, fill], axis=0).astype(jnp.bfloat16)
-
+    small[1].wait()
     core = core_ref[0]
     first = (core * HALF, (1 - core) * HALF)
 
@@ -84,32 +113,29 @@
     send_ref[...] = staged[HALF:, :].astype(jnp.bfloat16)
 
 
-def partial_spans(order, core, gate_up_t, out_grad, codes, scales):
+def partial_spans(order, core, gate_up_t, out_grad):
     hbm = pl.BlockSpec(memory_space=pltpu.HBM)
     vmem = pl.BlockSpec(memory_space=pltpu.VMEM)
     return pl.pallas_call(
         partial_kernel,
-        in_specs=[pl.BlockSpec(memory_space=pltpu.SMEM)] + [hbm] * 5,
-        out_specs=[vmem, vmem, vmem],
+        in_specs=[pl.BlockSpec(memory_space=pltpu.SMEM)] + [hbm] * 3,
+        out_specs=[vmem, vmem],
         scratch_shapes=[
             pltpu.SMEM((DEVICES,), jnp.int32),
             pltpu.VMEM((2 * FW, TOK), jnp.bfloat16),
-            pltpu.VMEM((NODE_ROWS, D), jnp.bfloat16),
-            pltpu.VMEM((NODE_ROWS, BLOCKS), jnp.bfloat16),
             pltpu.VMEM((TOK, D), jnp.bfloat16),
             pltpu.VMEM((ROWS, QBLK), jnp.float32),
             pltpu.VMEM((ROWS, QBLK), jnp.float32),
             pltpu.SemaphoreType.DMA((STEPS,)),
-            pltpu.SemaphoreType.DMA((4,)),
+            pltpu.SemaphoreType.DMA((2,)),
         ],
         out_shape=[
             jax.ShapeDtypeStruct((HALF, QBLK), jnp.bfloat16),
             jax.ShapeDtypeStruct((HALF, QBLK), jnp.bfloat16),
-            jax.ShapeDtypeStruct((PAD_ROWS, D), jnp.bfloat16),
         ],
         compiler_params=pltpu.CompilerParams(vmem_limit_bytes=56 * 2**20),
-        cost_estimate=pl.CostEstimate(flops=2 * FW * TOK * D, bytes_accessed=2 * TOK * D + 4 * HALF * QBLK, transcendentals=FW * TOK),
-    )(core, order, gate_up_t, out_grad, codes, scales)
+        cost_estimate=pl.CostEstimate(flops=2 * FW * TOK * D, bytes_accessed=6 * (2 * TOK * D + 4 * HALF * QBLK) // 2, transcendentals=FW * TOK),
+    )(core, order, gate_up_t, out_grad)
 
 
 def grads_kernel(place_ref, gate_up_ref, own_hbm, core_hbm, x_hbm, both_hbm, out_grad_hbm, out_ref, weight, out_grad, weight_sems, sems):
@@ -202,12 +228,14 @@
     gate_up_t = gate_up.T
     core = lax.axis_index("core").astype(jnp.int32).reshape(1)
     place = lax.axis_index(("xl", "core")).astype(jnp.int32).reshape(1)
-    keep, send, weight = partial_spans(shard_order, core, gate_up_t, out_grad, weight_codes, weight_scales)
+    weight = dequant(weight_codes, weight_scales)
+    weight, gate_up_first = lax.optimization_barrier((weight, gate_up_t))
+    weight_x = lax.ppermute(weight, ("xh", "xl", "core"), OPPOSITE)
+    keep, send = partial_spans(shard_order, core, gate_up_first, out_grad)
+    weight_x, weight, send = lax.optimization_barrier((weight_x, weight, send))
     got = lax.ppermute(send, "core", SWAP)
-    weight_x = lax.ppermute(weight, "xl", SWAP)
     pair = (keep.astype(jnp.float32) + got.astype(jnp.float32)).astype(jnp.bfloat16)
     got = lax.all_to_all(pair, PLANE, split_axis=0, concat_axis=0, tiled=True)
-    weight_x, weight = lax.optimization_barrier((weight_x, weight))
     weight_core = lax.ppermute(weight, "core", SWAP)
     weight_both = lax.ppermute(weight_x, "core", SWAP)
     grads = input_grads(place, gate_up_t, (weight, weight_core, weight_x, weight_both), out_grad)

time: 90 us -> 85.3 us (0.948)
  waiting for transfers between devices: 25.7 us -> 19.4 us
  Pallas kernels: 14.9 us -> 17.1 us
    ppermute x1, waiting for transfers between devices: 21.4 us -> 1.37 us  [per_device(): weight_x = lax.ppermute(weight, ('xh', 'xl', 'core'), OPPOSITE)]
    all_to_all x1, waiting for transfers between devices: 0.01 us -> 13.8 us  [per_device(): got = lax.all_to_all(pair, PLANE, split_axis=0, concat_axis=0, tiled=True)]
    pallas_call x0 -> x1, Pallas kernels: none -> 2.35 us  [dequant(): pl.pallas_call(dequant_kernel, in_specs=[hbm, hbm], out_specs=hbm, scratc...]
  transfers between devices with their start and end apart: 5 -> 5, of which waited for: 3 -> 4; matrix products, arithmetic and copies ran while one was open for 0% -> 0% of each run, Pallas kernels for 8% -> 16%
where the time goes in v4:
time: 85.3 us; the launch traced here: 84.8 us
  blocking collectives  22.2 us (26%)
  starting transfers between devices  22.1 us (26%)
  waiting for transfers between devices  19.4 us (23%)
  Pallas kernels  17.1 us (20%)
  other arithmetic  2.46 us (3%)
    all_to_all x1, blocking collectives, per_device(): got = lax.all_to_all(line, 'z', split_axis=0, concat_axis=0, tiled=True)  22.2 us
    all_to_all x1, waiting for transfers between devices, per_device(): got = lax.all_to_all(pair, PLANE, split_axis=0, concat_axis=0, tiled=True)  13.8 us
    all_to_all x1, starting transfers between devices, per_device(): got = lax.all_to_all(pair, PLANE, split_axis=0, concat_axis=0, tiled=True)  13.1 us
    pallas_call x1, Pallas kernels, partial_spans(): pl.pallas_call(partial_kernel, in_specs=[pl.BlockSpec(memory_space=pltpu....  7.16 us
    pallas_call x1, Pallas kernels, input_grads(): pl.pallas_call(grads_kernel, in_specs=[smem, vmem] + [anywhere] * 4 + [pl...  6.8 us
    ppermute x1, waiting for transfers between devices, per_device(): got = lax.ppermute(send, 'core', SWAP)  2.74 us
    ppermute x1, starting transfers between devices, per_device(): weight_x = lax.ppermute(weight, ('xh', 'xl', 'core'), OPPOSITE)  2.73 us
    convert_element_type x1, other arithmetic, per_device(): (keep.astype(jnp.float32) + got.astype(jnp.float32)).astype(jnp.bfloat16)  2.46 us
  transfers between devices with their start and end apart: 5, of which 4 were waited for; matrix products, arithmetic and copies ran while one was open for 0% of the time, Pallas kernels for 16%

profile of v4, /device:TPU:6, one launch (start us, length us, event | category | flops | bytes accessed | tf_op | source)
XLA Modules:
  0.0 84.8 jit_solution(7694935093006492978)
XLA Ops:
  0.6 2.3 %shard_map.68.own_hbm = bf16[32,8192]{1,0:T(8,128)(2,1)} custom-call(bf16[30,8192]{1,0:T(8,128)(2,1)} %codes_hbm.1, bf16[30,64]{1,0:T(8,128)(2,1)} %scales_hbm.1), custom_call_target="tpu_custom_call" | custom-call | flops 262144 | bytes 1048576 | tf_op jit(solution)/shard_map/pallas_call | solution.py:58
  3.0 2.7 %collective-permute-start = (bf16[32,8192]{1,0:T(8,128)(2,1)}, bf16[32,8192]{1,0:T(8,128)(2,1)S(1)}, u32[]{:S(2)}, u32[]{:S(2)}) collective-permute-start(bf16[32,8192]{1,0:T(8,128)(2,1)} %shard_map.68.own_hbm), channel_id=1, source_target_pairs={{0,2},{1,7},{2,0},{3,5},{4,6},{5,3},{6,4},{7,1},{8,10},{9,15},{10,... | collective-permute-start | bytes 1572872 | tf_op jit(solution)/shard_map/ppermute | solution.py:233
  5.7 7.2 %shard_map.69 = (bf16[3840,128]{1,0:T(8,128)(2,1)}, bf16[3840,128]{1,0:T(8,128)(2,1)}) custom-call(s32[1]{0:T(128)} %bitcast.core_ref, s32[768]{0:T(1024)} %order_hbm.1, bf16[240,256]{1,0:T(8,128)(2,1)} %bitcast.11, bf16[256,8192]{1,0:T(8,128)(2,1)} %out_grad_hbm.3), custom_call_target="tpu_custom_call" | custom-call | flops 503316480 | bytes 18481152 | tf_op jit(solution)/shard_map/pallas_call | solution.py:119
  12.9 1.4 %collective-permute-done.x_hbm = bf16[32,8192]{1,0:T(8,128)(2,1)S(1)} collective-permute-done((bf16[32,8192]{1,0:T(8,128)(2,1)}, bf16[32,8192]{1,0:T(8,128)(2,1)S(1)}, u32[]{:S(2)}, u32[]{:S(2)}) %collective-permute-start) | collective-permute-done | bytes 524320 | tf_op jit(solution)/shard_map/ppermute | solution.py:233
  14.3 0.0 copy-start.1
  14.3 1.9 %collective-permute-start.1 = (bf16[3840,128]{1,0:T(8,128)(2,1)}, bf16[3840,128]{1,0:T(8,128)(2,1)S(1)}, u32[]{:S(2)}, u32[]{:S(2)}) collective-permute-start(bf16[3840,128]{1,0:T(8,128)(2,1)} %get-tuple-element.15), channel_id=1, source_target_pairs={{0,1},{1,0},{2,3},{3,2},{4,5},{5,4},{6,7},{7,6},{8,9},{9,8},{10,11... | collective-permute-start | bytes 2949128 | tf_op jit(solution)/shard_map/ppermute | solution.py:236
  16.2 2.7 %collective-permute-done.1 = bf16[3840,128]{1,0:T(8,128)(2,1)S(1)} collective-permute-done((bf16[3840,128]{1,0:T(8,128)(2,1)}, bf16[3840,128]{1,0:T(8,128)(2,1)S(1)}, u32[]{:S(2)}, u32[]{:S(2)}) %collective-permute-start.1) | collective-permute-done | bytes 983072 | tf_op jit(solution)/shard_map/ppermute | solution.py:236
  18.9 0.0 copy-start
  18.9 2.5 %add_convert_fusion = bf16[3840,128]{1,0:T(8,128)(2,1)} fusion(bf16[3840,128]{1,0:T(8,128)(2,1)S(1)} %collective-permute-done.1, bf16[3840,128]{1,0:T(8,128)(2,1)} %get-tuple-element.12), kind=kLoop, calls=%fused_computation | loop fusion | flops 1966080 | bytes 2949120 | tf_op jit(solution)/shard_map/convert_element_type | solution.py:237
  21.4 13.1 %all-to-all-start = ((bf16[32,120,128]{2,1,0:T(8,128)(2,1)}), bf16[32,120,128]{2,1,0:T(8,128)(2,1)S(1)}, u32[]{:S(2)}, u32[]{:S(2)}) async-start(bf16[32,120,128]{2,1,0:T(8,128)(2,1)} %bitcast.2), calls=%async_computation | async-start | bytes 1966080 | tf_op jit(solution)/shard_map/all_to_all | solution.py:238
  34.5 0.0 copy-done
  34.5 1.9 %collective-permute-start.2 = (bf16[32,8192]{1,0:T(8,128)(2,1)S(1)}, bf16[32,8192]{1,0:T(8,128)(2,1)S(1)}, u32[]{:S(2)}, u32[]{:S(2)}) collective-permute-start(bf16[32,8192]{1,0:T(8,128)(2,1)S(1)} %copy-done), channel_id=1, source_target_pairs={{0,1},{1,0},{2,3},{3,2},{4,5},{5,4},{6,7},{7,6},{8,9},{9,8},{10,11... | collective-permute-start | bytes 1572872 | tf_op jit(solution)/shard_map/ppermute | solution.py:239
  36.4 0.0 copy-done.1
  36.4 2.4 %collective-permute-start.3 = (bf16[32,8192]{1,0:T(8,128)(2,1)S(1)}, bf16[32,8192]{1,0:T(8,128)(2,1)S(1)}, u32[]{:S(2)}, u32[]{:S(2)}) collective-permute-start(bf16[32,8192]{1,0:T(8,128)(2,1)S(1)} %collective-permute-done.x_hbm), channel_id=1, source_target_pairs={{0,1},{1,0},{2,3},{3,2},{4,5},{5,4},{6,7},{7,6},{8,9},{9,8},{10,11... | collective-permute-start | bytes 1572872 | tf_op jit(solution)/shard_map/ppermute | solution.py:240
  38.9 0.0 collective-permute-done.2.core_hbm
  38.9 0.0 copy-start.2
  38.9 1.5 %collective-permute-done.3.both_hbm = bf16[32,8192]{1,0:T(8,128)(2,1)S(1)} collective-permute-done((bf16[32,8192]{1,0:T(8,128)(2,1)S(1)}, bf16[32,8192]{1,0:T(8,128)(2,1)S(1)}, u32[]{:S(2)}, u32[]{:S(2)}) %collective-permute-start.3) | collective-permute-done | bytes 524320 | tf_op jit(solution)/shard_map/ppermute | solution.py:240
  40.4 0.0 copy-start.3
  40.4 0.0 copy-done.2
  40.4 0.8 copy-done.3
  41.2 6.8 %shard_map.70 = bf16[240,256]{1,0:T(8,128)(2,1)} custom-call(s32[1]{0:T(128)} %bitcast.4.place_ref, bf16[240,256]{1,0:T(8,128)(2,1)} %bitcast.12, bf16[32,8192]{1,0:T(8,128)(2,1)} %shard_map.68.own_hbm, bf16[32,8192]{1,0:T(8,128)(2,1)} %copy-done.2, bf16[32,8192]{1,0:T(8,128)(2,1)} %copy-done.1, bf16[32,8192]{1,0:T(8,128)(2,1)} %copy-done.3, ...), custom_call_target="tpu_custom_call" | custom-call | flops 503316480 | bytes 6291456 | tf_op jit(solution)/shard_map/pallas_call | solution.py:172
  48.0 13.8 %all-to-all-done = bf16[32,120,128]{2,1,0:T(8,128)(2,1)S(1)} async-done(((bf16[32,120,128]{2,1,0:T(8,128)(2,1)}), bf16[32,120,128]{2,1,0:T(8,128)(2,1)S(1)}, u32[]{:S(2)}, u32[]{:S(2)}) %all-to-all-start) | async-done | bytes 983072 | tf_op jit(solution)/shard_map/all_to_all | solution.py:238
  61.8 0.1 shard_map.71
  61.9 22.2 %all_to_all.17 = bf16[60,2,128]{2,1,0:T(2,128)(2,1)S(1)} all-to-all(bf16[60,2,128]{2,1,0:T(2,128)(2,1)S(1)} %bitcast.9), channel_id=1, replica_groups=mesh['y'=8,'z'=12,'xh'=2,'xl'=2,'core'=2] {'z'}, dimensions={0} | all-to-all | bytes 61440 | tf_op jit(solution)/shard_map/all_to_all | solution.py:244
  84.2 0.6 shard_map.72
Async XLA Ops:
  3.0 11.3 %collective-permute-start = (bf16[32,8192]{1,0:T(8,128)(2,1)}, bf16[32,8192]{1,0:T(8,128)(2,1)S(1)}, u32[]{:S(2)}, u32[]{:S(2)}) collective-permute-start(bf16[32,8192]{1,0:T(8,128)(2,1)} %shard_map.68.own_hbm), channel_id=1, source_target_pairs={{0,2},{1,7},{2,0},{3,5},{4,6},{5,3},{6,4},{7,1},{8,10},{9,15},{10,... | collective-permute-start | bytes 1572872 | tf_op jit(solution)/shard_map/ppermute | solution.py:233
  14.3 22.2 %copy-start.1 = (bf16[32,8192]{1,0:T(8,128)(2,1)}, bf16[32,8192]{1,0:T(8,128)(2,1)S(1)}, u32[]{:S(2)}) copy-start(bf16[32,8192]{1,0:T(8,128)(2,1)S(1)} %collective-permute-done.x_hbm) | copy-start | bytes 1572868
  14.3 4.7 %collective-permute-start.1 = (bf16[3840,128]{1,0:T(8,128)(2,1)}, bf16[3840,128]{1,0:T(8,128)(2,1)S(1)}, u32[]{:S(2)}, u32[]{:S(2)}) collective-permute-start(bf16[3840,128]{1,0:T(8,128)(2,1)} %get-tuple-element.15), channel_id=1, source_target_pairs={{0,1},{1,0},{2,3},{3,2},{4,5},{5,4},{6,7},{7,6},{8,9},{9,8},{10,11... | collective-permute-start | bytes 2949128 | tf_op jit(solution)/shard_map/ppermute | solution.py:236
  18.9 15.6 %copy-start = (bf16[32,8192]{1,0:T(8,128)(2,1)S(1)}, bf16[32,8192]{1,0:T(8,128)(2,1)}, u32[]{:S(2)}) copy-start(bf16[32,8192]{1,0:T(8,128)(2,1)} %shard_map.68.own_hbm) | copy-start | bytes 1572868
  21.4 40.4 %all-to-all-start = ((bf16[32,120,128]{2,1,0:T(8,128)(2,1)}), bf16[32,120,128]{2,1,0:T(8,128)(2,1)S(1)}, u32[]{:S(2)}, u32[]{:S(2)}) async-start(bf16[32,120,128]{2,1,0:T(8,128)(2,1)} %bitcast.2), calls=%async_computation | async-start | bytes 1966080 | tf_op jit(solution)/shard_map/all_to_all | solution.py:238
  34.5 4.4 %collective-permute-start.2 = (bf16[32,8192]{1,0:T(8,128)(2,1)S(1)}, bf16[32,8192]{1,0:T(8,128)(2,1)S(1)}, u32[]{:S(2)}, u32[]{:S(2)}) collective-permute-start(bf16[32,8192]{1,0:T(8,128)(2,1)S(1)} %copy-done), channel_id=1, source_target_pairs={{0,1},{1,0},{2,3},{3,2},{4,5},{5,4},{6,7},{7,6},{8,9},{9,8},{10,11... | collective-permute-start | bytes 1572872 | tf_op jit(solution)/shard_map/ppermute | solution.py:239
  36.4 3.9 %collective-permute-start.3 = (bf16[32,8192]{1,0:T(8,128)(2,1)S(1)}, bf16[32,8192]{1,0:T(8,128)(2,1)S(1)}, u32[]{:S(2)}, u32[]{:S(2)}) collective-permute-start(bf16[32,8192]{1,0:T(8,128)(2,1)S(1)} %collective-permute-done.x_hbm), channel_id=1, source_target_pairs={{0,1},{1,0},{2,3},{3,2},{4,5},{5,4},{6,7},{7,6},{8,9},{9,8},{10,11... | collective-permute-start | bytes 1572872 | tf_op jit(solution)/shard_map/ppermute | solution.py:240
  38.9 1.5 %copy-start.2 = (bf16[32,8192]{1,0:T(8,128)(2,1)}, bf16[32,8192]{1,0:T(8,128)(2,1)S(1)}, u32[]{:S(2)}) copy-start(bf16[32,8192]{1,0:T(8,128)(2,1)S(1)} %collective-permute-done.2.core_hbm) | copy-start | bytes 1572868
  40.4 0.8 copy-start.3

commit v5 on v3

--- a/solution.py
+++ b/solution.py
@@ -23,6 +23,7 @@
 STEPS = BLOCKS // STEP_BLOCKS
 WIDTH = STEP_BLOCKS * QBLK
 SWAP = [(0, 1), (1, 0)]
+OPPOSITE = [(x * 2 + c, (x + (1 if (x + c) % 2 == 0 else -1)) % NX * 2 + c) for x in range(NX) for c in range(2)]
 ALL = ("y", "z", "xh", "xl", "core")
 PLANE = ("y", "xh", "xl")
 
@@ -204,16 +205,17 @@
     place = lax.axis_index(("xl", "core")).astype(jnp.int32).reshape(1)
     keep, send, weight = partial_spans(shard_order, core, gate_up_t, out_grad, weight_codes, weight_scales)
     got = lax.ppermute(send, "core", SWAP)
-    weight_x = lax.ppermute(weight, "xl", SWAP)
+    weight_x = lax.ppermute(weight, ("xh", "xl", "core"), OPPOSITE)
     pair = (keep.astype(jnp.float32) + got.astype(jnp.float32)).astype(jnp.bfloat16)
+    weight_x, weight, pair = lax.optimization_barrier((weight_x, weight, pair))
     got = lax.all_to_all(pair, PLANE, split_axis=0, concat_axis=0, tiled=True)
-    weight_x, weight = lax.optimization_barrier((weight_x, weight))
+    line = plane_sum(got)
+    weight_x, weight, line = lax.optimization_barrier((weight_x, weight, line))
     weight_core = lax.ppermute(weight, "core", SWAP)
     weight_both = lax.ppermute(weight_x, "core", SWAP)
+    got = lax.all_to_all(line.reshape(NZ * SPAN // 2, 2, QBLK), "z", split_axis=0, concat_axis=0, tiled=True)
     grads = input_grads(place, gate_up_t, (weight, weight_core, weight_x, weight_both), out_grad)
     got, grads = lax.optimization_barrier((got, grads))
-    line = plane_sum(got).reshape(NZ * SPAN // 2, 2, QBLK)
-    got = lax.all_to_all(line, "z", split_axis=0, concat_axis=0, tiled=True)
     weight_grad = last_sum(got.reshape(NZ * SPAN, QBLK))
     return (grads.T, weight_grad)
 

time: 90 us -> 90.2 us (level)
  blocking collectives: 22.5 us -> 39.3 us
  waiting for transfers between devices: 25.7 us -> 9.81 us
  other arithmetic: 2.46 us -> 1.46 us
    all_to_all x1, blocking collectives: 22.5 us -> 39.3 us  [per_device(): got = lax.all_to_all(pair, PLANE, split_axis=0, concat_axis=0, tiled=True)]
    ppermute x1, waiting for transfers between devices: 21.4 us -> 7.05 us  [per_device(): weight_x = lax.ppermute(weight, ('xh', 'xl', 'core'), OPPOSITE)]
    all_to_all x1, waiting for transfers between devices: 0.01 us -> 2.75 us  [per_device(): lax.all_to_all(line.reshape(NZ * SPAN // 2, 2, QBLK), 'z', split_axis=0,...]
    ppermute x1, waiting for transfers between devices: 2.74 us -> 0.01 us  [per_device(): got = lax.ppermute(send, 'core', SWAP)]
    ppermute x1, waiting for transfers between devices: 1.49 us -> 0.01 us  [per_device(): weight_both = lax.ppermute(weight_x, 'core', SWAP)]
    convert_element_type x1, other arithmetic: 2.46 us -> 1.46 us  [per_device(): (keep.astype(jnp.float32) + got.astype(jnp.float32)).astype(jnp.bfloat16)]
  transfers between devices with their start and end apart: 5 -> 5, of which waited for: 3 -> 2; matrix products, arithmetic and copies ran while one was open for 0% -> 2% of each run, Pallas kernels for 8% -> 8%
where the time goes in v5:
time: 90.2 us; the launch traced here: 89.7 us
  blocking collectives  39.3 us (44%)
  starting transfers between devices  21.9 us (24%)
  Pallas kernels  15.5 us (17%)
  waiting for transfers between devices  9.81 us (11%)
  other arithmetic  1.46 us (2%)
  local copies, waits for them, and re-layouts  0.97 us (1%)
    all_to_all x1, blocking collectives, per_device(): got = lax.all_to_all(pair, PLANE, split_axis=0, concat_axis=0, tiled=True)  39.3 us
    all_to_all x1, starting transfers between devices, per_device(): lax.all_to_all(line.reshape(NZ * SPAN // 2, 2, QBLK), 'z', split_axis=0,...  12.9 us
    pallas_call x1, Pallas kernels, partial_spans(): pl.pallas_call(partial_kernel, in_specs=[pl.BlockSpec(memory_space=pltpu....  7.35 us
    ppermute x1, waiting for transfers between devices, per_device(): weight_x = lax.ppermute(weight, ('xh', 'xl', 'core'), OPPOSITE)  7.05 us
    pallas_call x1, Pallas kernels, input_grads(): pl.pallas_call(grads_kernel, in_specs=[smem, vmem] + [anywhere] * 4 + [pl...  6.77 us
    all_to_all x1, waiting for transfers between devices, per_device(): lax.all_to_all(line.reshape(NZ * SPAN // 2, 2, QBLK), 'z', split_axis=0,...  2.75 us
    ppermute x1, starting transfers between devices, per_device(): weight_x = lax.ppermute(weight, ('xh', 'xl', 'core'), OPPOSITE)  2.74 us
    ppermute x1, starting transfers between devices, per_device(): weight_both = lax.ppermute(weight_x, 'core', SWAP)  2.34 us
  transfers between devices with their start and end apart: 5, of which 2 were waited for; matrix products, arithmetic and copies ran while one was open for 2% of the time, Pallas kernels for 8%

profile of v5, /device:TPU:6, one launch (start us, length us, event | category | flops | bytes accessed | tf_op | source)
XLA Modules:
  0.0 89.7 jit_solution(6317642927325127393)
XLA Ops:
  0.6 7.4 %shard_map.68 = (bf16[3840,128]{1,0:T(8,128)(2,1)}, bf16[3840,128]{1,0:T(8,128)(2,1)}, bf16[32,8192]{1,0:T(8,128)(2,1)}) custom-call(s32[1]{0:T(128)} %bitcast.core_ref, s32[768]{0:T(1024)} %order_hbm.1, bf16[240,256]{1,0:T(8,128)(2,1)} %bitcast.11, bf16[256,8192]{1,0:T(8,128)(2,1)} %out_grad_hbm.3, bf16[30,8192]{1,0:T(8,128)(2,1)} %codes_hbm.1, ...), custom_call_target="tpu_custom_call" | custom-call | flops 503316480 | bytes 6160384 | tf_op jit(solution)/shard_map/pallas_call | solution.py:91
  8.0 1.9 %collective-permute-start.1 = (bf16[3840,128]{1,0:T(8,128)(2,1)}, bf16[3840,128]{1,0:T(8,128)(2,1)S(1)}, u32[]{:S(2)}, u32[]{:S(2)}) collective-permute-start(bf16[3840,128]{1,0:T(8,128)(2,1)} %get-tuple-element.15), channel_id=1, source_target_pairs={{0,1},{1,0},{2,3},{3,2},{4,5},{5,4},{6,7},{7,6},{8,9},{9,8},{10,11... | collective-permute-start | bytes 2949128 | tf_op jit(solution)/shard_map/ppermute | solution.py:207
  9.9 2.7 %collective-permute-start = (bf16[32,8192]{1,0:T(8,128)(2,1)}, bf16[32,8192]{1,0:T(8,128)(2,1)S(1)}, u32[]{:S(2)}, u32[]{:S(2)}) collective-permute-start(bf16[32,8192]{1,0:T(8,128)(2,1)} %get-tuple-element.20.own_hbm), channel_id=1, source_target_pairs={{0,2},{1,7},{2,0},{3,5},{4,6},{5,3},{6,4},{7,1},{8,10},{9,15},{10,... | collective-permute-start | bytes 1572872 | tf_op jit(solution)/shard_map/ppermute | solution.py:208
  12.7 0.0 collective-permute-done.1
  12.7 1.5 %add_convert_fusion = bf16[3840,128]{1,0:T(8,128)(2,1)S(1)} fusion(bf16[3840,128]{1,0:T(8,128)(2,1)S(1)} %collective-permute-done.1, bf16[3840,128]{1,0:T(8,128)(2,1)} %get-tuple-element.14), kind=kLoop, calls=%fused_computation | loop fusion | flops 1966080 | bytes 2949120 | tf_op jit(solution)/shard_map/convert_element_type | solution.py:209
  14.1 0.0 copy-start
  14.2 7.1 %collective-permute-done.x_hbm = bf16[32,8192]{1,0:T(8,128)(2,1)S(1)} collective-permute-done((bf16[32,8192]{1,0:T(8,128)(2,1)}, bf16[32,8192]{1,0:T(8,128)(2,1)S(1)}, u32[]{:S(2)}, u32[]{:S(2)}) %collective-permute-start) | collective-permute-done | bytes 524320 | tf_op jit(solution)/shard_map/ppermute | solution.py:208
  21.2 0.0 copy-start.1
  21.2 39.3 %all_to_all.16 = bf16[32,120,128]{2,1,0:T(8,128)(2,1)S(1)} all-to-all(bf16[32,120,128]{2,1,0:T(8,128)(2,1)S(1)} %bitcast.10), channel_id=1, replica_groups=mesh['y'=8,'z'=12,'xh'=2,'xl'=2,'core'=2] {'y','xh','xl'}, dimensions={0} | all-to-all | bytes 1966080 | tf_op jit(solution)/shard_map/all_to_all | solution.py:211
  60.5 0.8 shard_map.69
  61.3 0.0 copy-done
  61.3 2.0 %collective-permute-start.2 = (bf16[32,8192]{1,0:T(8,128)(2,1)S(1)}, bf16[32,8192]{1,0:T(8,128)(2,1)S(1)}, u32[]{:S(2)}, u32[]{:S(2)}) collective-permute-start(bf16[32,8192]{1,0:T(8,128)(2,1)S(1)} %copy-done), channel_id=1, source_target_pairs={{0,1},{1,0},{2,3},{3,2},{4,5},{5,4},{6,7},{7,6},{8,9},{9,8},{10,11... | collective-permute-start | bytes 1572872 | tf_op jit(solution)/shard_map/ppermute | solution.py:214
  63.3 2.3 %collective-permute-start.3 = (bf16[32,8192]{1,0:T(8,128)(2,1)S(1)}, bf16[32,8192]{1,0:T(8,128)(2,1)S(1)}, u32[]{:S(2)}, u32[]{:S(2)}) collective-permute-start(bf16[32,8192]{1,0:T(8,128)(2,1)S(1)} %collective-permute-done.x_hbm), channel_id=1, source_target_pairs={{0,1},{1,0},{2,3},{3,2},{4,5},{5,4},{6,7},{7,6},{8,9},{9,8},{10,11... | collective-permute-start | bytes 1572872 | tf_op jit(solution)/shard_map/ppermute | solution.py:215
  65.6 12.9 %all-to-all-start.1 = ((bf16[60,2,128]{2,1,0:T(2,128)(2,1)}), bf16[60,2,128]{2,1,0:T(2,128)(2,1)S(1)}, u32[]{:S(2)}, u32[]{:S(2)}) async-start(bf16[60,2,128]{2,1,0:T(2,128)(2,1)} %bitcast.4), calls=%async_computation.1 | async-start | bytes 61440 | tf_op jit(solution)/shard_map/all_to_all | solution.py:216
  78.6 0.0 collective-permute-done.2.core_hbm
  78.6 0.0 copy-start.2
  78.6 0.0 collective-permute-done.3.both_hbm
  78.6 0.0 copy-start.3
  78.6 0.0 copy-done.1
  78.6 0.7 copy-done.2
  79.4 0.2 copy-done.3
  79.6 6.8 %shard_map.70 = bf16[240,256]{1,0:T(8,128)(2,1)} custom-call(s32[1]{0:T(128)} %bitcast.5.place_ref, bf16[240,256]{1,0:T(8,128)(2,1)} %bitcast.12, bf16[32,8192]{1,0:T(8,128)(2,1)} %get-tuple-element.20.own_hbm, bf16[32,8192]{1,0:T(8,128)(2,1)} %copy-done.2, bf16[32,8192]{1,0:T(8,128)(2,1)} %copy-done.1, bf16[32,8192]{1,0:T(8,128)(2,1)} %copy-done.3, ...), custom_call_target="tpu_custom_call" | custom-call | flops 503316480 | bytes 6291456 | tf_op jit(solution)/shard_map/pallas_call | solution.py:147
  86.4 2.8 %all-to-all-done.1 = bf16[60,2,128]{2,1,0:T(2,128)(2,1)S(1)} async-done(((bf16[60,2,128]{2,1,0:T(2,128)(2,1)}), bf16[60,2,128]{2,1,0:T(2,128)(2,1)S(1)}, u32[]{:S(2)}, u32[]{:S(2)}) %all-to-all-start.1) | async-done | bytes 30752 | tf_op jit(solution)/shard_map/all_to_all | solution.py:216
  89.1 0.6 shard_map.71
Async XLA Ops:
  8.0 4.7 %collective-permute-start.1 = (bf16[3840,128]{1,0:T(8,128)(2,1)}, bf16[3840,128]{1,0:T(8,128)(2,1)S(1)}, u32[]{:S(2)}, u32[]{:S(2)}) collective-permute-start(bf16[3840,128]{1,0:T(8,128)(2,1)} %get-tuple-element.15), channel_id=1, source_target_pairs={{0,1},{1,0},{2,3},{3,2},{4,5},{5,4},{6,7},{7,6},{8,9},{9,8},{10,11... | collective-permute-start | bytes 2949128 | tf_op jit(solution)/shard_map/ppermute | solution.py:207
  9.9 11.3 %collective-permute-start = (bf16[32,8192]{1,0:T(8,128)(2,1)}, bf16[32,8192]{1,0:T(8,128)(2,1)S(1)}, u32[]{:S(2)}, u32[]{:S(2)}) collective-permute-start(bf16[32,8192]{1,0:T(8,128)(2,1)} %get-tuple-element.20.own_hbm), channel_id=1, source_target_pairs={{0,2},{1,7},{2,0},{3,5},{4,6},{5,3},{6,4},{7,1},{8,10},{9,15},{10,... | collective-permute-start | bytes 1572872 | tf_op jit(solution)/shard_map/ppermute | solution.py:208
  14.1 47.2 %copy-start = (bf16[32,8192]{1,0:T(8,128)(2,1)S(1)}, bf16[32,8192]{1,0:T(8,128)(2,1)}, u32[]{:S(2)}) copy-start(bf16[32,8192]{1,0:T(8,128)(2,1)} %get-tuple-element.20.own_hbm) | copy-start | bytes 1572868
  21.2 57.4 %copy-start.1 = (bf16[32,8192]{1,0:T(8,128)(2,1)}, bf16[32,8192]{1,0:T(8,128)(2,1)S(1)}, u32[]{:S(2)}) copy-start(bf16[32,8192]{1,0:T(8,128)(2,1)S(1)} %collective-permute-done.x_hbm) | copy-start | bytes 1572868
  61.3 17.3 %collective-permute-start.2 = (bf16[32,8192]{1,0:T(8,128)(2,1)S(1)}, bf16[32,8192]{1,0:T(8,128)(2,1)S(1)}, u32[]{:S(2)}, u32[]{:S(2)}) collective-permute-start(bf16[32,8192]{1,0:T(8,128)(2,1)S(1)} %copy-done), channel_id=1, source_target_pairs={{0,1},{1,0},{2,3},{3,2},{4,5},{5,4},{6,7},{7,6},{8,9},{9,8},{10,11... | collective-permute-start | bytes 1572872 | tf_op jit(solution)/shard_map/ppermute | solution.py:214
  63.3 15.3 %collective-permute-start.3 = (bf16[32,8192]{1,0:T(8,128)(2,1)S(1)}, bf16[32,8192]{1,0:T(8,128)(2,1)S(1)}, u32[]{:S(2)}, u32[]{:S(2)}) collective-permute-start(bf16[32,8192]{1,0:T(8,128)(2,1)S(1)} %collective-permute-done.x_hbm), channel_id=1, source_target_pairs={{0,1},{1,0},{2,3},{3,2},{4,5},{5,4},{6,7},{7,6},{8,9},{9,8},{10,11... | collective-permute-start | bytes 1572872 | tf_op jit(solution)/shard_map/ppermute | solution.py:215
  65.6 23.5 %all-to-all-start.1 = ((bf16[60,2,128]{2,1,0:T(2,128)(2,1)}), bf16[60,2,128]{2,1,0:T(2,128)(2,1)S(1)}, u32[]{:S(2)}, u32[]{:S(2)}) async-start(bf16[60,2,128]{2,1,0:T(2,128)(2,1)} %bitcast.4), calls=%async_computation.1 | async-start | bytes 61440 | tf_op jit(solution)/shard_map/all_to_all | solution.py:216
  78.6 0.8 copy-start.2
  78.6 1.0 %copy-start.3 = (bf16[32,8192]{1,0:T(8,128)(2,1)}, bf16[32,8192]{1,0:T(8,128)(2,1)S(1)}, u32[]{:S(2)}) copy-start(bf16[32,8192]{1,0:T(8,128)(2,1)S(1)} %collective-permute-done.3.both_hbm) | copy-start | bytes 1572868

commit v6 on v3

--- a/solution.py
+++ b/solution.py
@@ -23,8 +23,11 @@
 STEPS = BLOCKS // STEP_BLOCKS
 WIDTH = STEP_BLOCKS * QBLK
 SWAP = [(0, 1), (1, 0)]
+FIRST = [(x * 2 + c, (x + (1 if (x + c) % 2 == 0 else -1)) % NX * 2 + c) for x in range(NX) for c in range(2)]
+SECOND = [(x * 2 + c, (x + (-1 if (x + c) % 2 == 0 else 1)) % NX * 2 + c) for x in range(NX) for c in range(2)]
+XROWS = HALF // NX
 ALL = ("y", "z", "xh", "xl", "core")
-PLANE = ("y", "xh", "xl")
+XC = ("xh", "xl", "core")
 
 
 def read_columns(source, target, sems, chunk):
@@ -33,7 +36,7 @@
 
 
 def partial_kernel(
-    core_ref, order_hbm, gate_up_hbm, out_grad_hbm, codes_hbm, scales_hbm, keep_ref, send_ref, weight_ref,
+    core_ref, x_ref, order_hbm, gate_up_hbm, out_grad_hbm, codes_hbm, scales_hbm, keep_ref, send_ref, weight_ref,
     order, gate_up, codes, scales, out_grad, blocks, staged, sems, small_sems,
 ):
     small = [
@@ -68,28 +71,33 @@
         weight = codes[:, columns].astype(jnp.float32) * wide
         weight_ref[:, columns] = jnp.concatenate([weight, fill], axis=0).astype(jnp.bfloat16)
 
-    core = core_ref[0]
-    first = (core * HALF, (1 - core) * HALF)
-
-    def gather(y, carry):
-        for z in range(NZ):
-            for low in range(8):
-                span = order[y * (8 * NZ) + z * 8 + low]
-                place = first[low % 2] + y * (NX * NZ * SPAN) + ((low // 2) * NZ + z) * SPAN
-                staged[pl.ds(place, SPAN), :] = blocks[pl.ds(span * SPAN, SPAN), :]
+    core, x = core_ref[0], x_ref[0]
+    bases = []
+    for low in range(8):
+        owner_x, owner_core = low // 2, low % 2
+        away = (owner_x - x) & (NX - 1)
+        ahead_first = ((x + owner_core) & 1) == 0
+        beside = jnp.where((away == 1) == ahead_first, 2, 1)
+        slot = jnp.where(away == 0, 0, jnp.where(away == 2, 3, beside))
+        bases.append(jnp.where(core == owner_core, 0, HALF) + slot * XROWS)
+
+    def gather(yz, carry):
+        for low in range(8):
+            span = order[yz * 8 + low]
+            staged[pl.ds(bases[low] + yz * SPAN, SPAN), :] = blocks[pl.ds(span * SPAN, SPAN), :]
         return carry
 
-    lax.fori_loop(0, NY, gather, 0)
+    lax.fori_loop(0, NY * NZ, gather, 0, unroll=4)
     keep_ref[...] = staged[:HALF, :].astype(jnp.bfloat16)
     send_ref[...] = staged[HALF:, :].astype(jnp.bfloat16)
 
 
-def partial_spans(order, core, gate_up_t, out_grad, codes, scales):
+def partial_spans(order, core, x, gate_up_t, out_grad, codes, scales):
     hbm = pl.BlockSpec(memory_space=pltpu.HBM)
     vmem = pl.BlockSpec(memory_space=pltpu.VMEM)
     return pl.pallas_call(
         partial_kernel,
-        in_specs=[pl.BlockSpec(memory_space=pltpu.SMEM)] + [hbm] * 5,
+        in_specs=[pl.BlockSpec(memory_space=pltpu.SMEM)] * 2 + [hbm] * 5,
         out_specs=[vmem, vmem, vmem],
         scratch_shapes=[
             pltpu.SMEM((DEVICES,), jnp.int32),
@@ -109,7 +117,7 @@
         ],
         compiler_params=pltpu.CompilerParams(vmem_limit_bytes=56 * 2**20),
         cost_estimate=pl.CostEstimate(flops=2 * FW * TOK * D, bytes_accessed=2 * TOK * D + 4 * HALF * QBLK, transcendentals=FW * TOK),
-    )(core, order, gate_up_t, out_grad, codes, scales)
+    )(core, x, order, gate_up_t, out_grad, codes, scales)
 
 
 def grads_kernel(place_ref, gate_up_ref, own_hbm, core_hbm, x_hbm, both_hbm, out_grad_hbm, out_ref, weight, out_grad, weight_sems, sems):
@@ -159,17 +167,17 @@
     )(place, gate_up_t, *parts, out_grad)
 
 
-def plane_sum_kernel(got_ref, out_ref):
+def y_sum_kernel(got_ref, out_ref):
     rows = 2 * NZ * SPAN
     total = got_ref[:rows, :].astype(jnp.float32)
-    for i in range(1, HALF // rows):
+    for i in range(1, XROWS // rows):
         total += got_ref[i * rows : (i + 1) * rows, :].astype(jnp.float32)
     out_ref[...] = (total[: rows // 2] + total[rows // 2 :]).astype(jnp.bfloat16)
 
 
-def plane_sum(got):
-    return pl.pallas_call(
-        plane_sum_kernel,
+def y_sum(got):
+    return pl.pallas_call(
+        y_sum_kernel,
         in_specs=[pl.BlockSpec(memory_space=pltpu.VMEM)],
         out_specs=pl.BlockSpec(memory_space=pltpu.VMEM),
         out_shape=jax.ShapeDtypeStruct((NZ * SPAN, QBLK), jnp.bfloat16),
@@ -202,18 +210,23 @@
     gate_up_t = gate_up.T
     core = lax.axis_index("core").astype(jnp.int32).reshape(1)
     place = lax.axis_index(("xl", "core")).astype(jnp.int32).reshape(1)
-    keep, send, weight = partial_spans(shard_order, core, gate_up_t, out_grad, weight_codes, weight_scales)
+    x = lax.axis_index(("xh", "xl")).astype(jnp.int32).reshape(1)
+    keep, send, weight = partial_spans(shard_order, core, x, gate_up_t, out_grad, weight_codes, weight_scales)
     got = lax.ppermute(send, "core", SWAP)
-    weight_x = lax.ppermute(weight, "xl", SWAP)
-    pair = (keep.astype(jnp.float32) + got.astype(jnp.float32)).astype(jnp.bfloat16)
-    got = lax.all_to_all(pair, PLANE, split_axis=0, concat_axis=0, tiled=True)
-    weight_x, weight = lax.optimization_barrier((weight_x, weight))
+    pair = lambda first, last: keep[first:last].astype(jnp.float32) + got[first:last].astype(jnp.float32)
+    first_got = lax.ppermute(pair(2 * XROWS, 4 * XROWS).astype(jnp.bfloat16), XC, FIRST)
+    second_send = (pair(XROWS, 2 * XROWS) + first_got[XROWS:].astype(jnp.float32)).astype(jnp.bfloat16)
+    second_got = lax.ppermute(second_send, XC, SECOND).astype(jnp.float32)
+    line = (pair(0, XROWS) + first_got[:XROWS].astype(jnp.float32) + second_got).astype(jnp.bfloat16)
+    weight, line = lax.optimization_barrier((weight, line))
+    weight_x = lax.ppermute(weight, XC, FIRST)
     weight_core = lax.ppermute(weight, "core", SWAP)
+    got = y_sum(lax.all_to_all(line, "y", split_axis=0, concat_axis=0, tiled=True))
+    weight_x, got = lax.optimization_barrier((weight_x, got))
     weight_both = lax.ppermute(weight_x, "core", SWAP)
+    got = lax.all_to_all(got.reshape(NZ * SPAN // 2, 2, QBLK), "z", split_axis=0, concat_axis=0, tiled=True)
     grads = input_grads(place, gate_up_t, (weight, weight_core, weight_x, weight_both), out_grad)
     got, grads = lax.optimization_barrier((got, grads))
-    line = plane_sum(got).reshape(NZ * SPAN // 2, 2, QBLK)
-    got = lax.all_to_all(line, "z", split_axis=0, concat_axis=0, tiled=True)
     weight_grad = last_sum(got.reshape(NZ * SPAN, QBLK))
     return (grads.T, weight_grad)
 

time: 90 us -> 87.9 us (0.977)
  the two profiles are of different devices: /device:TPU:6 before, /device:TPU:1 now
where the time goes in v6:
time: 87.9 us; the launch traced here: 87.4 us
  starting transfers between devices  42.8 us (49%)
  waiting for transfers between devices  23 us (26%)
  Pallas kernels  15.8 us (18%)
  other arithmetic  4 us (5%)
  local copies, waits for them, and re-layouts  0.96 us (1%)
    ppermute x1, starting transfers between devices, per_device(): got = lax.ppermute(send, 'core', SWAP)  12.4 us
    all_to_all x1, starting transfers between devices, per_device(): lax.all_to_all(got.reshape(NZ * SPAN // 2, 2, QBLK), 'z', split_axis=0, c...  11.6 us
    ppermute x1, waiting for transfers between devices, per_device(): lax.ppermute(pair(2 * XROWS, 4 * XROWS).astype(jnp.bfloat16), XC, FIRST)  8.86 us
    pallas_call x1, Pallas kernels, partial_spans(): pl.pallas_call(partial_kernel, in_specs=[pl.BlockSpec(memory_space=pltpu....  7.8 us
    pallas_call x1, Pallas kernels, input_grads(): pl.pallas_call(grads_kernel, in_specs=[smem, vmem] + [anywhere] * 4 + [pl...  6.77 us
    ppermute x1, starting transfers between devices, per_device(): weight_both = lax.ppermute(weight_x, 'core', SWAP)  5.33 us
    ppermute x1, waiting for transfers between devices, per_device(): second_got = lax.ppermute(second_send, XC, SECOND).astype(jnp.float32)  5.31 us
    all_to_all x1, waiting for transfers between devices, per_device(): lax.all_to_all(line, 'y', split_axis=0, concat_axis=0, tiled=True)  4.88 us
  transfers between devices with their start and end apart: 8, of which 5 were waited for; matrix products, arithmetic and copies ran while one was open for 0% of the time, Pallas kernels for 8%

profile of v6, /device:TPU:1, one launch (start us, length us, event | category | flops | bytes accessed | tf_op | source)
XLA Modules:
  0.0 87.4 jit_solution(11833713807117477746)
XLA Ops:
  0.6 7.8 %shard_map.68 = (bf16[3840,128]{1,0:T(8,128)(2,1)}, bf16[3840,128]{1,0:T(8,128)(2,1)}, bf16[32,8192]{1,0:T(8,128)(2,1)}) custom-call(s32[1]{0:T(128)} %bitcast.core_ref, s32[1]{0:T(128)} %bitcast.1.x_ref, s32[768]{0:T(1024)} %order_hbm.1, bf16[240,256]{1,0:T(8,128)(2,1)} %bitcast.11, bf16[256,8192]{1,0:T(8,128)(2,1)} %out_grad_hbm.3, ...), custom_call_target="tpu_custom_call" | custom-call | flops 503316480 | bytes 6160384 | tf_op jit(solution)/shard_map/pallas_call | solution.py:98
  8.4 12.4 %collective-permute-start = (bf16[3840,128]{1,0:T(8,128)(2,1)}, bf16[3840,128]{1,0:T(8,128)(2,1)S(1)}, u32[]{:S(2)}, u32[]{:S(2)}) collective-permute-start(bf16[3840,128]{1,0:T(8,128)(2,1)} %get-tuple-element.13), channel_id=1, source_target_pairs={{0,1},{1,0},{2,3},{3,2},{4,5},{5,4},{6,7},{7,6},{8,9},{9,8},{10,11... | collective-permute-start | bytes 2949128 | tf_op jit(solution)/shard_map/ppermute | solution.py:215
  20.9 2.4 %collective-permute-done = bf16[3840,128]{1,0:T(8,128)(2,1)S(1)} collective-permute-done((bf16[3840,128]{1,0:T(8,128)(2,1)}, bf16[3840,128]{1,0:T(8,128)(2,1)S(1)}, u32[]{:S(2)}, u32[]{:S(2)}) %collective-permute-start) | collective-permute-done | bytes 983072 | tf_op jit(solution)/shard_map/ppermute | solution.py:215
  23.3 1.2 %add_convert_fusion = bf16[1920,128]{1,0:T(8,128)(2,1)S(1)} fusion(bf16[3840,128]{1,0:T(8,128)(2,1)S(1)} %collective-permute-done, bf16[3840,128]{1,0:T(8,128)(2,1)} %get-tuple-element.12), kind=kLoop, calls=%fused_computation | loop fusion | flops 983040 | bytes 1474560 | tf_op jit(solution)/shard_map/convert_element_type | solution.py:217
  24.4 1.9 %collective-permute-start.1 = (bf16[1920,128]{1,0:T(8,128)(2,1)S(1)}, bf16[1920,128]{1,0:T(8,128)(2,1)S(1)}, u32[]{:S(2)}, u32[]{:S(2)}) collective-permute-start(bf16[1920,128]{1,0:T(8,128)(2,1)S(1)} %add_convert_fusion), channel_id=1, source_target_pairs={{0,2},{1,7},{2,0},{3,5},{4,6},{5,3},{6,4},{7,1},{8,10},{9,15},{10,... | collective-permute-start | bytes 1474568 | tf_op jit(solution)/shard_map/ppermute | solution.py:217
  26.3 8.9 %collective-permute-done.1 = bf16[1920,128]{1,0:T(8,128)(2,1)S(1)} collective-permute-done((bf16[1920,128]{1,0:T(8,128)(2,1)S(1)}, bf16[1920,128]{1,0:T(8,128)(2,1)S(1)}, u32[]{:S(2)}, u32[]{:S(2)}) %collective-permute-start.1) | collective-permute-done | bytes 491552 | tf_op jit(solution)/shard_map/ppermute | solution.py:217
  35.2 1.0 %add_convert_fusion.2 = bf16[960,128]{1,0:T(8,128)(2,1)S(1)} fusion(bf16[1920,128]{1,0:T(8,128)(2,1)S(1)} %collective-permute-done.1, bf16[3840,128]{1,0:T(8,128)(2,1)S(1)} %collective-permute-done, bf16[3840,128]{1,0:T(8,128)(2,1)} %get-tuple-element.12), kind=kLoop, calls=%fused_computation.2 | loop fusion | flops 737280 | bytes 983040 | tf_op jit(solution)/shard_map/convert_element_type | solution.py:218
  36.2 1.9 %collective-permute-start.2 = (bf16[960,128]{1,0:T(8,128)(2,1)S(1)}, bf16[960,128]{1,0:T(8,128)(2,1)S(1)}, u32[]{:S(2)}, u32[]{:S(2)}) collective-permute-start(bf16[960,128]{1,0:T(8,128)(2,1)S(1)} %add_convert_fusion.2), channel_id=1, source_target_pairs={{0,6},{1,3},{2,4},{3,1},{4,2},{5,7},{6,0},{7,5},{8,14},{9,11},{10,... | collective-permute-start | bytes 737288 | tf_op jit(solution)/shard_map/ppermute | solution.py:219
  38.2 5.3 %collective-permute-done.2 = bf16[960,128]{1,0:T(8,128)(2,1)S(1)} collective-permute-done((bf16[960,128]{1,0:T(8,128)(2,1)S(1)}, bf16[960,128]{1,0:T(8,128)(2,1)S(1)}, u32[]{:S(2)}, u32[]{:S(2)}) %collective-permute-start.2) | collective-permute-done | bytes 245792 | tf_op jit(solution)/shard_map/ppermute | solution.py:219
  43.5 1.8 %add_convert_fusion.1 = bf16[960,128]{1,0:T(8,128)(2,1)} fusion(bf16[960,128]{1,0:T(8,128)(2,1)S(1)} %collective-permute-done.2, bf16[1920,128]{1,0:T(8,128)(2,1)S(1)} %collective-permute-done.1, bf16[3840,128]{1,0:T(8,128)(2,1)S(1)} %collective-permute-done, bf16[3840,128]{1,0:T(8,128)(2,1)} %get-tuple-element.12), kind=kLoop, calls=%fused_computation.1 | loop fusion | flops 983040 | bytes 1228800 | tf_op jit(solution)/shard_map/convert_element_type | solution.py:220
  45.3 1.9 %collective-permute-start.3 = (bf16[32,8192]{1,0:T(8,128)(2,1)}, bf16[32,8192]{1,0:T(8,128)(2,1)S(1)}, u32[]{:S(2)}, u32[]{:S(2)}) collective-permute-start(bf16[32,8192]{1,0:T(8,128)(2,1)} %get-tuple-element.14.own_hbm), channel_id=1, source_target_pairs={{0,2},{1,7},{2,0},{3,5},{4,6},{5,3},{6,4},{7,1},{8,10},{9,15},{10,... | collective-permute-start | bytes 1572872 | tf_op jit(solution)/shard_map/ppermute | solution.py:222
  47.2 3.4 %all-to-all-start = ((bf16[8,120,128]{2,1,0:T(8,128)(2,1)}), bf16[8,120,128]{2,1,0:T(8,128)(2,1)S(1)}, u32[]{:S(2)}, u32[]{:S(2)}) async-start(bf16[8,120,128]{2,1,0:T(8,128)(2,1)} %bitcast.3), calls=%async_computation | async-start | bytes 491520 | tf_op jit(solution)/shard_map/all_to_all | solution.py:224
  50.6 4.3 %collective-permute-start.4 = (bf16[32,8192]{1,0:T(8,128)(2,1)}, bf16[32,8192]{1,0:T(8,128)(2,1)S(1)}, u32[]{:S(2)}, u32[]{:S(2)}) collective-permute-start(bf16[32,8192]{1,0:T(8,128)(2,1)} %get-tuple-element.14.own_hbm), channel_id=1, source_target_pairs={{0,1},{1,0},{2,3},{3,2},{4,5},{5,4},{6,7},{7,6},{8,9},{9,8},{10,11... | collective-permute-start | bytes 1572872 | tf_op jit(solution)/shard_map/ppermute | solution.py:223
  54.9 4.9 %all-to-all-done = bf16[8,120,128]{2,1,0:T(8,128)(2,1)S(1)} async-done(((bf16[8,120,128]{2,1,0:T(8,128)(2,1)}), bf16[8,120,128]{2,1,0:T(8,128)(2,1)S(1)}, u32[]{:S(2)}, u32[]{:S(2)}) %all-to-all-start) | async-done | bytes 245792 | tf_op jit(solution)/shard_map/all_to_all | solution.py:224
  59.8 0.6 shard_map.69
  60.4 0.0 collective-permute-done.3.x_hbm
  60.4 0.0 copy-start
  60.4 5.3 %collective-permute-start.5 = (bf16[32,8192]{1,0:T(8,128)(2,1)S(1)}, bf16[32,8192]{1,0:T(8,128)(2,1)S(1)}, u32[]{:S(2)}, u32[]{:S(2)}) collective-permute-start(bf16[32,8192]{1,0:T(8,128)(2,1)S(1)} %collective-permute-done.3.x_hbm), channel_id=1, source_target_pairs={{0,1},{1,0},{2,3},{3,2},{4,5},{5,4},{6,7},{7,6},{8,9},{9,8},{10,11... | collective-permute-start | bytes 1572872 | tf_op jit(solution)/shard_map/ppermute | solution.py:226
  65.8 11.6 %all-to-all-start.1 = ((bf16[60,2,128]{2,1,0:T(2,128)(2,1)}), bf16[60,2,128]{2,1,0:T(2,128)(2,1)S(1)}, u32[]{:S(2)}, u32[]{:S(2)}) async-start(bf16[60,2,128]{2,1,0:T(2,128)(2,1)} %bitcast.5), calls=%async_computation.1 | async-start | bytes 61440 | tf_op jit(solution)/shard_map/all_to_all | solution.py:227
  77.4 0.0 collective-permute-done.4.core_hbm
  77.4 0.0 copy-start.1
  77.4 0.0 collective-permute-done.5.both_hbm
  77.5 0.0 copy-start.2
  77.5 0.0 copy-done
  77.5 0.8 copy-done.1
  78.2 0.2 copy-done.2
  78.4 6.8 %shard_map.70 = bf16[240,256]{1,0:T(8,128)(2,1)} custom-call(s32[1]{0:T(128)} %bitcast.6.place_ref, bf16[240,256]{1,0:T(8,128)(2,1)} %bitcast.12, bf16[32,8192]{1,0:T(8,128)(2,1)} %get-tuple-element.14.own_hbm, bf16[32,8192]{1,0:T(8,128)(2,1)} %copy-done.1, bf16[32,8192]{1,0:T(8,128)(2,1)} %copy-done, bf16[32,8192]{1,0:T(8,128)(2,1)} %copy-done.2, ...), custom_call_target="tpu_custom_call" | custom-call | flops 503316480 | bytes 6291456 | tf_op jit(solution)/shard_map/pallas_call | solution.py:154
  85.2 1.5 %all-to-all-done.1 = bf16[60,2,128]{2,1,0:T(2,128)(2,1)S(1)} async-done(((bf16[60,2,128]{2,1,0:T(2,128)(2,1)}), bf16[60,2,128]{2,1,0:T(2,128)(2,1)S(1)}, u32[]{:S(2)}, u32[]{:S(2)}) %all-to-all-start.1) | async-done | bytes 30752 | tf_op jit(solution)/shard_map/all_to_all | solution.py:227
  86.7 0.6 shard_map.71
Async XLA Ops:
  8.4 14.8 %collective-permute-start = (bf16[3840,128]{1,0:T(8,128)(2,1)}, bf16[3840,128]{1,0:T(8,128)(2,1)S(1)}, u32[]{:S(2)}, u32[]{:S(2)}) collective-permute-start(bf16[3840,128]{1,0:T(8,128)(2,1)} %get-tuple-element.13), channel_id=1, source_target_pairs={{0,1},{1,0},{2,3},{3,2},{4,5},{5,4},{6,7},{7,6},{8,9},{9,8},{10,11... | collective-permute-start | bytes 2949128 | tf_op jit(solution)/shard_map/ppermute | solution.py:215
  24.4 10.8 %collective-permute-start.1 = (bf16[1920,128]{1,0:T(8,128)(2,1)S(1)}, bf16[1920,128]{1,0:T(8,128)(2,1)S(1)}, u32[]{:S(2)}, u32[]{:S(2)}) collective-permute-start(bf16[1920,128]{1,0:T(8,128)(2,1)S(1)} %add_convert_fusion), channel_id=1, source_target_pairs={{0,2},{1,7},{2,0},{3,5},{4,6},{5,3},{6,4},{7,1},{8,10},{9,15},{10,... | collective-permute-start | bytes 1474568 | tf_op jit(solution)/shard_map/ppermute | solution.py:217
  36.2 7.2 %collective-permute-start.2 = (bf16[960,128]{1,0:T(8,128)(2,1)S(1)}, bf16[960,128]{1,0:T(8,128)(2,1)S(1)}, u32[]{:S(2)}, u32[]{:S(2)}) collective-permute-start(bf16[960,128]{1,0:T(8,128)(2,1)S(1)} %add_convert_fusion.2), channel_id=1, source_target_pairs={{0,6},{1,3},{2,4},{3,1},{4,2},{5,7},{6,0},{7,5},{8,14},{9,11},{10,... | collective-permute-start | bytes 737288 | tf_op jit(solution)/shard_map/ppermute | solution.py:219
  45.3 15.2 %collective-permute-start.3 = (bf16[32,8192]{1,0:T(8,128)(2,1)}, bf16[32,8192]{1,0:T(8,128)(2,1)S(1)}, u32[]{:S(2)}, u32[]{:S(2)}) collective-permute-start(bf16[32,8192]{1,0:T(8,128)(2,1)} %get-tuple-element.14.own_hbm), channel_id=1, source_target_pairs={{0,2},{1,7},{2,0},{3,5},{4,6},{5,3},{6,4},{7,1},{8,10},{9,15},{10,... | collective-permute-start | bytes 1572872 | tf_op jit(solution)/shard_map/ppermute | solution.py:222
  47.2 12.6 %all-to-all-start = ((bf16[8,120,128]{2,1,0:T(8,128)(2,1)}), bf16[8,120,128]{2,1,0:T(8,128)(2,1)S(1)}, u32[]{:S(2)}, u32[]{:S(2)}) async-start(bf16[8,120,128]{2,1,0:T(8,128)(2,1)} %bitcast.3), calls=%async_computation | async-start | bytes 491520 | tf_op jit(solution)/shard_map/all_to_all | solution.py:224
  50.6 26.8 %collective-permute-start.4 = (bf16[32,8192]{1,0:T(8,128)(2,1)}, bf16[32,8192]{1,0:T(8,128)(2,1)S(1)}, u32[]{:S(2)}, u32[]{:S(2)}) collective-permute-start(bf16[32,8192]{1,0:T(8,128)(2,1)} %get-tuple-element.14.own_hbm), channel_id=1, source_target_pairs={{0,1},{1,0},{2,3},{3,2},{4,5},{5,4},{6,7},{7,6},{8,9},{9,8},{10,11... | collective-permute-start | bytes 1572872 | tf_op jit(solution)/shard_map/ppermute | solution.py:223
  60.4 17.0 %copy-start = (bf16[32,8192]{1,0:T(8,128)(2,1)}, bf16[32,8192]{1,0:T(8,128)(2,1)S(1)}, u32[]{:S(2)}) copy-start(bf16[32,8192]{1,0:T(8,128)(2,1)S(1)} %collective-permute-done.3.x_hbm) | copy-start | bytes 1572868
  60.4 17.0 %collective-permute-start.5 = (bf16[32,8192]{1,0:T(8,128)(2,1)S(1)}, bf16[32,8192]{1,0:T(8,128)(2,1)S(1)}, u32[]{:S(2)}, u32[]{:S(2)}) collective-permute-start(bf16[32,8192]{1,0:T(8,128)(2,1)S(1)} %collective-permute-done.3.x_hbm), channel_id=1, source_target_pairs={{0,1},{1,0},{2,3},{3,2},{4,5},{5,4},{6,7},{7,6},{8,9},{9,8},{10,11... | collective-permute-start | bytes 1572872 | tf_op jit(solution)/shard_map/ppermute | solution.py:226
  65.8 21.0 %all-to-all-start.1 = ((bf16[60,2,128]{2,1,0:T(2,128)(2,1)}), bf16[60,2,128]{2,1,0:T(2,128)(2,1)S(1)}, u32[]{:S(2)}, u32[]{:S(2)}) async-start(bf16[60,2,128]{2,1,0:T(2,128)(2,1)} %bitcast.5), calls=%async_computation.1 | async-start | bytes 61440 | tf_op jit(solution)/shard_map/all_to_all | solution.py:227
  77.4 0.8 copy-start.1
  77.5 1.0 %copy-start.2 = (bf16[32,8192]{1,0:T(8,128)(2,1)}, bf16[32,8192]{1,0:T(8,128)(2,1)S(1)}, u32[]{:S(2)}) copy-start(bf16[32,8192]{1,0:T(8,128)(2,1)S(1)} %collective-permute-done.5.both_hbm) | copy-start | bytes 1572868

commit v7 on v5

--- a/solution.py
+++ b/solution.py
@@ -24,8 +24,9 @@
 WIDTH = STEP_BLOCKS * QBLK
 SWAP = [(0, 1), (1, 0)]
 OPPOSITE = [(x * 2 + c, (x + (1 if (x + c) % 2 == 0 else -1)) % NX * 2 + c) for x in range(NX) for c in range(2)]
+XROWS = HALF // NX
 ALL = ("y", "z", "xh", "xl", "core")
-PLANE = ("y", "xh", "xl")
+XC = ("xh", "xl", "core")
 
 
 def read_columns(source, target, sems, chunk):
@@ -72,15 +73,14 @@
     core = core_ref[0]
     first = (core * HALF, (1 - core) * HALF)
 
-    def gather(y, carry):
-        for z in range(NZ):
-            for low in range(8):
-                span = order[y * (8 * NZ) + z * 8 + low]
-                place = first[low % 2] + y * (NX * NZ * SPAN) + ((low // 2) * NZ + z) * SPAN
-                staged[pl.ds(place, SPAN), :] = blocks[pl.ds(span * SPAN, SPAN), :]
+    def gather(yz, carry):
+        for low in range(8):
+            span = order[yz * 8 + low]
+            place = first[low % 2] + (low // 2) * XROWS + yz * SPAN
+            staged[pl.ds(place, SPAN), :] = blocks[pl.ds(span * SPAN, SPAN), :]
         return carry
 
-    lax.fori_loop(0, NY, gather, 0)
+    lax.fori_loop(0, NY * NZ, gather, 0, unroll=4)
     keep_ref[...] = staged[:HALF, :].astype(jnp.bfloat16)
     send_ref[...] = staged[HALF:, :].astype(jnp.bfloat16)
 
@@ -160,29 +160,15 @@
     )(place, gate_up_t, *parts, out_grad)
 
 
-def plane_sum_kernel(got_ref, out_ref):
-    rows = 2 * NZ * SPAN
-    total = got_ref[:rows, :].astype(jnp.float32)
-    for i in range(1, HALF // rows):
-        total += got_ref[i * rows : (i + 1) * rows, :].astype(jnp.float32)
-    out_ref[...] = (total[: rows // 2] + total[rows // 2 :]).astype(jnp.bfloat16)
-
-
-def plane_sum(got):
-    return pl.pallas_call(
-        plane_sum_kernel,
-        in_specs=[pl.BlockSpec(memory_space=pltpu.VMEM)],
-        out_specs=pl.BlockSpec(memory_space=pltpu.VMEM),
-        out_shape=jax.ShapeDtypeStruct((NZ * SPAN, QBLK), jnp.bfloat16),
-        compiler_params=pltpu.CompilerParams(vmem_limit_bytes=4 * 2**20),
-    )(got)
-
-
-def last_sum_kernel(got_ref, out_ref, spans):
-    spans[...] = got_ref[...].astype(jnp.float32)
-    span = spans[:SPAN, :]
-    for i in range(1, NZ):
-        span += spans[i * SPAN : (i + 1) * SPAN, :]
+def last_sum_kernel(got_ref, out_ref, total):
+    rows = 8 * SPAN
+    eight = got_ref[:rows, :].astype(jnp.float32)
+    for i in range(1, XROWS // rows):
+        eight += got_ref[i * rows : (i + 1) * rows, :].astype(jnp.float32)
+    total[...] = eight
+    span = total[:SPAN, :]
+    for i in range(1, 8):
+        span += total[i * SPAN : (i + 1) * SPAN, :]
     span = span * (1.0 / DEVICES)
     for i in range(SPAN):
         out_ref[:, i * QBLK : (i + 1) * QBLK] = span[i : i + 1, :]
@@ -194,7 +180,7 @@
         in_specs=[pl.BlockSpec(memory_space=pltpu.VMEM)],
         out_specs=pl.BlockSpec(memory_space=pltpu.VMEM),
         out_shape=jax.ShapeDtypeStruct((1, SPAN * QBLK), jnp.float32),
-        scratch_shapes=[pltpu.VMEM((NZ * SPAN, QBLK), jnp.float32)],
+        scratch_shapes=[pltpu.VMEM((8 * SPAN, QBLK), jnp.float32)],
         compiler_params=pltpu.CompilerParams(vmem_limit_bytes=2 * 2**20),
     )(got)
 
@@ -205,18 +191,18 @@
     place = lax.axis_index(("xl", "core")).astype(jnp.int32).reshape(1)
     keep, send, weight = partial_spans(shard_order, core, gate_up_t, out_grad, weight_codes, weight_scales)
     got = lax.ppermute(send, "core", SWAP)
-    weight_x = lax.ppermute(weight, ("xh", "xl", "core"), OPPOSITE)
     pair = (keep.astype(jnp.float32) + got.astype(jnp.float32)).astype(jnp.bfloat16)
-    weight_x, weight, pair = lax.optimization_barrier((weight_x, weight, pair))
-    got = lax.all_to_all(pair, PLANE, split_axis=0, concat_axis=0, tiled=True)
-    line = plane_sum(got)
-    weight_x, weight, line = lax.optimization_barrier((weight_x, weight, line))
+    got = lax.all_to_all(pair, ("xh", "xl"), split_axis=0, concat_axis=0, tiled=True)
+    parts = [got[i * XROWS : (i + 1) * XROWS].astype(jnp.float32) for i in range(NX)]
+    line = (parts[0] + parts[1] + parts[2] + parts[3]).astype(jnp.bfloat16)
+    weight, line = lax.optimization_barrier((weight, line))
+    weight_x = lax.ppermute(weight, XC, OPPOSITE)
     weight_core = lax.ppermute(weight, "core", SWAP)
     weight_both = lax.ppermute(weight_x, "core", SWAP)
-    got = lax.all_to_all(line.reshape(NZ * SPAN // 2, 2, QBLK), "z", split_axis=0, concat_axis=0, tiled=True)
+    got = lax.all_to_all(line.reshape(XROWS // 2, 2, QBLK), ("y", "z"), split_axis=0, concat_axis=0, tiled=True)
     grads = input_grads(place, gate_up_t, (weight, weight_core, weight_x, weight_both), out_grad)
     got, grads = lax.optimization_barrier((got, grads))
-    weight_grad = last_sum(got.reshape(NZ * SPAN, QBLK))
+    weight_grad = last_sum(got.reshape(XROWS, QBLK))
     return (grads.T, weight_grad)
 
 

time: 90.2 us -> 77.2 us (0.86)
  blocking collectives: 39.3 us -> 24.9 us
  starting transfers between devices: 21.9 us -> 23 us
    all_to_all x1, blocking collectives: 39.3 us -> 24.9 us  [per_device(): lax.all_to_all(pair, ('xh', 'xl'), split_axis=0, concat_axis=0, tiled=True)]
    ppermute x1, waiting for transfers between devices: 7.05 us -> 0.01 us  [per_device(): weight_x = lax.ppermute(weight, XC, OPPOSITE)]
    ppermute x1, waiting for transfers between devices: 0.01 us -> 2.74 us  [per_device(): got = lax.ppermute(send, 'core', SWAP)]
    all_to_all x1, waiting for transfers between devices: 2.75 us -> 5.41 us  [per_device(): lax.all_to_all(line.reshape(XROWS // 2, 2, QBLK), ('y', 'z'), split_axis=...]
    all_to_all x1, starting transfers between devices: 12.9 us -> 14.4 us  [per_device(): lax.all_to_all(line.reshape(XROWS // 2, 2, QBLK), ('y', 'z'), split_axis=...]
    ppermute x1, waiting for transfers between devices: 0.01 us -> 1.49 us  [per_device(): weight_both = lax.ppermute(weight_x, 'core', SWAP)]
  transfers between devices with their start and end apart: 5 -> 5, of which waited for: 2 -> 3; matrix products, arithmetic and copies ran while one was open for 2% -> 0% of each run, Pallas kernels for 8% -> 9%
where the time goes in v7:
time: 77.2 us; the launch traced here: 76.4 us
  blocking collectives  24.9 us (32%)
  starting transfers between devices  23 us (30%)
  Pallas kernels  15 us (19%)
  waiting for transfers between devices  9.65 us (12%)
  other arithmetic  2.27 us (3%)
  local copies, waits for them, and re-layouts  0.84 us (1%)
    all_to_all x1, blocking collectives, per_device(): lax.all_to_all(pair, ('xh', 'xl'), split_axis=0, concat_axis=0, tiled=True)  24.9 us
    all_to_all x1, starting transfers between devices, per_device(): lax.all_to_all(line.reshape(XROWS // 2, 2, QBLK), ('y', 'z'), split_axis=...  14.4 us
    pallas_call x1, Pallas kernels, partial_spans(): pl.pallas_call(partial_kernel, in_specs=[pl.BlockSpec(memory_space=pltpu....  7.6 us
    pallas_call x1, Pallas kernels, input_grads(): pl.pallas_call(grads_kernel, in_specs=[smem, vmem] + [anywhere] * 4 + [pl...  6.76 us
    all_to_all x1, waiting for transfers between devices, per_device(): lax.all_to_all(line.reshape(XROWS // 2, 2, QBLK), ('y', 'z'), split_axis=...  5.41 us
    ppermute x1, waiting for transfers between devices, per_device(): got = lax.ppermute(send, 'core', SWAP)  2.74 us
    ppermute x1, starting transfers between devices, per_device(): weight_both = lax.ppermute(weight_x, 'core', SWAP)  2.34 us
    ppermute x1, starting transfers between devices, per_device(): weight_x = lax.ppermute(weight, XC, OPPOSITE)  2.29 us
  transfers between devices with their start and end apart: 5, of which 3 were waited for; matrix products, arithmetic and copies ran while one was open for 0% of the time, Pallas kernels for 9%

profile of v7, /device:TPU:6, one launch (start us, length us, event | category | flops | bytes accessed | tf_op | source)
XLA Modules:
  0.0 76.4 jit_solution(4792282570463910880)
XLA Ops:
  0.6 7.6 %shard_map.68 = (bf16[3840,128]{1,0:T(8,128)(2,1)}, bf16[3840,128]{1,0:T(8,128)(2,1)}, bf16[32,8192]{1,0:T(8,128)(2,1)}) custom-call(s32[1]{0:T(128)} %bitcast.core_ref, s32[768]{0:T(1024)} %order_hbm.1, bf16[240,256]{1,0:T(8,128)(2,1)} %bitcast.11, bf16[256,8192]{1,0:T(8,128)(2,1)} %out_grad_hbm.3, bf16[30,8192]{1,0:T(8,128)(2,1)} %codes_hbm.1, ...), custom_call_target="tpu_custom_call" | custom-call | flops 503316480 | bytes 6160384 | tf_op jit(solution)/shard_map/pallas_call | solution.py:91
  8.2 1.9 %collective-permute-start = (bf16[3840,128]{1,0:T(8,128)(2,1)}, bf16[3840,128]{1,0:T(8,128)(2,1)S(1)}, u32[]{:S(2)}, u32[]{:S(2)}) collective-permute-start(bf16[3840,128]{1,0:T(8,128)(2,1)} %get-tuple-element.11), channel_id=1, source_target_pairs={{0,1},{1,0},{2,3},{3,2},{4,5},{5,4},{6,7},{7,6},{8,9},{9,8},{10,11... | collective-permute-start | bytes 2949128 | tf_op jit(solution)/shard_map/ppermute | solution.py:193
  10.2 2.7 %collective-permute-done = bf16[3840,128]{1,0:T(8,128)(2,1)S(1)} collective-permute-done((bf16[3840,128]{1,0:T(8,128)(2,1)}, bf16[3840,128]{1,0:T(8,128)(2,1)S(1)}, u32[]{:S(2)}, u32[]{:S(2)}) %collective-permute-start) | collective-permute-done | bytes 983072 | tf_op jit(solution)/shard_map/ppermute | solution.py:193
  12.9 1.5 %add_convert_fusion = bf16[3840,128]{1,0:T(8,128)(2,1)S(1)} fusion(bf16[3840,128]{1,0:T(8,128)(2,1)S(1)} %collective-permute-done, bf16[3840,128]{1,0:T(8,128)(2,1)} %get-tuple-element.10), kind=kLoop, calls=%fused_computation | loop fusion | flops 1966080 | bytes 2949120 | tf_op jit(solution)/shard_map/convert_element_type | solution.py:194
  14.4 0.0 copy-start
  14.4 24.9 %all_to_all.14 = bf16[4,960,128]{2,1,0:T(8,128)(2,1)S(1)} all-to-all(bf16[4,960,128]{2,1,0:T(8,128)(2,1)S(1)} %bitcast.10), channel_id=1, replica_groups=mesh['y'=8,'z'=12,'xh'=2,'xl'=2,'core'=2] {'xh','xl'}, dimensions={0} | all-to-all | bytes 1966080 | tf_op jit(solution)/shard_map/all_to_all | solution.py:195
  39.3 0.8 %fusion = bf16[960,128]{1,0:T(8,128)(2,1)} fusion(bf16[4,960,128]{2,1,0:T(8,128)(2,1)S(1)} %all_to_all.14), kind=kLoop, calls=%fused_computation.2 | loop fusion | flops 983040 | bytes 1228800 | tf_op jit(solution)/shard_map/add | solution.py:197
  40.1 0.0 copy-done
  40.1 2.3 %collective-permute-start.2 = (bf16[32,8192]{1,0:T(8,128)(2,1)S(1)}, bf16[32,8192]{1,0:T(8,128)(2,1)S(1)}, u32[]{:S(2)}, u32[]{:S(2)}) collective-permute-start(bf16[32,8192]{1,0:T(8,128)(2,1)S(1)} %copy-done), channel_id=1, source_target_pairs={{0,2},{1,7},{2,0},{3,5},{4,6},{5,3},{6,4},{7,1},{8,10},{9,15},{10,... | collective-permute-start | bytes 1572872 | tf_op jit(solution)/shard_map/ppermute | solution.py:199
  42.4 14.4 %all-to-all-start.1 = ((bf16[480,2,128]{2,1,0:T(2,128)(2,1)}), bf16[480,2,128]{2,1,0:T(2,128)(2,1)S(1)}, u32[]{:S(2)}, u32[]{:S(2)}) async-start(bf16[480,2,128]{2,1,0:T(2,128)(2,1)} %bitcast.4), calls=%async_computation.1 | async-start | bytes 491520 | tf_op jit(solution)/shard_map/all_to_all | solution.py:202
  56.9 2.0 %collective-permute-start.1 = (bf16[32,8192]{1,0:T(8,128)(2,1)S(1)}, bf16[32,8192]{1,0:T(8,128)(2,1)S(1)}, u32[]{:S(2)}, u32[]{:S(2)}) collective-permute-start(bf16[32,8192]{1,0:T(8,128)(2,1)S(1)} %copy-done), channel_id=1, source_target_pairs={{0,1},{1,0},{2,3},{3,2},{4,5},{5,4},{6,7},{7,6},{8,9},{9,8},{10,11... | collective-permute-start | bytes 1572872 | tf_op jit(solution)/shard_map/ppermute | solution.py:200
  58.9 0.0 collective-permute-done.2.x_hbm
  58.9 0.0 copy-start.1
  58.9 2.3 %collective-permute-start.3 = (bf16[32,8192]{1,0:T(8,128)(2,1)S(1)}, bf16[32,8192]{1,0:T(8,128)(2,1)S(1)}, u32[]{:S(2)}, u32[]{:S(2)}) collective-permute-start(bf16[32,8192]{1,0:T(8,128)(2,1)S(1)} %collective-permute-done.2.x_hbm), channel_id=1, source_target_pairs={{0,1},{1,0},{2,3},{3,2},{4,5},{5,4},{6,7},{7,6},{8,9},{9,8},{10,11... | collective-permute-start | bytes 1572872 | tf_op jit(solution)/shard_map/ppermute | solution.py:201
  61.2 0.0 collective-permute-done.1.core_hbm
  61.3 0.0 copy-start.2
  61.3 1.5 %collective-permute-done.3.both_hbm = bf16[32,8192]{1,0:T(8,128)(2,1)S(1)} collective-permute-done((bf16[32,8192]{1,0:T(8,128)(2,1)S(1)}, bf16[32,8192]{1,0:T(8,128)(2,1)S(1)}, u32[]{:S(2)}, u32[]{:S(2)}) %collective-permute-start.3) | collective-permute-done | bytes 524320 | tf_op jit(solution)/shard_map/ppermute | solution.py:201
  62.8 0.0 copy-start.3
  62.8 0.0 copy-done.1
  62.8 0.0 copy-done.2
  62.8 0.8 %copy-done.3 = bf16[32,8192]{1,0:T(8,128)(2,1)} copy-done((bf16[32,8192]{1,0:T(8,128)(2,1)}, bf16[32,8192]{1,0:T(8,128)(2,1)S(1)}, u32[]{:S(2)}) %copy-start.3) | copy-done | bytes 524312
  63.6 6.8 %shard_map.69 = bf16[240,256]{1,0:T(8,128)(2,1)} custom-call(s32[1]{0:T(128)} %bitcast.5.place_ref, bf16[240,256]{1,0:T(8,128)(2,1)} %bitcast.12, bf16[32,8192]{1,0:T(8,128)(2,1)} %get-tuple-element.13.own_hbm, bf16[32,8192]{1,0:T(8,128)(2,1)} %copy-done.2, bf16[32,8192]{1,0:T(8,128)(2,1)} %copy-done.1, bf16[32,8192]{1,0:T(8,128)(2,1)} %copy-done.3, ...), custom_call_target="tpu_custom_call" | custom-call | flops 503316480 | bytes 6291456 | tf_op jit(solution)/shard_map/pallas_call | solution.py:147
  70.4 5.4 %all-to-all-done.1 = bf16[480,2,128]{2,1,0:T(2,128)(2,1)S(1)} async-done(((bf16[480,2,128]{2,1,0:T(2,128)(2,1)}), bf16[480,2,128]{2,1,0:T(2,128)(2,1)S(1)}, u32[]{:S(2)}, u32[]{:S(2)}) %all-to-all-start.1) | async-done | bytes 245792 | tf_op jit(solution)/shard_map/all_to_all | solution.py:202
  75.8 0.6 shard_map.70
Async XLA Ops:
  8.2 4.7 %collective-permute-start = (bf16[3840,128]{1,0:T(8,128)(2,1)}, bf16[3840,128]{1,0:T(8,128)(2,1)S(1)}, u32[]{:S(2)}, u32[]{:S(2)}) collective-permute-start(bf16[3840,128]{1,0:T(8,128)(2,1)} %get-tuple-element.11), channel_id=1, source_target_pairs={{0,1},{1,0},{2,3},{3,2},{4,5},{5,4},{6,7},{7,6},{8,9},{9,8},{10,11... | collective-permute-start | bytes 2949128 | tf_op jit(solution)/shard_map/ppermute | solution.py:193
  14.4 25.8 %copy-start = (bf16[32,8192]{1,0:T(8,128)(2,1)S(1)}, bf16[32,8192]{1,0:T(8,128)(2,1)}, u32[]{:S(2)}) copy-start(bf16[32,8192]{1,0:T(8,128)(2,1)} %get-tuple-element.13.own_hbm) | copy-start | bytes 1572868
  40.1 18.7 %collective-permute-start.2 = (bf16[32,8192]{1,0:T(8,128)(2,1)S(1)}, bf16[32,8192]{1,0:T(8,128)(2,1)S(1)}, u32[]{:S(2)}, u32[]{:S(2)}) collective-permute-start(bf16[32,8192]{1,0:T(8,128)(2,1)S(1)} %copy-done), channel_id=1, source_target_pairs={{0,2},{1,7},{2,0},{3,5},{4,6},{5,3},{6,4},{7,1},{8,10},{9,15},{10,... | collective-permute-start | bytes 1572872 | tf_op jit(solution)/shard_map/ppermute | solution.py:199
  42.4 33.3 %all-to-all-start.1 = ((bf16[480,2,128]{2,1,0:T(2,128)(2,1)}), bf16[480,2,128]{2,1,0:T(2,128)(2,1)S(1)}, u32[]{:S(2)}, u32[]{:S(2)}) async-start(bf16[480,2,128]{2,1,0:T(2,128)(2,1)} %bitcast.4), calls=%async_computation.1 | async-start | bytes 491520 | tf_op jit(solution)/shard_map/all_to_all | solution.py:202
  56.9 4.4 %collective-permute-start.1 = (bf16[32,8192]{1,0:T(8,128)(2,1)S(1)}, bf16[32,8192]{1,0:T(8,128)(2,1)S(1)}, u32[]{:S(2)}, u32[]{:S(2)}) collective-permute-start(bf16[32,8192]{1,0:T(8,128)(2,1)S(1)} %copy-done), channel_id=1, source_target_pairs={{0,1},{1,0},{2,3},{3,2},{4,5},{5,4},{6,7},{7,6},{8,9},{9,8},{10,11... | collective-permute-start | bytes 1572872 | tf_op jit(solution)/shard_map/ppermute | solution.py:200
  58.9 3.9 %copy-start.1 = (bf16[32,8192]{1,0:T(8,128)(2,1)}, bf16[32,8192]{1,0:T(8,128)(2,1)S(1)}, u32[]{:S(2)}) copy-start(bf16[32,8192]{1,0:T(8,128)(2,1)S(1)} %collective-permute-done.2.x_hbm) | copy-start | bytes 1572868
  58.9 3.9 %collective-permute-start.3 = (bf16[32,8192]{1,0:T(8,128)(2,1)S(1)}, bf16[32,8192]{1,0:T(8,128)(2,1)S(1)}, u32[]{:S(2)}, u32[]{:S(2)}) collective-permute-start(bf16[32,8192]{1,0:T(8,128)(2,1)S(1)} %collective-permute-done.2.x_hbm), channel_id=1, source_target_pairs={{0,1},{1,0},{2,3},{3,2},{4,5},{5,4},{6,7},{7,6},{8,9},{9,8},{10,11... | collective-permute-start | bytes 1572872 | tf_op jit(solution)/shard_map/ppermute | solution.py:201
  61.3 1.5 %copy-start.2 = (bf16[32,8192]{1,0:T(8,128)(2,1)}, bf16[32,8192]{1,0:T(8,128)(2,1)S(1)}, u32[]{:S(2)}) copy-start(bf16[32,8192]{1,0:T(8,128)(2,1)S(1)} %collective-permute-done.1.core_hbm) | copy-start | bytes 1572868
  62.8 0.8 %copy-start.3 = (bf16[32,8192]{1,0:T(8,128)(2,1)}, bf16[32,8192]{1,0:T(8,128)(2,1)S(1)}, u32[]{:S(2)}) copy-start(bf16[32,8192]{1,0:T(8,128)(2,1)S(1)} %collective-permute-done.3.both_hbm) | copy-start | bytes 1572868

commit v8 on v7

--- a/solution.py
+++ b/solution.py
@@ -22,6 +22,8 @@
 STEP_BLOCKS = 16
 STEPS = BLOCKS // STEP_BLOCKS
 WIDTH = STEP_BLOCKS * QBLK
+GRAD_STEPS = 2
+GRAD_WIDTH = D // GRAD_STEPS
 SWAP = [(0, 1), (1, 0)]
 OPPOSITE = [(x * 2 + c, (x + (1 if (x + c) % 2 == 0 else -1)) % NX * 2 + c) for x in range(NX) for c in range(2)]
 XROWS = HALF // NX
@@ -29,14 +31,14 @@
 XC = ("xh", "xl", "core")
 
 
-def read_columns(source, target, sems, chunk):
-    columns = pl.ds(chunk * WIDTH, WIDTH)
+def read_columns(source, target, sems, chunk, width=WIDTH):
+    columns = pl.ds(chunk * width, width)
     return pltpu.make_async_copy(source.at[:, columns], target.at[:, columns], sems.at[chunk])
 
 
 def partial_kernel(
-    core_ref, order_hbm, gate_up_hbm, out_grad_hbm, codes_hbm, scales_hbm, keep_ref, send_ref, weight_ref,
-    order, gate_up, codes, scales, out_grad, blocks, staged, sems, small_sems,
+    core_ref, order_hbm, gate_up_hbm, out_grad_hbm, codes_hbm, scales_hbm, keep_hbm, send_hbm, weight_hbm,
+    order, gate_up, codes, scales, out_grad, blocks, staged, spans_out, weight_out, sems, small_sems, write_sems,
 ):
     small = [
         pltpu.make_async_copy(source, target, small_sems.at[i])
@@ -68,30 +70,36 @@
         one_hot = (lax.broadcasted_iota(jnp.int32, (BLOCKS, WIDTH), 0) == block_of).astype(jnp.float32)
         wide = jnp.dot(scales[...], one_hot.astype(jnp.bfloat16), preferred_element_type=jnp.float32)
         weight = codes[:, columns].astype(jnp.float32) * wide
-        weight_ref[:, columns] = jnp.concatenate([weight, fill], axis=0).astype(jnp.bfloat16)
-
+        weight_out[:, columns] = jnp.concatenate([weight, fill], axis=0).astype(jnp.bfloat16)
+
+    weight_write = pltpu.make_async_copy(weight_out, weight_hbm, write_sems.at[2 * NX])
+    weight_write.start()
     core = core_ref[0]
-    first = (core * HALF, (1 - core) * HALF)
-
-    def gather(yz, carry):
-        for low in range(8):
-            span = order[yz * 8 + low]
-            place = first[low % 2] + (low // 2) * XROWS + yz * SPAN
-            staged[pl.ds(place, SPAN), :] = blocks[pl.ds(span * SPAN, SPAN), :]
-        return carry
-
-    lax.fori_loop(0, NY * NZ, gather, 0, unroll=4)
-    keep_ref[...] = staged[:HALF, :].astype(jnp.bfloat16)
-    send_ref[...] = staged[HALF:, :].astype(jnp.bfloat16)
+    writes = [weight_write]
+    for side, (owner_core, target) in enumerate(((core, keep_hbm), (1 - core, send_hbm))):
+        for x in range(NX):
+            rows = pl.ds(x * XROWS, XROWS)
+
+            def gather(yz, carry):
+                span = order[yz * 8 + x * 2 + owner_core]
+                staged[pl.ds(yz * SPAN, SPAN), :] = blocks[pl.ds(span * SPAN, SPAN), :]
+                return carry
+
+            lax.fori_loop(0, NY * NZ, gather, 0, unroll=32)
+            spans_out[side, rows, :] = staged[...].astype(jnp.bfloat16)
+            write = pltpu.make_async_copy(spans_out.at[side, rows, :], target.at[rows, :], write_sems.at[side * NX + x])
+            write.start()
+            writes.append(write)
+    for write in writes:
+        write.wait()
 
 
 def partial_spans(order, core, gate_up_t, out_grad, codes, scales):
     hbm = pl.BlockSpec(memory_space=pltpu.HBM)
-    vmem = pl.BlockSpec(memory_space=pltpu.VMEM)
     return pl.pallas_call(
         partial_kernel,
         in_specs=[pl.BlockSpec(memory_space=pltpu.SMEM)] + [hbm] * 5,
-        out_specs=[vmem, vmem, vmem],
+        out_specs=[hbm, hbm, hbm],
         scratch_shapes=[
             pltpu.SMEM((DEVICES,), jnp.int32),
             pltpu.VMEM((2 * FW, TOK), jnp.bfloat16),
@@ -99,9 +107,12 @@
             pltpu.VMEM((NODE_ROWS, BLOCKS), jnp.bfloat16),
             pltpu.VMEM((TOK, D), jnp.bfloat16),
             pltpu.VMEM((ROWS, QBLK), jnp.float32),
-            pltpu.VMEM((ROWS, QBLK), jnp.float32),
+            pltpu.VMEM((XROWS, QBLK), jnp.float32),
+            pltpu.VMEM((2, HALF, QBLK), jnp.bfloat16),
+            pltpu.VMEM((PAD_ROWS, D), jnp.bfloat16),
             pltpu.SemaphoreType.DMA((STEPS,)),
             pltpu.SemaphoreType.DMA((4,)),
+            pltpu.SemaphoreType.DMA((2 * NX + 1,)),
         ],
         out_shape=[
             jax.ShapeDtypeStruct((HALF, QBLK), jnp.bfloat16),
@@ -119,17 +130,17 @@
         row = pl.multiple_of(jnp.bitwise_xor(place_ref[0], i) * PAD_ROWS, PAD_ROWS)
         reads.append(pltpu.make_async_copy(part, weight.at[pl.ds(row, PAD_ROWS), :], weight_sems.at[i]))
         reads[-1].start()
-    for chunk in range(STEPS):
-        read_columns(out_grad_hbm, out_grad, sems, chunk).start()
+    for chunk in range(GRAD_STEPS):
+        read_columns(out_grad_hbm, out_grad, sems, chunk, GRAD_WIDTH).start()
     both = gate_up_ref[...].astype(jnp.float32)
     gate, up = both[:FW], both[FW:]
     sig = jax.nn.sigmoid(gate)
     for read in reads:
         read.wait()
     total = jnp.zeros((TOK, 4 * PAD_ROWS), jnp.float32)
-    for chunk in range(STEPS):
-        columns = slice(chunk * WIDTH, (chunk + 1) * WIDTH)
-        read_columns(out_grad_hbm, out_grad, sems, chunk).wait()
+    for chunk in range(GRAD_STEPS):
+        columns = slice(chunk * GRAD_WIDTH, (chunk + 1) * GRAD_WIDTH)
+        read_columns(out_grad_hbm, out_grad, sems, chunk, GRAD_WIDTH).wait()
         total += lax.dot_general(
             out_grad[:, columns], weight[:, columns], (((1,), (1,)), ((), ())), preferred_element_type=jnp.float32
         )
@@ -152,7 +163,7 @@
             pltpu.VMEM((4 * PAD_ROWS, D), jnp.bfloat16),
             pltpu.VMEM((TOK, D), jnp.bfloat16),
             pltpu.SemaphoreType.DMA((4,)),
-            pltpu.SemaphoreType.DMA((STEPS,)),
+            pltpu.SemaphoreType.DMA((GRAD_STEPS,)),
         ],
         out_shape=jax.ShapeDtypeStruct((2 * FW, TOK), jnp.bfloat16),
         compiler_params=pltpu.CompilerParams(vmem_limit_bytes=56 * 2**20),

time: 77.2 us -> 76.7 us (level)
  Pallas kernels: 15 us -> 13.6 us
  waiting for transfers between devices: 9.65 us -> 10.6 us
    pallas_call x1, Pallas kernels: 6.76 us -> 5.81 us  [input_grads(): pl.pallas_call(grads_kernel, in_specs=[smem, vmem] + [anywhere] * 4 + [pl...]
    all_to_all x1, waiting for transfers between devices: 5.41 us -> 6.37 us  [per_device(): lax.all_to_all(line.reshape(XROWS // 2, 2, QBLK), ('y', 'z'), split_axis=...]
  transfers between devices with their start and end apart: 5 -> 5, of which waited for: 3 -> 3; matrix products, arithmetic and copies ran while one was open for 0% -> 0% of each run, Pallas kernels for 9% -> 8%
where the time goes in v8:
time: 76.7 us; the launch traced here: 75.9 us
  blocking collectives  24.9 us (32%)
  starting transfers between devices  23 us (30%)
  Pallas kernels  13.6 us (18%)
  waiting for transfers between devices  10.6 us (14%)
  other arithmetic  2.27 us (3%)
  local copies, waits for them, and re-layouts  0.84 us (1%)
    all_to_all x1, blocking collectives, per_device(): lax.all_to_all(pair, ('xh', 'xl'), split_axis=0, concat_axis=0, tiled=True)  24.9 us
    all_to_all x1, starting transfers between devices, per_device(): lax.all_to_all(line.reshape(XROWS // 2, 2, QBLK), ('y', 'z'), split_axis=...  14.4 us
    pallas_call x1, Pallas kernels, partial_spans(): pl.pallas_call(partial_kernel, in_specs=[pl.BlockSpec(memory_space=pltpu....  7.11 us
    all_to_all x1, waiting for transfers between devices, per_device(): lax.all_to_all(line.reshape(XROWS // 2, 2, QBLK), ('y', 'z'), split_axis=...  6.37 us
    pallas_call x1, Pallas kernels, input_grads(): pl.pallas_call(grads_kernel, in_specs=[smem, vmem] + [anywhere] * 4 + [pl...  5.81 us
    ppermute x1, waiting for transfers between devices, per_device(): got = lax.ppermute(send, 'core', SWAP)  2.74 us
    ppermute x1, starting transfers between devices, per_device(): weight_both = lax.ppermute(weight_x, 'core', SWAP)  2.34 us
    ppermute x1, starting transfers between devices, per_device(): weight_x = lax.ppermute(weight, XC, OPPOSITE)  2.29 us
  transfers between devices with their start and end apart: 5, of which 3 were waited for; matrix products, arithmetic and copies ran while one was open for 0% of the time, Pallas kernels for 8%

profile of v8, /device:TPU:6, one launch (start us, length us, event | category | flops | bytes accessed | tf_op | source)
XLA Modules:
  0.0 75.9 jit_solution(8019898356147306245)
XLA Ops:
  0.6 7.1 %shard_map.68 = (bf16[3840,128]{1,0:T(8,128)(2,1)}, bf16[3840,128]{1,0:T(8,128)(2,1)}, bf16[32,8192]{1,0:T(8,128)(2,1)}) custom-call(s32[1]{0:T(128)} %bitcast.core_ref, s32[768]{0:T(1024)} %order_hbm.1, bf16[240,256]{1,0:T(8,128)(2,1)} %bitcast.11, bf16[256,8192]{1,0:T(8,128)(2,1)} %out_grad_hbm.3, bf16[30,8192]{1,0:T(8,128)(2,1)} %codes_hbm.1, ...), custom_call_target="tpu_custom_call" | custom-call | flops 503316480 | bytes 6160384 | tf_op jit(solution)/shard_map/pallas_call | solution.py:99
  7.8 1.9 %collective-permute-start = (bf16[3840,128]{1,0:T(8,128)(2,1)}, bf16[3840,128]{1,0:T(8,128)(2,1)S(1)}, u32[]{:S(2)}, u32[]{:S(2)}) collective-permute-start(bf16[3840,128]{1,0:T(8,128)(2,1)} %get-tuple-element.11), channel_id=1, source_target_pairs={{0,1},{1,0},{2,3},{3,2},{4,5},{5,4},{6,7},{7,6},{8,9},{9,8},{10,11... | collective-permute-start | bytes 2949128 | tf_op jit(solution)/shard_map/ppermute | solution.py:204
  9.7 2.7 %collective-permute-done = bf16[3840,128]{1,0:T(8,128)(2,1)S(1)} collective-permute-done((bf16[3840,128]{1,0:T(8,128)(2,1)}, bf16[3840,128]{1,0:T(8,128)(2,1)S(1)}, u32[]{:S(2)}, u32[]{:S(2)}) %collective-permute-start) | collective-permute-done | bytes 983072 | tf_op jit(solution)/shard_map/ppermute | solution.py:204
  12.4 1.5 %add_convert_fusion = bf16[3840,128]{1,0:T(8,128)(2,1)S(1)} fusion(bf16[3840,128]{1,0:T(8,128)(2,1)S(1)} %collective-permute-done, bf16[3840,128]{1,0:T(8,128)(2,1)} %get-tuple-element.10), kind=kLoop, calls=%fused_computation | loop fusion | flops 1966080 | bytes 2949120 | tf_op jit(solution)/shard_map/convert_element_type | solution.py:205
  13.9 0.0 copy-start
  13.9 24.9 %all_to_all.14 = bf16[4,960,128]{2,1,0:T(8,128)(2,1)S(1)} all-to-all(bf16[4,960,128]{2,1,0:T(8,128)(2,1)S(1)} %bitcast.10), channel_id=1, replica_groups=mesh['y'=8,'z'=12,'xh'=2,'xl'=2,'core'=2] {'xh','xl'}, dimensions={0} | all-to-all | bytes 1966080 | tf_op jit(solution)/shard_map/all_to_all | solution.py:206
  38.8 0.8 %fusion = bf16[960,128]{1,0:T(8,128)(2,1)} fusion(bf16[4,960,128]{2,1,0:T(8,128)(2,1)S(1)} %all_to_all.14), kind=kLoop, calls=%fused_computation.2 | loop fusion | flops 983040 | bytes 1228800 | tf_op jit(solution)/shard_map/add | solution.py:208
  39.6 0.0 copy-done
  39.6 2.3 %collective-permute-start.2 = (bf16[32,8192]{1,0:T(8,128)(2,1)S(1)}, bf16[32,8192]{1,0:T(8,128)(2,1)S(1)}, u32[]{:S(2)}, u32[]{:S(2)}) collective-permute-start(bf16[32,8192]{1,0:T(8,128)(2,1)S(1)} %copy-done), channel_id=1, source_target_pairs={{0,2},{1,7},{2,0},{3,5},{4,6},{5,3},{6,4},{7,1},{8,10},{9,15},{10,... | collective-permute-start | bytes 1572872 | tf_op jit(solution)/shard_map/ppermute | solution.py:210
  41.9 14.4 %all-to-all-start.1 = ((bf16[480,2,128]{2,1,0:T(2,128)(2,1)}), bf16[480,2,128]{2,1,0:T(2,128)(2,1)S(1)}, u32[]{:S(2)}, u32[]{:S(2)}) async-start(bf16[480,2,128]{2,1,0:T(2,128)(2,1)} %bitcast.4), calls=%async_computation.1 | async-start | bytes 491520 | tf_op jit(solution)/shard_map/all_to_all | solution.py:213
  56.4 2.0 %collective-permute-start.1 = (bf16[32,8192]{1,0:T(8,128)(2,1)S(1)}, bf16[32,8192]{1,0:T(8,128)(2,1)S(1)}, u32[]{:S(2)}, u32[]{:S(2)}) collective-permute-start(bf16[32,8192]{1,0:T(8,128)(2,1)S(1)} %copy-done), channel_id=1, source_target_pairs={{0,1},{1,0},{2,3},{3,2},{4,5},{5,4},{6,7},{7,6},{8,9},{9,8},{10,11... | collective-permute-start | bytes 1572872 | tf_op jit(solution)/shard_map/ppermute | solution.py:211
  58.4 0.0 collective-permute-done.2.x_hbm
  58.4 0.0 copy-start.1
  58.4 2.3 %collective-permute-start.3 = (bf16[32,8192]{1,0:T(8,128)(2,1)S(1)}, bf16[32,8192]{1,0:T(8,128)(2,1)S(1)}, u32[]{:S(2)}, u32[]{:S(2)}) collective-permute-start(bf16[32,8192]{1,0:T(8,128)(2,1)S(1)} %collective-permute-done.2.x_hbm), channel_id=1, source_target_pairs={{0,1},{1,0},{2,3},{3,2},{4,5},{5,4},{6,7},{7,6},{8,9},{9,8},{10,11... | collective-permute-start | bytes 1572872 | tf_op jit(solution)/shard_map/ppermute | solution.py:212
  60.8 0.0 collective-permute-done.1.core_hbm
  60.8 0.0 copy-start.2
  60.8 1.5 %collective-permute-done.3.both_hbm = bf16[32,8192]{1,0:T(8,128)(2,1)S(1)} collective-permute-done((bf16[32,8192]{1,0:T(8,128)(2,1)S(1)}, bf16[32,8192]{1,0:T(8,128)(2,1)S(1)}, u32[]{:S(2)}, u32[]{:S(2)}) %collective-permute-start.3) | collective-permute-done | bytes 524320 | tf_op jit(solution)/shard_map/ppermute | solution.py:212
  62.3 0.0 copy-start.3
  62.3 0.0 copy-done.1
  62.3 0.0 copy-done.2
  62.3 0.8 %copy-done.3 = bf16[32,8192]{1,0:T(8,128)(2,1)} copy-done((bf16[32,8192]{1,0:T(8,128)(2,1)}, bf16[32,8192]{1,0:T(8,128)(2,1)S(1)}, u32[]{:S(2)}) %copy-start.3) | copy-done | bytes 524312
  63.1 5.8 %shard_map.69 = bf16[240,256]{1,0:T(8,128)(2,1)} custom-call(s32[1]{0:T(128)} %bitcast.5.place_ref, bf16[240,256]{1,0:T(8,128)(2,1)} %bitcast.12, bf16[32,8192]{1,0:T(8,128)(2,1)} %get-tuple-element.13.own_hbm, bf16[32,8192]{1,0:T(8,128)(2,1)} %copy-done.2, bf16[32,8192]{1,0:T(8,128)(2,1)} %copy-done.1, bf16[32,8192]{1,0:T(8,128)(2,1)} %copy-done.3, ...), custom_call_target="tpu_custom_call" | custom-call | flops 503316480 | bytes 6291456 | tf_op jit(solution)/shard_map/pallas_call | solution.py:158
  68.9 6.4 %all-to-all-done.1 = bf16[480,2,128]{2,1,0:T(2,128)(2,1)S(1)} async-done(((bf16[480,2,128]{2,1,0:T(2,128)(2,1)}), bf16[480,2,128]{2,1,0:T(2,128)(2,1)S(1)}, u32[]{:S(2)}, u32[]{:S(2)}) %all-to-all-start.1) | async-done | bytes 245792 | tf_op jit(solution)/shard_map/all_to_all | solution.py:213
  75.3 0.6 shard_map.70
Async XLA Ops:
  7.8 4.7 %collective-permute-start = (bf16[3840,128]{1,0:T(8,128)(2,1)}, bf16[3840,128]{1,0:T(8,128)(2,1)S(1)}, u32[]{:S(2)}, u32[]{:S(2)}) collective-permute-start(bf16[3840,128]{1,0:T(8,128)(2,1)} %get-tuple-element.11), channel_id=1, source_target_pairs={{0,1},{1,0},{2,3},{3,2},{4,5},{5,4},{6,7},{7,6},{8,9},{9,8},{10,11... | collective-permute-start | bytes 2949128 | tf_op jit(solution)/shard_map/ppermute | solution.py:204
  13.9 25.8 %copy-start = (bf16[32,8192]{1,0:T(8,128)(2,1)S(1)}, bf16[32,8192]{1,0:T(8,128)(2,1)}, u32[]{:S(2)}) copy-start(bf16[32,8192]{1,0:T(8,128)(2,1)} %get-tuple-element.13.own_hbm) | copy-start | bytes 1572868
  39.6 18.7 %collective-permute-start.2 = (bf16[32,8192]{1,0:T(8,128)(2,1)S(1)}, bf16[32,8192]{1,0:T(8,128)(2,1)S(1)}, u32[]{:S(2)}, u32[]{:S(2)}) collective-permute-start(bf16[32,8192]{1,0:T(8,128)(2,1)S(1)} %copy-done), channel_id=1, source_target_pairs={{0,2},{1,7},{2,0},{3,5},{4,6},{5,3},{6,4},{7,1},{8,10},{9,15},{10,... | collective-permute-start | bytes 1572872 | tf_op jit(solution)/shard_map/ppermute | solution.py:210
  41.9 33.3 %all-to-all-start.1 = ((bf16[480,2,128]{2,1,0:T(2,128)(2,1)}), bf16[480,2,128]{2,1,0:T(2,128)(2,1)S(1)}, u32[]{:S(2)}, u32[]{:S(2)}) async-start(bf16[480,2,128]{2,1,0:T(2,128)(2,1)} %bitcast.4), calls=%async_computation.1 | async-start | bytes 491520 | tf_op jit(solution)/shard_map/all_to_all | solution.py:213
  56.4 4.4 %collective-permute-start.1 = (bf16[32,8192]{1,0:T(8,128)(2,1)S(1)}, bf16[32,8192]{1,0:T(8,128)(2,1)S(1)}, u32[]{:S(2)}, u32[]{:S(2)}) collective-permute-start(bf16[32,8192]{1,0:T(8,128)(2,1)S(1)} %copy-done), channel_id=1, source_target_pairs={{0,1},{1,0},{2,3},{3,2},{4,5},{5,4},{6,7},{7,6},{8,9},{9,8},{10,11... | collective-permute-start | bytes 1572872 | tf_op jit(solution)/shard_map/ppermute | solution.py:211
  58.4 3.9 %copy-start.1 = (bf16[32,8192]{1,0:T(8,128)(2,1)}, bf16[32,8192]{1,0:T(8,128)(2,1)S(1)}, u32[]{:S(2)}) copy-start(bf16[32,8192]{1,0:T(8,128)(2,1)S(1)} %collective-permute-done.2.x_hbm) | copy-start | bytes 1572868
  58.4 3.9 %collective-permute-start.3 = (bf16[32,8192]{1,0:T(8,128)(2,1)S(1)}, bf16[32,8192]{1,0:T(8,128)(2,1)S(1)}, u32[]{:S(2)}, u32[]{:S(2)}) collective-permute-start(bf16[32,8192]{1,0:T(8,128)(2,1)S(1)} %collective-permute-done.2.x_hbm), channel_id=1, source_target_pairs={{0,1},{1,0},{2,3},{3,2},{4,5},{5,4},{6,7},{7,6},{8,9},{9,8},{10,11... | collective-permute-start | bytes 1572872 | tf_op jit(solution)/shard_map/ppermute | solution.py:212
  60.8 1.5 %copy-start.2 = (bf16[32,8192]{1,0:T(8,128)(2,1)}, bf16[32,8192]{1,0:T(8,128)(2,1)S(1)}, u32[]{:S(2)}) copy-start(bf16[32,8192]{1,0:T(8,128)(2,1)S(1)} %collective-permute-done.1.core_hbm) | copy-start | bytes 1572868
  62.3 0.8 %copy-start.3 = (bf16[32,8192]{1,0:T(8,128)(2,1)}, bf16[32,8192]{1,0:T(8,128)(2,1)S(1)}, u32[]{:S(2)}) copy-start(bf16[32,8192]{1,0:T(8,128)(2,1)S(1)} %collective-permute-done.3.both_hbm) | copy-start | bytes 1572868

commit v9 on v8

--- a/solution.py
+++ b/solution.py
@@ -80,9 +80,10 @@
         for x in range(NX):
             rows = pl.ds(x * XROWS, XROWS)
 
-            def gather(yz, carry):
-                span = order[yz * 8 + x * 2 + owner_core]
-                staged[pl.ds(yz * SPAN, SPAN), :] = blocks[pl.ds(span * SPAN, SPAN), :]
+            def gather(zy, carry):
+                owner = ((zy & (NY - 1)) * NZ + (zy >> 3)) * 8 + x * 2 + owner_core
+                span = order[owner]
+                staged[pl.ds(zy * SPAN, SPAN), :] = blocks[pl.ds(span * SPAN, SPAN), :]
                 return carry
 
             lax.fori_loop(0, NY * NZ, gather, 0, unroll=32)
@@ -210,7 +211,7 @@
     weight_x = lax.ppermute(weight, XC, OPPOSITE)
     weight_core = lax.ppermute(weight, "core", SWAP)
     weight_both = lax.ppermute(weight_x, "core", SWAP)
-    got = lax.all_to_all(line.reshape(XROWS // 2, 2, QBLK), ("y", "z"), split_axis=0, concat_axis=0, tiled=True)
+    got = lax.all_to_all(line.reshape(XROWS // 2, 2, QBLK), ("z", "y"), split_axis=0, concat_axis=0, tiled=True)
     grads = input_grads(place, gate_up_t, (weight, weight_core, weight_x, weight_both), out_grad)
     got, grads = lax.optimization_barrier((got, grads))
     weight_grad = last_sum(got.reshape(XROWS, QBLK))

time: 76.7 us -> 78.3 us (1.021)
  Pallas kernels: 13.6 us -> 14.6 us
  waiting for transfers between devices: 10.6 us -> 11.6 us
    pallas_call x1, Pallas kernels: 7.11 us -> 8.13 us  [partial_spans(): pl.pallas_call(partial_kernel, in_specs=[pl.BlockSpec(memory_space=pltpu....]
    all_to_all x1, waiting for transfers between devices: 6.37 us -> 7.33 us  [per_device(): lax.all_to_all(line.reshape(XROWS // 2, 2, QBLK), ('z', 'y'), split_axis=...]
  transfers between devices with their start and end apart: 5 -> 5, of which waited for: 3 -> 3; matrix products, arithmetic and copies ran while one was open for 0% -> 0% of each run, Pallas kernels for 8% -> 7%
where the time goes in v9:
time: 78.3 us; the launch traced here: 77.9 us
  blocking collectives  24.9 us (32%)
  starting transfers between devices  23 us (29%)
  Pallas kernels  14.6 us (19%)
  waiting for transfers between devices  11.6 us (15%)
  other arithmetic  2.27 us (3%)
  local copies, waits for them, and re-layouts  0.84 us (1%)
    all_to_all x1, blocking collectives, per_device(): lax.all_to_all(pair, ('xh', 'xl'), split_axis=0, concat_axis=0, tiled=True)  24.9 us
    all_to_all x1, starting transfers between devices, per_device(): lax.all_to_all(line.reshape(XROWS // 2, 2, QBLK), ('z', 'y'), split_axis=...  14.4 us
    pallas_call x1, Pallas kernels, partial_spans(): pl.pallas_call(partial_kernel, in_specs=[pl.BlockSpec(memory_space=pltpu....  8.13 us
    all_to_all x1, waiting for transfers between devices, per_device(): lax.all_to_all(line.reshape(XROWS // 2, 2, QBLK), ('z', 'y'), split_axis=...  7.33 us
    pallas_call x1, Pallas kernels, input_grads(): pl.pallas_call(grads_kernel, in_specs=[smem, vmem] + [anywhere] * 4 + [pl...  5.81 us
    ppermute x1, waiting for transfers between devices, per_device(): got = lax.ppermute(send, 'core', SWAP)  2.74 us
    ppermute x1, starting transfers between devices, per_device(): weight_both = lax.ppermute(weight_x, 'core', SWAP)  2.34 us
    ppermute x1, starting transfers between devices, per_device(): weight_x = lax.ppermute(weight, XC, OPPOSITE)  2.29 us
  transfers between devices with their start and end apart: 5, of which 3 were waited for; matrix products, arithmetic and copies ran while one was open for 0% of the time, Pallas kernels for 7%

profile of v9, /device:TPU:6, one launch (start us, length us, event | category | flops | bytes accessed | tf_op | source)
XLA Modules:
  0.0 77.9 jit_solution(3358041223312852860)
XLA Ops:
  0.6 8.1 %shard_map.68 = (bf16[3840,128]{1,0:T(8,128)(2,1)}, bf16[3840,128]{1,0:T(8,128)(2,1)}, bf16[32,8192]{1,0:T(8,128)(2,1)}) custom-call(s32[1]{0:T(128)} %bitcast.core_ref, s32[768]{0:T(1024)} %order_hbm.1, bf16[240,256]{1,0:T(8,128)(2,1)} %bitcast.11, bf16[256,8192]{1,0:T(8,128)(2,1)} %out_grad_hbm.3, bf16[30,8192]{1,0:T(8,128)(2,1)} %codes_hbm.1, ...), custom_call_target="tpu_custom_call" | custom-call | flops 503316480 | bytes 6160384 | tf_op jit(solution)/shard_map/pallas_call | solution.py:100
  8.8 1.9 %collective-permute-start = (bf16[3840,128]{1,0:T(8,128)(2,1)}, bf16[3840,128]{1,0:T(8,128)(2,1)S(1)}, u32[]{:S(2)}, u32[]{:S(2)}) collective-permute-start(bf16[3840,128]{1,0:T(8,128)(2,1)} %get-tuple-element.11), channel_id=1, source_target_pairs={{0,1},{1,0},{2,3},{3,2},{4,5},{5,4},{6,7},{7,6},{8,9},{9,8},{10,11... | collective-permute-start | bytes 2949128 | tf_op jit(solution)/shard_map/ppermute | solution.py:205
  10.7 2.7 %collective-permute-done = bf16[3840,128]{1,0:T(8,128)(2,1)S(1)} collective-permute-done((bf16[3840,128]{1,0:T(8,128)(2,1)}, bf16[3840,128]{1,0:T(8,128)(2,1)S(1)}, u32[]{:S(2)}, u32[]{:S(2)}) %collective-permute-start) | collective-permute-done | bytes 983072 | tf_op jit(solution)/shard_map/ppermute | solution.py:205
  13.4 1.5 %add_convert_fusion = bf16[3840,128]{1,0:T(8,128)(2,1)S(1)} fusion(bf16[3840,128]{1,0:T(8,128)(2,1)S(1)} %collective-permute-done, bf16[3840,128]{1,0:T(8,128)(2,1)} %get-tuple-element.10), kind=kLoop, calls=%fused_computation | loop fusion | flops 1966080 | bytes 2949120 | tf_op jit(solution)/shard_map/convert_element_type | solution.py:206
  14.9 0.0 copy-start
  14.9 24.9 %all_to_all.14 = bf16[4,960,128]{2,1,0:T(8,128)(2,1)S(1)} all-to-all(bf16[4,960,128]{2,1,0:T(8,128)(2,1)S(1)} %bitcast.10), channel_id=1, replica_groups=mesh['y'=8,'z'=12,'xh'=2,'xl'=2,'core'=2] {'xh','xl'}, dimensions={0} | all-to-all | bytes 1966080 | tf_op jit(solution)/shard_map/all_to_all | solution.py:207
  39.8 0.8 %fusion = bf16[960,128]{1,0:T(8,128)(2,1)} fusion(bf16[4,960,128]{2,1,0:T(8,128)(2,1)S(1)} %all_to_all.14), kind=kLoop, calls=%fused_computation.2 | loop fusion | flops 983040 | bytes 1228800 | tf_op jit(solution)/shard_map/add | solution.py:209
  40.7 0.0 copy-done
  40.7 2.3 %collective-permute-start.2 = (bf16[32,8192]{1,0:T(8,128)(2,1)S(1)}, bf16[32,8192]{1,0:T(8,128)(2,1)S(1)}, u32[]{:S(2)}, u32[]{:S(2)}) collective-permute-start(bf16[32,8192]{1,0:T(8,128)(2,1)S(1)} %copy-done), channel_id=1, source_target_pairs={{0,2},{1,7},{2,0},{3,5},{4,6},{5,3},{6,4},{7,1},{8,10},{9,15},{10,... | collective-permute-start | bytes 1572872 | tf_op jit(solution)/shard_map/ppermute | solution.py:211
  43.0 14.4 %all-to-all-start.1 = ((bf16[480,2,128]{2,1,0:T(2,128)(2,1)}), bf16[480,2,128]{2,1,0:T(2,128)(2,1)S(1)}, u32[]{:S(2)}, u32[]{:S(2)}) async-start(bf16[480,2,128]{2,1,0:T(2,128)(2,1)} %bitcast.4), calls=%async_computation.1 | async-start | bytes 491520 | tf_op jit(solution)/shard_map/all_to_all | solution.py:214
  57.4 2.0 %collective-permute-start.1 = (bf16[32,8192]{1,0:T(8,128)(2,1)S(1)}, bf16[32,8192]{1,0:T(8,128)(2,1)S(1)}, u32[]{:S(2)}, u32[]{:S(2)}) collective-permute-start(bf16[32,8192]{1,0:T(8,128)(2,1)S(1)} %copy-done), channel_id=1, source_target_pairs={{0,1},{1,0},{2,3},{3,2},{4,5},{5,4},{6,7},{7,6},{8,9},{9,8},{10,11... | collective-permute-start | bytes 1572872 | tf_op jit(solution)/shard_map/ppermute | solution.py:212
  59.4 0.0 collective-permute-done.2.x_hbm
  59.4 0.0 copy-start.1
  59.4 2.3 %collective-permute-start.3 = (bf16[32,8192]{1,0:T(8,128)(2,1)S(1)}, bf16[32,8192]{1,0:T(8,128)(2,1)S(1)}, u32[]{:S(2)}, u32[]{:S(2)}) collective-permute-start(bf16[32,8192]{1,0:T(8,128)(2,1)S(1)} %collective-permute-done.2.x_hbm), channel_id=1, source_target_pairs={{0,1},{1,0},{2,3},{3,2},{4,5},{5,4},{6,7},{7,6},{8,9},{9,8},{10,11... | collective-permute-start | bytes 1572872 | tf_op jit(solution)/shard_map/ppermute | solution.py:213
  61.8 0.0 collective-permute-done.1.core_hbm
  61.8 0.0 copy-start.2
  61.8 1.5 %collective-permute-done.3.both_hbm = bf16[32,8192]{1,0:T(8,128)(2,1)S(1)} collective-permute-done((bf16[32,8192]{1,0:T(8,128)(2,1)S(1)}, bf16[32,8192]{1,0:T(8,128)(2,1)S(1)}, u32[]{:S(2)}, u32[]{:S(2)}) %collective-permute-start.3) | collective-permute-done | bytes 524320 | tf_op jit(solution)/shard_map/ppermute | solution.py:213
  63.3 0.0 copy-start.3
  63.3 0.0 copy-done.1
  63.3 0.0 copy-done.2
  63.3 0.8 %copy-done.3 = bf16[32,8192]{1,0:T(8,128)(2,1)} copy-done((bf16[32,8192]{1,0:T(8,128)(2,1)}, bf16[32,8192]{1,0:T(8,128)(2,1)S(1)}, u32[]{:S(2)}) %copy-start.3) | copy-done | bytes 524312
  64.1 5.8 %shard_map.69 = bf16[240,256]{1,0:T(8,128)(2,1)} custom-call(s32[1]{0:T(128)} %bitcast.5.place_ref, bf16[240,256]{1,0:T(8,128)(2,1)} %bitcast.12, bf16[32,8192]{1,0:T(8,128)(2,1)} %get-tuple-element.13.own_hbm, bf16[32,8192]{1,0:T(8,128)(2,1)} %copy-done.2, bf16[32,8192]{1,0:T(8,128)(2,1)} %copy-done.1, bf16[32,8192]{1,0:T(8,128)(2,1)} %copy-done.3, ...), custom_call_target="tpu_custom_call" | custom-call | flops 503316480 | bytes 6291456 | tf_op jit(solution)/shard_map/pallas_call | solution.py:159
  69.9 7.3 %all-to-all-done.1 = bf16[480,2,128]{2,1,0:T(2,128)(2,1)S(1)} async-done(((bf16[480,2,128]{2,1,0:T(2,128)(2,1)}), bf16[480,2,128]{2,1,0:T(2,128)(2,1)S(1)}, u32[]{:S(2)}, u32[]{:S(2)}) %all-to-all-start.1) | async-done | bytes 245792 | tf_op jit(solution)/shard_map/all_to_all | solution.py:214
  77.3 0.6 shard_map.70
Async XLA Ops:
  8.8 4.7 %collective-permute-start = (bf16[3840,128]{1,0:T(8,128)(2,1)}, bf16[3840,128]{1,0:T(8,128)(2,1)S(1)}, u32[]{:S(2)}, u32[]{:S(2)}) collective-permute-start(bf16[3840,128]{1,0:T(8,128)(2,1)} %get-tuple-element.11), channel_id=1, source_target_pairs={{0,1},{1,0},{2,3},{3,2},{4,5},{5,4},{6,7},{7,6},{8,9},{9,8},{10,11... | collective-permute-start | bytes 2949128 | tf_op jit(solution)/shard_map/ppermute | solution.py:205
  14.9 25.8 %copy-start = (bf16[32,8192]{1,0:T(8,128)(2,1)S(1)}, bf16[32,8192]{1,0:T(8,128)(2,1)}, u32[]{:S(2)}) copy-start(bf16[32,8192]{1,0:T(8,128)(2,1)} %get-tuple-element.13.own_hbm) | copy-start | bytes 1572868
  40.7 18.7 %collective-permute-start.2 = (bf16[32,8192]{1,0:T(8,128)(2,1)S(1)}, bf16[32,8192]{1,0:T(8,128)(2,1)S(1)}, u32[]{:S(2)}, u32[]{:S(2)}) collective-permute-start(bf16[32,8192]{1,0:T(8,128)(2,1)S(1)} %copy-done), channel_id=1, source_target_pairs={{0,2},{1,7},{2,0},{3,5},{4,6},{5,3},{6,4},{7,1},{8,10},{9,15},{10,... | collective-permute-start | bytes 1572872 | tf_op jit(solution)/shard_map/ppermute | solution.py:211
  43.0 34.3 %all-to-all-start.1 = ((bf16[480,2,128]{2,1,0:T(2,128)(2,1)}), bf16[480,2,128]{2,1,0:T(2,128)(2,1)S(1)}, u32[]{:S(2)}, u32[]{:S(2)}) async-start(bf16[480,2,128]{2,1,0:T(2,128)(2,1)} %bitcast.4), calls=%async_computation.1 | async-start | bytes 491520 | tf_op jit(solution)/shard_map/all_to_all | solution.py:214
  57.4 4.4 %collective-permute-start.1 = (bf16[32,8192]{1,0:T(8,128)(2,1)S(1)}, bf16[32,8192]{1,0:T(8,128)(2,1)S(1)}, u32[]{:S(2)}, u32[]{:S(2)}) collective-permute-start(bf16[32,8192]{1,0:T(8,128)(2,1)S(1)} %copy-done), channel_id=1, source_target_pairs={{0,1},{1,0},{2,3},{3,2},{4,5},{5,4},{6,7},{7,6},{8,9},{9,8},{10,11... | collective-permute-start | bytes 1572872 | tf_op jit(solution)/shard_map/ppermute | solution.py:212
  59.4 3.9 %copy-start.1 = (bf16[32,8192]{1,0:T(8,128)(2,1)}, bf16[32,8192]{1,0:T(8,128)(2,1)S(1)}, u32[]{:S(2)}) copy-start(bf16[32,8192]{1,0:T(8,128)(2,1)S(1)} %collective-permute-done.2.x_hbm) | copy-start | bytes 1572868
  59.4 3.9 %collective-permute-start.3 = (bf16[32,8192]{1,0:T(8,128)(2,1)S(1)}, bf16[32,8192]{1,0:T(8,128)(2,1)S(1)}, u32[]{:S(2)}, u32[]{:S(2)}) collective-permute-start(bf16[32,8192]{1,0:T(8,128)(2,1)S(1)} %collective-permute-done.2.x_hbm), channel_id=1, source_target_pairs={{0,1},{1,0},{2,3},{3,2},{4,5},{5,4},{6,7},{7,6},{8,9},{9,8},{10,11... | collective-permute-start | bytes 1572872 | tf_op jit(solution)/shard_map/ppermute | solution.py:213
  61.8 1.5 %copy-start.2 = (bf16[32,8192]{1,0:T(8,128)(2,1)}, bf16[32,8192]{1,0:T(8,128)(2,1)S(1)}, u32[]{:S(2)}) copy-start(bf16[32,8192]{1,0:T(8,128)(2,1)S(1)} %collective-permute-done.1.core_hbm) | copy-start | bytes 1572868
  63.3 0.8 %copy-start.3 = (bf16[32,8192]{1,0:T(8,128)(2,1)}, bf16[32,8192]{1,0:T(8,128)(2,1)S(1)}, u32[]{:S(2)}) copy-start(bf16[32,8192]{1,0:T(8,128)(2,1)S(1)} %collective-permute-done.3.both_hbm) | copy-start | bytes 1572868
